TPU v7x, 32 devices: a whole 2x2x4 slice. The times are simulated.
32 devices in a mesh: dp: 4 (over z), expert: 8 (over y, x, core).
Axes of the slice: x: 2, y: 2, z: 4, core: 2. Of those that a mesh axis runs over, the one named last changes fastest.
Arguments:
- tokens: bfloat16 [4096, 2048], P(('dp', 'expert')), may hold values from -6 to 6
- attn_gain: bfloat16 [2048], P('dp'), may hold values from 0.5 to 1.5
- qkv_weight: bfloat16 [2048, 6144], P('dp'), may hold values from -0.125 to 0.125
- qkv_bias: bfloat16 [3, 2048], P(None, 'dp'), may hold values from -3 to 3
- out_weight: bfloat16 [2048, 2048], P('dp'), may hold values from -0.5 to 0.5
- ffn_gain: bfloat16 [2048], P('dp'), may hold values from 0.5 to 1.5
- router_weight: bfloat16 [2048, 8], P('dp'), may hold values from -0.0625 to 0.0625
- shared_gate_weight: bfloat16 [2048], P('dp'), may hold values from -0.125 to 0.125
- shared_weight: bfloat16 [5632, 3, 2048], P('dp'), may hold values from -0.125 to 0.125
- expert_up: bfloat16 [8, 1408, 2, 2048], P('expert', None, None, 'dp'), may hold values from -0.125 to 0.125
- expert_down: bfloat16 [8, 1408, 2048], P('expert', None, 'dp'), may hold values from -1.25 to 1.25
- routes: int32 [4096, 4], P(('dp', 'expert')), may hold values from 0 to 7, all different within a row; in each aligned block of 128 rows (0 to 127, 128 to 255, ...) at most 128 rows name the same one
- segment_ids: int32 [32, 128], P(('dp', 'expert')), may hold values from 0 to 3, never falling along the last dimension, each value on 1 to 48 neighbouring positions
- cotangent: bfloat16 [4096, 2048], P(('dp', 'expert')), may hold values from -6 to 6
Outputs:
- output: bfloat16 [4096, 2048], P(('dp', 'expert'))
- tokens_grad: float32 [4096, 2048], P(('dp', 'expert'))
- attn_gain_grad: float32 [2048], P('dp')
- qkv_weight_grad: float32 [2048, 6144], P('dp')
- qkv_bias_grad: float32 [3, 2048], P(None, 'dp')
- out_weight_grad: float32 [2048, 2048], P('dp')
- ffn_gain_grad: float32 [2048], P('dp')
- router_weight_grad: float32 [2048, 8], P('dp')
- shared_gate_weight_grad: float32 [2048], P('dp')
- shared_weight_grad: float32 [5632, 3, 2048], P('dp')
- expert_up_grad: float32 [8, 1408, 2, 2048], P('expert', None, None, 'dp')
- expert_down_grad: float32 [8, 1408, 2048], P('expert', None, 'dp')
Inputs may be any that keep to these rules, and one draw needn't show every extreme that they name: `routes`: each row names 4 different experts. Within the rows of one sequence (an aligned block of 128 rows) no expert is named more than 128 times, and in every draw some expert is named exactly 128 times in some block. `segment_ids`: along a sequence the document ids never fall; each document holds 1 to 48 positions, and some document holds exactly 48.
All inputs are finite; a program needn't handle non-finite values.
Results may differ from a plain program's by a relative error of at most 0.02.
Values may be sent and summed in bfloat16 or wider, within the bound.
A program may use at most 384 MiB of HBM per device.

v0:
```python
import math

import jax
import jax.numpy as jnp
from jax import lax
from jax.sharding import PartitionSpec as P

HEADS = 16
HEAD = 128
TOP = 4


EPS = 1e-06
THETA = 1000000.0
NEGATIVE = -1e30


def rms_scale(values):
    return lax.rsqrt(jnp.mean(values * values, axis=-1, keepdims=True) + EPS)


def silu_grad(values):
    logistic = jax.nn.sigmoid(values)
    return logistic * (1.0 + values * (1.0 - logistic))


def route_slots(block_routes, num_experts):
    flat_routes = block_routes.reshape(-1)
    onehot = (flat_routes[:, None] == jnp.arange(num_experts, dtype=jnp.int32)[None, :]).astype(
        jnp.int32
    )
    before = jnp.cumsum(onehot, axis=0, dtype=jnp.int32) - onehot
    return jnp.sum(before * onehot, axis=1, dtype=jnp.int32).reshape(block_routes.shape)


def rope_tables(length, head_width):
    indices = jnp.arange(head_width // 2).astype(jnp.float32)
    frequency = jnp.exp(indices * (-2.0 * math.log(THETA) / head_width))
    angles = jnp.arange(length).astype(jnp.float32)[:, None] * frequency[None, :]
    return (jnp.cos(angles), jnp.sin(angles))


def rotate(values, cosine_table, sine_table):
    half_width = values.shape[-1] // 2
    lower_half = values[..., :half_width]
    upper_half = values[..., half_width:]
    cos_rows = cosine_table[:, None, :]
    sin_rows = sine_table[:, None, :]
    return jnp.concatenate(
        [
            lower_half * cos_rows - upper_half * sin_rows,
            upper_half * cos_rows + lower_half * sin_rows,
        ],
        axis=-1,
    )


def unrotate(values, cosine_table, sine_table):
    half_width = values.shape[-1] // 2
    lower_half = values[..., :half_width]
    upper_half = values[..., half_width:]
    cos_rows = cosine_table[:, None, :]
    sin_rows = sine_table[:, None, :]
    return jnp.concatenate(
        [
            lower_half * cos_rows + upper_half * sin_rows,
            upper_half * cos_rows - lower_half * sin_rows,
        ],
        axis=-1,
    )


def norm_back(values, scale_rows, gain_row, upstream):
    scaled = gain_row * upstream
    gain_grad = jnp.sum(upstream * values * scale_rows, axis=0)
    input_grad = scale_rows * scaled - values * scale_rows**3 * jnp.mean(
        scaled * values, axis=-1, keepdims=True
    )
    return (gain_grad, input_grad)


def shared_back(d_out_low, gate_up, weight):
    d_act = jnp.einsum("td,fd->tf", d_out_low, weight[:, 2], preferred_element_type=jnp.float32)
    gate_part = gate_up[:, 0]
    up_part = gate_up[:, 1]
    return jnp.stack(
        [d_act * up_part * silu_grad(gate_part), d_act * jax.nn.silu(gate_part)], axis=1
    ).astype(jnp.bfloat16)


def shared_grad_rows(d_gate_up, act_low, normed_rows, d_out_low):
    gu_term = jnp.einsum("tgf,td->fgd", d_gate_up, normed_rows, preferred_element_type=jnp.float32)
    down_term = jnp.einsum("tf,td->fd", act_low, d_out_low, preferred_element_type=jnp.float32)
    return jnp.concatenate([gu_term, down_term[:, None, :]], axis=1)


def shards(
    tokens,
    attn_gain,
    qkv_weight,
    qkv_bias,
    out_weight,
    ffn_gain,
    router_weight,
    shared_gate_weight,
    shared_weight,
    expert_up,
    expert_down,
    routes,
    segment_ids,
    cotangent,
):
    gathered = (
        lax.all_gather(attn_gain, "dp", axis=0, tiled=True),
        lax.all_gather(qkv_bias, "dp", axis=1, tiled=True),
        lax.all_gather(out_weight, "dp", axis=0, tiled=True),
        lax.all_gather(ffn_gain, "dp", axis=0, tiled=True),
        lax.all_gather(router_weight, "dp", axis=0, tiled=True),
        lax.all_gather(shared_gate_weight, "dp", axis=0, tiled=True),
        lax.all_gather(expert_up, "dp", axis=3, tiled=True),
        lax.all_gather(expert_down, "dp", axis=2, tiled=True),
    )
    gain_one = gathered[0].astype(jnp.float32)
    b_qkv = gathered[1].reshape(-1).astype(jnp.float32)
    w_out = gathered[2]
    gain_two = gathered[3].astype(jnp.float32)
    w_router = gathered[4]
    w_sgate = gathered[5]
    w_up = gathered[6][0]
    w_down = gathered[7][0]
    seq_len = tokens.shape[0]
    model_width = tokens.shape[1]
    num_experts = w_router.shape[1]
    capacity = 2 * seq_len * TOP // num_experts
    score_scale = HEAD ** (-0.5)
    route_total = seq_len * TOP
    resid_in = tokens.astype(jnp.float32)
    rms_one = rms_scale(resid_in)
    normed_one = (resid_in * rms_one * gain_one).astype(jnp.bfloat16)
    normed_cols = lax.all_to_all(normed_one, "dp", split_axis=1, concat_axis=0, tiled=True)
    big = (
        lax.all_gather(qkv_weight, "dp", axis=0, tiled=True),
        lax.all_gather(shared_weight, "dp", axis=0, tiled=True),
    )
    w_qkv = big[0]
    w_shared = big[1]
    qkv_rows = jnp.dot(normed_one, w_qkv, preferred_element_type=jnp.float32) + b_qkv
    qkv_rows = qkv_rows.reshape(seq_len, 3, HEADS, HEAD)
    cosine_table, sine_table = rope_tables(seq_len, HEAD)
    query_rows = rotate(qkv_rows[:, 0], cosine_table, sine_table).astype(jnp.bfloat16)
    key_rows = rotate(qkv_rows[:, 1], cosine_table, sine_table).astype(jnp.bfloat16)
    value_rows = qkv_rows[:, 2].astype(jnp.bfloat16)
    doc_ids = segment_ids[0]
    positions = jnp.arange(seq_len)
    allowed = ((doc_ids[:, None] == doc_ids[None, :]) & (positions[:, None] >= positions[None, :]))[
        None
    ]

    def masked_scores():
        raw_scores = (
            jnp.einsum("thd,shd->hts", query_rows, key_rows, preferred_element_type=jnp.float32)
            * score_scale
        )
        return jnp.where(allowed, raw_scores, NEGATIVE)

    scores = masked_scores()
    row_max = jnp.max(scores, axis=-1, keepdims=True)
    exp_scores = jnp.exp(scores - row_max)
    row_total = jnp.sum(exp_scores, axis=-1, keepdims=True)
    log_total = row_max + jnp.log(row_total)
    probs_low = (exp_scores / row_total).astype(jnp.bfloat16)
    mixed_heads = (
        jnp.einsum("hts,shd->thd", probs_low, value_rows, preferred_element_type=jnp.float32)
        .reshape(seq_len, model_width)
        .astype(jnp.bfloat16)
    )
    hidden_state = resid_in + jnp.dot(mixed_heads, w_out, preferred_element_type=jnp.float32)
    rms_two = rms_scale(hidden_state)
    normed_two = (hidden_state * rms_two * gain_two).astype(jnp.bfloat16)
    logits = jnp.dot(normed_two, w_router, preferred_element_type=jnp.float32)
    router_probs = jax.nn.softmax(logits, axis=-1)
    route_hot = (
        routes[:, :, None] == jnp.arange(num_experts, dtype=jnp.int32)[None, None, :]
    ).astype(jnp.float32)
    gate_values = jnp.sum(route_hot * router_probs[:, None, :], axis=-1)
    slot_index = route_slots(routes, num_experts)
    target = (routes * capacity + slot_index).reshape(-1)
    slot_table = (
        jnp.full((num_experts * capacity,), route_total, dtype=jnp.int32)
        .at[target]
        .set(jnp.arange(route_total, dtype=jnp.int32))
    )
    slot_filled = (slot_table < route_total)[:, None]
    slot_route = jnp.minimum(slot_table, route_total - 1)
    slot_token = slot_route // TOP
    send_rows = jnp.where(slot_filled, normed_two[slot_token], jnp.zeros((), jnp.bfloat16)).reshape(
        num_experts, capacity, model_width
    )
    received = lax.all_to_all(send_rows, "expert", split_axis=0, concat_axis=0, tiled=True)
    gate_up = jnp.einsum("scd,fgd->scgf", received, w_up, preferred_element_type=jnp.float32)
    expert_act = (jax.nn.silu(gate_up[:, :, 0]) * gate_up[:, :, 1]).astype(jnp.bfloat16)
    expert_res = jnp.einsum(
        "scf,fd->scd", expert_act, w_down, preferred_element_type=jnp.float32
    ).astype(jnp.bfloat16)
    coming_back = lax.all_to_all(expert_res, "expert", split_axis=0, concat_axis=0, tiled=True)
    coming_back, received, gate_up, expert_act = (coming_back, received, gate_up, expert_act)
    picked = (
        coming_back.reshape(num_experts * capacity, model_width)[target]
        .reshape(seq_len, TOP, model_width)
        .astype(jnp.float32)
    )
    expert_sum = jnp.sum(gate_values[:, :, None] * picked, axis=1)
    gate_logit = jnp.dot(normed_two, w_sgate, preferred_element_type=jnp.float32)
    logistic_gate = jax.nn.sigmoid(gate_logit)
    back_grad = cotangent.astype(jnp.float32)
    row_pool = (
        lax.all_gather(normed_two, "dp", axis=0, tiled=True),
        lax.all_gather(cotangent, "dp", axis=0, tiled=True),
    )
    pooled_normed = row_pool[0]
    pooled_grad = row_pool[1]
    own_gu = jnp.einsum(
        "td,fgd->tgf", normed_two, w_shared[:, 0:2], preferred_element_type=jnp.float32
    )
    own_act = (jax.nn.silu(own_gu[:, 0]) * own_gu[:, 1]).astype(jnp.bfloat16)
    shared_out = jnp.dot(own_act, w_shared[:, 2], preferred_element_type=jnp.float32)
    shared_gu = jnp.einsum(
        "td,fgd->tgf", pooled_normed, shared_weight[:, 0:2], preferred_element_type=jnp.float32
    )
    shared_act = (jax.nn.silu(shared_gu[:, 0]) * shared_gu[:, 1]).astype(jnp.bfloat16)
    block_out = hidden_state + expert_sum + logistic_gate[:, None] * shared_out
    output = block_out.astype(jnp.bfloat16)
    d_gate_logit = (
        jnp.sum(back_grad * shared_out, axis=-1) * logistic_gate * (1.0 - logistic_gate)
    ).astype(jnp.bfloat16)
    sgate_grad = jnp.dot(d_gate_logit, normed_two, preferred_element_type=jnp.float32)
    d_normed = d_gate_logit.astype(jnp.float32)[:, None] * w_sgate.astype(jnp.float32)[None, :]
    pooled_gate = jax.nn.sigmoid(
        jnp.dot(pooled_normed, w_sgate, preferred_element_type=jnp.float32)
    )
    pooled_d_out = (pooled_grad.astype(jnp.float32) * pooled_gate[:, None]).astype(jnp.bfloat16)
    d_shared_gu = shared_back(pooled_d_out, shared_gu, shared_weight)
    d_pooled = jnp.einsum(
        "tgf,fgd->td", d_shared_gu, shared_weight[:, 0:2], preferred_element_type=jnp.float32
    )
    d_normed = d_normed + lax.psum_scatter(
        d_pooled.astype(jnp.bfloat16), "dp", scatter_dimension=0, tiled=True
    ).astype(jnp.float32)
    shared_local = shared_grad_rows(d_shared_gu, shared_act, pooled_normed, pooled_d_out)
    d_gates = jnp.sum(back_grad[:, None, :] * picked, axis=-1)
    d_router_probs = jnp.sum(route_hot * d_gates[:, :, None], axis=1)
    d_logits = (
        router_probs
        * (d_router_probs - jnp.sum(router_probs * d_router_probs, axis=-1, keepdims=True))
    ).astype(jnp.bfloat16)
    router_grad = jnp.einsum("td,te->de", normed_two, d_logits, preferred_element_type=jnp.float32)
    d_normed = d_normed + jnp.einsum(
        "te,de->td", d_logits, w_router, preferred_element_type=jnp.float32
    )
    gate_flat = gate_values.reshape(-1)
    back_rows = (
        jnp.where(slot_filled, back_grad[slot_token] * gate_flat[slot_route][:, None], 0.0)
        .astype(jnp.bfloat16)
        .reshape(num_experts, capacity, model_width)
    )
    d_received = lax.all_to_all(back_rows, "expert", split_axis=0, concat_axis=0, tiled=True)
    d_act = jnp.einsum("scd,fd->scf", d_received, w_down, preferred_element_type=jnp.float32)
    gate_part = gate_up[:, :, 0]
    up_part = gate_up[:, :, 1]
    d_gate_up = jnp.stack(
        [d_act * up_part * silu_grad(gate_part), d_act * jax.nn.silu(gate_part)], axis=2
    ).astype(jnp.bfloat16)
    up_grad = jnp.einsum("scgf,scd->fgd", d_gate_up, received, preferred_element_type=jnp.float32)
    down_grad = jnp.einsum(
        "scf,scd->fd", expert_act, d_received, preferred_element_type=jnp.float32
    )
    d_sent = jnp.einsum(
        "scgf,fgd->scd", d_gate_up, w_up, preferred_element_type=jnp.float32
    ).astype(jnp.bfloat16)
    expert_grads = (
        lax.psum_scatter(
            up_grad[None].astype(jnp.bfloat16), "dp", scatter_dimension=3, tiled=True
        ).astype(jnp.float32),
        lax.psum_scatter(
            down_grad[None].astype(jnp.bfloat16), "dp", scatter_dimension=2, tiled=True
        ).astype(jnp.float32),
    )
    d_back = lax.all_to_all(d_sent, "expert", split_axis=0, concat_axis=0, tiled=True)
    d_routed = (
        d_back.reshape(num_experts * capacity, model_width)[target]
        .reshape(seq_len, TOP, model_width)
        .astype(jnp.float32)
    )
    d_normed = d_normed + jnp.sum(d_routed, axis=1)
    ffn_gain_grad, d_hidden = norm_back(hidden_state, rms_two, gain_two, d_normed)
    d_hidden = back_grad + d_hidden
    d_attn_out = d_hidden.astype(jnp.bfloat16)
    out_weight_grad = jnp.einsum(
        "td,te->de", mixed_heads, d_attn_out, preferred_element_type=jnp.float32
    )
    d_mixed = (
        jnp.einsum("te,de->td", d_attn_out, w_out, preferred_element_type=jnp.float32)
        .astype(jnp.bfloat16)
        .reshape(seq_len, HEADS, HEAD)
    )
    attn_probs = jnp.exp(masked_scores() - log_total)
    probs_again = attn_probs.astype(jnp.bfloat16)
    values_grad = jnp.einsum(
        "hts,thd->shd", probs_again, d_mixed, preferred_element_type=jnp.float32
    )
    d_probs = jnp.einsum("thd,shd->hts", d_mixed, value_rows, preferred_element_type=jnp.float32)
    d_scores = (
        attn_probs * (d_probs - jnp.sum(attn_probs * d_probs, axis=-1, keepdims=True))
    ).astype(jnp.bfloat16)
    d_query = unrotate(
        jnp.einsum("hts,shd->thd", d_scores, key_rows, preferred_element_type=jnp.float32)
        * score_scale,
        cosine_table,
        sine_table,
    )
    d_keys = unrotate(
        jnp.einsum("hts,thd->shd", d_scores, query_rows, preferred_element_type=jnp.float32)
        * score_scale,
        cosine_table,
        sine_table,
    )
    d_qkv = (
        jnp.stack([d_query, d_keys, values_grad], axis=1)
        .reshape(seq_len, 3 * model_width)
        .astype(jnp.bfloat16)
    )
    bias_grad = jnp.sum(d_qkv.astype(jnp.float32), axis=0).reshape(3, model_width)
    pooled_d_qkv = lax.all_gather(d_qkv, "dp", axis=0, tiled=True)
    local_qkv_grad = jnp.einsum(
        "td,te->de", normed_cols, pooled_d_qkv, preferred_element_type=jnp.float32
    )
    d_normed_one = jnp.einsum("te,de->td", d_qkv, w_qkv, preferred_element_type=jnp.float32)
    summed_pieces = (
        lax.psum_scatter(
            local_qkv_grad.astype(jnp.bfloat16), "expert", scatter_dimension=0, tiled=True
        ).astype(jnp.float32),
        lax.psum_scatter(
            shared_local.astype(jnp.bfloat16), "expert", scatter_dimension=0, tiled=True
        ).astype(jnp.float32),
    )
    qkv_piece = summed_pieces[0]
    shared_piece = summed_pieces[1]
    attn_gain_grad, d_input = norm_back(resid_in, rms_one, gain_one, d_normed_one)
    tokens_grad = d_hidden + d_input
    reduced = (
        lax.psum_scatter(attn_gain_grad, ("dp", "expert"), scatter_dimension=0, tiled=True),
        lax.psum_scatter(bias_grad, ("dp", "expert"), scatter_dimension=1, tiled=True),
        lax.psum_scatter(out_weight_grad, ("dp", "expert"), scatter_dimension=0, tiled=True),
        lax.psum_scatter(ffn_gain_grad, ("dp", "expert"), scatter_dimension=0, tiled=True),
        lax.psum_scatter(router_grad, ("dp", "expert"), scatter_dimension=0, tiled=True),
        lax.psum_scatter(sgate_grad, ("dp", "expert"), scatter_dimension=0, tiled=True),
    )
    regrouped = (
        lax.all_gather(reduced[0].astype(jnp.bfloat16), "expert", axis=0, tiled=True).astype(
            jnp.float32
        ),
        lax.all_gather(reduced[1].astype(jnp.bfloat16), "expert", axis=1, tiled=True).astype(
            jnp.float32
        ),
        lax.all_gather(reduced[2].astype(jnp.bfloat16), "expert", axis=0, tiled=True).astype(
            jnp.float32
        ),
        lax.all_gather(reduced[3].astype(jnp.bfloat16), "expert", axis=0, tiled=True).astype(
            jnp.float32
        ),
        lax.all_gather(reduced[4].astype(jnp.bfloat16), "expert", axis=0, tiled=True).astype(
            jnp.float32
        ),
        lax.all_gather(reduced[5].astype(jnp.bfloat16), "expert", axis=0, tiled=True).astype(
            jnp.float32
        ),
        lax.all_gather(qkv_piece.astype(jnp.bfloat16), "expert", axis=0, tiled=True).astype(
            qkv_piece.dtype
        ),
        lax.all_gather(shared_piece.astype(jnp.bfloat16), "expert", axis=0, tiled=True).astype(
            shared_piece.dtype
        ),
    )
    return (
        output,
        tokens_grad,
        regrouped[0],
        regrouped[6],
        regrouped[1],
        regrouped[2],
        regrouped[3],
        regrouped[4],
        regrouped[5],
        regrouped[7],
        expert_grads[0],
        expert_grads[1],
    )


def solution(mesh):
    return jax.shard_map(
        shards,
        mesh=mesh,
        in_specs=(
            P(("dp", "expert"), None),
            P("dp"),
            P("dp", None),
            P(None, "dp"),
            P("dp", None),
            P("dp"),
            P("dp", None),
            P("dp"),
            P("dp", None, None),
            P("expert", None, None, "dp"),
            P("expert", None, "dp"),
            P(("dp", "expert"), None),
            P(("dp", "expert"), None),
            P(("dp", "expert"), None),
        ),
        out_specs=(
            P(("dp", "expert"), None),
            P(("dp", "expert"), None),
            P("dp"),
            P("dp", None),
            P(None, "dp"),
            P("dp", None),
            P("dp"),
            P("dp", None),
            P("dp"),
            P("dp", None, None),
            P("expert", None, None, "dp"),
            P("expert", None, "dp"),
        ),
        check_vma=False,
    )
```

profile of v0, /device:TPU:1, one launch (start us, length us, event | category | flops | bytes accessed | tf_op | source)
XLA Modules:
  0.0 3622.3 jit_solution(16519898095662472241)
XLA Ops:
  11.7 10.3 all-gather.1
  22.1 9.3 all-gather
  31.4 34.6 all_gather.65
  67.4 370.0 %all-gather.17.cloned.1.call-done = bf16[2048,6144]{1,0:T(8,128)(2,1)} async-done(((bf16[512,6144]{1,0:T(8,128)(2,1)}), bf16[2048,6144]{1,0:T(8,128)(2,1)}) %all-gather.17.cloned.1.call-update) | async-done | bytes 25165840 | tf_op jit(solution)/shard_map/all_gather | solution.py:142
  437.4 10.7 fusion.62
  457.2 129.7 %all-gather.19.cloned.1.call-done = bf16[2048,2048]{1,0:T(8,128)(2,1)} async-done(((bf16[512,2048]{1,0:T(8,128)(2,1)}), bf16[2048,2048]{1,0:T(8,128)(2,1)}) %all-gather.19.cloned.1.call-update) | async-done | bytes 8388624 | tf_op jit(solution)/shard_map/all_gather | solution.py:116
  622.1 12.6 all_gather.68
  647.7 13.2 all-to-all-done
  660.9 8.5 all-to-all-start.2
  669.4 119.5 %all-gather.21.cloned.1.call-done = bf16[1,1408,2,2048]{3,1,2,0:T(8,128)(2,1)} async-done(((bf16[1,1408,2,512]{3,1,2,0:T(8,128)(2,1)}), bf16[1,1408,2,2048]{3,1,2,0:T(8,128)(2,1)}) %all-gather.21.cloned.1.call-update) | async-done | bytes 11534352 | tf_op jit(solution)/shard_map/all_gather | solution.py:120
  788.9 18.8 fusion.17
  807.6 87.6 %all-gather.23.cloned.1.call-done = bf16[1,1408,2048]{2,1,0:T(8,128)(2,1)} async-done(((bf16[1,1408,512]{2,1,0:T(8,128)(2,1)}), bf16[1,1408,2048]{2,1,0:T(8,128)(2,1)}) %all-gather.23.cloned.1.call-update) | async-done | bytes 5767184 | tf_op jit(solution)/shard_map/all_gather | solution.py:121
  895.2 13.4 fusion.58
  911.2 16.2 bitcast_convert_fusion.2
  932.4 9.9 all-gather.2
  944.7 12.8 fusion.47
  957.4 20.6 all-to-all-done.3
  986.1 12.0 fusion.40
  998.1 14.0 fusion.66
  1014.0 10.9 bitcast_convert_fusion.3
  1025.3 8.4 gather_fusion.4
  1033.7 8.4 gather_fusion.1
  1063.1 1071.1 %all-gather.25.cloned.1.call-done = bf16[5632,3,2048]{2,0,1:T(8,128)(2,1)} async-done(((bf16[1408,3,2048]{2,0,1:T(8,128)(2,1)}), bf16[5632,3,2048]{2,0,1:T(8,128)(2,1)}) %all-gather.25.cloned.1.call-update) | async-done | bytes 69206032 | tf_op jit(solution)/shard_map/all_gather | solution.py:143
  2134.3 23.3 fusion.12
  2157.6 12.3 multiply_reduce_fusion.5
  2219.7 37.3 %copy.258 = bf16[1408,3,2048]{2,1,0:T(4,128)(2,1)} copy(bf16[1408,3,2048]{0,2,1:T(8,128)(2,1)} %pad_maximum_fusion) | data formatting | bytes 34603008 | tf_op jit(solution)/shard_map/concatenate | solution.py:94
  2258.1 22.7 all_to_all.39
  2280.7 44.2 %all-gather.31.cloned.1.call-done = bf16[512,6144]{0,1:T(8,128)(2,1)} async-done(((bf16[128,6144]{0,1:T(8,128)(2,1)}), bf16[512,6144]{0,1:T(8,128)(2,1)}) %all-gather.31.cloned.1.call-update) | async-done | bytes 6291472 | tf_op jit(solution)/shard_map/all_gather | solution.py:333
  2343.9 13.5 fusion.16
  2357.7 18.3 fusion.11
  2377.9 238.2 %all-reduce.11.cloned.1.call-done = bf16[1408,3,2048]{2,1,0:T(4,128)(2,1)} async-done(((bf16[1408,3,2048]{2,1,0:T(4,128)(2,1)}), bf16[1408,3,2048]{2,1,0:T(4,128)(2,1)}) %all-reduce.11.cloned.1.call-update) | async-done | bytes 17301520
  2623.8 57.3 %reduce-scatter.14.cloned.1.call-done = bf16[64,6144]{1,0:T(8,128)(2,1)} async-done(((bf16[512,6144]{1,0:T(8,128)(2,1)}), bf16[64,6144]{1,0:T(8,128)(2,1)}) %reduce-scatter.14.cloned.1.call-update) | async-done | bytes 786448 | tf_op jit(solution)/shard_map/reduce_scatter | solution.py:339
  2681.2 185.4 %reduce-scatter.16.cloned.1.call-done = f32[64,2048]{1,0:T(8,128)} async-done(((f32[2048,2048]{1,0:T(8,128)}), f32[64,2048]{1,0:T(8,128)}) %reduce-scatter.16.cloned.1.call-update) | async-done | bytes 524304 | tf_op jit(solution)/shard_map/reduce_scatter | solution.py:353
  2869.0 131.3 %reduce-scatter.24.cloned.1.call-done = f32[64,8]{1,0:T(8,128)} async-done(((f32[2048,8]{1,0:T(8,128)}), f32[64,8]{1,0:T(8,128)}) %reduce-scatter.24.cloned.1.call-update) | async-done | bytes 2064
  3001.2 13.4 all-gather.4
  3015.2 91.3 %reduce-scatter.20.cloned.1.call-done = bf16[1,1408,512]{2,1,0:T(8,128)(2,1)} async-done(((bf16[1,1408,2048]{2,1,0:T(8,128)(2,1)}), bf16[1,1408,512]{2,1,0:T(8,128)(2,1)}) %reduce-scatter.20.cloned.1.call-update) | async-done | bytes 1441808 | tf_op jit(solution)/shard_map/reduce_scatter | solution.py:284
  3109.9 194.9 %reduce-scatter.18.cloned.1.call-done = bf16[1,1408,2,512]{1,3,2,0:T(8,128)(2,1)} async-done(((bf16[1,1408,2,2048]{1,3,2,0:T(8,128)(2,1)}), bf16[1,1408,2,512]{1,3,2,0:T(8,128)(2,1)}) %reduce-scatter.18.cloned.1.call-update) | async-done | bytes 2883600 | tf_op jit(solution)/shard_map/reduce_scatter | solution.py:281
  3304.8 8.4 copy.262
  3313.2 87.5 %all-gather.37.cloned.1.call-done = bf16[1408,3,2048]{2,0,1:T(8,128)(2,1)} async-done(((bf16[176,3,2048]{2,0,1:T(8,128)(2,1)}), bf16[1408,3,2048]{2,0,1:T(8,128)(2,1)}) %all-gather.37.cloned.1.call-update) | async-done | bytes 17301520 | tf_op jit(solution)/shard_map/all_gather | solution.py:380
  3400.7 19.4 convert_element_type.353
  3420.3 18.0 fusion.82
  3438.3 38.8 %all-reduce.7 = (bf16[2048]{0:T(1024)(128)(2,1)S(1)}, bf16[2048]{0:T(1024)(128)(2,1)S(1)}, bf16[2048]{0:T(1024)(128)(2,1)S(1)}) all-reduce(f32[2048]{0:T(1024)S(1)} %get-tuple-element.100, f32[2048]{0:T(1024)S(1)} %copy-done.37, f32[2048]{0:T(1024)S(1)} %bitcast.327), channel_id=3, replica_groups=mesh['dp'=4,'expert'=8] {'dp','expert'}, use_global_device_ids=true, to_apply=%region_22.23.clone | all-reduce | flops 6144 | bytes 36864
  3478.0 13.0 all-reduce.8
  3495.4 36.8 %reduce-scatter.22.cloned.1.call-done = f32[64,3]{1,0:T(8,128)} async-done(((f32[2048,3]{1,0:T(8,128)}), f32[64,3]{1,0:T(8,128)}) %reduce-scatter.22.cloned.1.call-update) | async-done | bytes 784
  3533.0 12.3 all-gather.3
  3546.0 35.2 all-gather.33.cloned.1.call-done
  3581.2 9.2 convert_element_type.340
  3590.4 20.8 all-gather.35.cloned.1.call-done
  (285 shorter events, 200.2 us)
Async XLA Ops:
  7.2 430.2 %all-gather.17.cloned.1.call-start = ((), (), s32[]{:S(2)}) async-start(), calls=%async_computation.12 | async-start | bytes 31457280 | tf_op jit(solution)/shard_map/all_gather | solution.py:142
  7.9 578.9 %all-gather.19.cloned.1.call-start = ((), (), s32[]{:S(2)}) async-start(), calls=%async_computation.13 | async-start | bytes 10485760 | tf_op jit(solution)/shard_map/all_gather | solution.py:116
  8.7 22.7 copy-start.44
  8.7 57.3 %copy-start.6 = (bf16[128,2048]{1,0:T(8,128)(2,1)S(1)}, bf16[128,2048]{1,0:T(8,128)(2,1)}, u32[]{:S(2)}) copy-start(bf16[128,2048]{1,0:T(8,128)(2,1)} %param.14) | copy-start | bytes 1572868
  8.7 58.0 %copy-start.45 = (s32[1,128]{1,0:T(1,128)S(1)}, s32[1,128]{1,0:T(1,128)}, u32[]{:S(2)}) copy-start(s32[1,128]{1,0:T(1,128)} %param.26) | copy-start | bytes 1540
  8.7 780.1 %all-gather.21.cloned.1.call-start = ((), (), s32[]{:S(2)}) async-start(), calls=%async_computation.14 | async-start | bytes 14417920 | tf_op jit(solution)/shard_map/all_gather | solution.py:120
  11.1 884.2 %all-gather.23.cloned.1.call-start = ((), (), s32[]{:S(2)}) async-start(), calls=%async_computation.15 | async-start | bytes 7208960 | tf_op jit(solution)/shard_map/all_gather | solution.py:121
  11.6 930.8 %all-gather.29.cloned.1.call-start = ((), (), s32[]{:S(2)}) async-start(), calls=%async_computation.18 | async-start | bytes 2621440 | tf_op jit(solution)/shard_map/all_gather | solution.py:217
  22.1 570.1 %copy-start.35 = (f32[4,1,512]{2,1,0:T(1,128)}, f32[4,1,512]{2,1,0:T(1,128)S(1)}, u32[]{:S(2)}) copy-start(f32[4,1,512]{2,1,0:T(1,128)S(1)} %convert_element_type.366) | copy-start | bytes 24580
  31.4 416.8 %copy-start.33 = (f32[4,1,512]{2,1,0:T(1,128)}, f32[4,1,512]{2,1,0:T(1,128)S(1)}, u32[]{:S(2)}) copy-start(f32[4,1,512]{2,1,0:T(1,128)S(1)} %convert_element_type.365) | copy-start | bytes 24580
  66.7 381.4 %copy-start.40 = (f32[128]{0:T(128)}, f32[128]{0:T(128)S(1)}, u32[]{:S(2)}) copy-start(f32[128]{0:T(128)S(1)} %get-tuple-element.137) | copy-start | bytes 1540
  67.1 386.3 %copy-start.27 = (f32[128,64]{1,0:T(8,128)}, f32[128,64]{1,0:T(8,128)S(1)}, u32[]{:S(2)}) copy-start(f32[128,64]{1,0:T(8,128)S(1)} %get-tuple-element.132) | copy-start | bytes 98308
  67.2 386.3 %copy-start.29 = (f32[128,64]{1,0:T(8,128)}, f32[128,64]{1,0:T(8,128)S(1)}, u32[]{:S(2)}) copy-start(f32[128,64]{1,0:T(8,128)S(1)} %get-tuple-element.133) | copy-start | bytes 98308
  67.4 380.8 %copy-start.9 = (bf16[128,2048]{1,0:T(8,128)(2,1)}, bf16[128,2048]{1,0:T(8,128)(2,1)S(1)}, u32[]{:S(2)}) copy-start(bf16[128,2048]{1,0:T(8,128)(2,1)S(1)} %fusion.76) | copy-start | bytes 1572868
  457.2 134.4 %copy-start.21 = (bf16[16,128,128]{2,1,0:T(8,128)(2,1)}, bf16[16,128,128]{2,1,0:T(8,128)(2,1)S(1)}, u32[]{:S(2)}) copy-start(bf16[16,128,128]{2,1,0:T(8,128)(2,1)S(1)} %convolution_convert_fusion.3) | copy-start | bytes 1572868
  593.6 404.6 %all-gather.27.cloned.1.call-start = ((), (), s32[]{:S(2)}) async-start(), calls=%async_computation.17 | async-start | bytes 2621440 | tf_op jit(solution)/shard_map/all_gather | solution.py:218
  594.1 1540.1 %all-gather.25.cloned.1.call-start = ((), (), s32[]{:S(2)}) async-start(), calls=%async_computation.16 | async-start | bytes 86507520 | tf_op jit(solution)/shard_map/all_gather | solution.py:143
  610.2 50.6 %all-to-all-start = ((bf16[8,128,2048]{2,1,0:T(8,128)(2,1)}), bf16[8,128,2048]{2,1,0:T(8,128)(2,1)}, u32[]{:S(2)}, u32[]{:S(2)}) async-start(bf16[8,128,2048]{2,1,0:T(8,128)(2,1)} %broadcast_select_fusion), calls=%async_computation | async-start | bytes 8388608 | tf_op jit(solution)/shard_map/all_to_all | solution.py:199
  660.9 234.3 %all-to-all-start.2 = ((bf16[8,128,2048]{2,1,0:T(8,128)(2,1)}), bf16[8,128,2048]{2,1,0:T(8,128)(2,1)}, u32[]{:S(2)}, u32[]{:S(2)}) async-start(bf16[8,128,2048]{2,1,0:T(8,128)(2,1)} %select_convert_fusion), calls=%async_computation.3 | async-start | bytes 8388608 | tf_op jit(solution)/shard_map/all_to_all | solution.py:266
  927.4 50.7 %all-to-all-start.3 = ((bf16[8,128,2048]{2,1,0:T(8,128)(2,1)}), bf16[8,128,2048]{2,1,0:T(8,128)(2,1)}, u32[]{:S(2)}, u32[]{:S(2)}) async-start(bf16[8,128,2048]{2,1,0:T(8,128)(2,1)} %bitcast_convert_fusion.2), calls=%async_computation.4 | async-start | bytes 8388608 | tf_op jit(solution)/shard_map/all_to_all | solution.py:288
  978.0 55.6 %all-to-all-start.1 = ((bf16[8,128,2048]{2,1,0:T(8,128)(2,1)}), bf16[8,128,2048]{2,1,0:T(8,128)(2,1)}, u32[]{:S(2)}, u32[]{:S(2)}) async-start(bf16[8,128,2048]{2,1,0:T(8,128)(2,1)} %fusion.47), calls=%async_computation.1 | async-start | bytes 8388608 | tf_op jit(solution)/shard_map/all_to_all | solution.py:205
  986.1 1192.2 %reduce-scatter.12.cloned.1.call-start = ((), (), s32[]{:S(2)}) async-start(), calls=%async_computation.19 | async-start | bytes 2621440 | tf_op jit(solution)/shard_map/reduce_scatter | solution.py:246
  1025.0 1299.9 %all-gather.31.cloned.1.call-start = ((), (), s32[]{:S(2)}) async-start(), calls=%async_computation.20 | async-start | bytes 7864320 | tf_op jit(solution)/shard_map/all_gather | solution.py:333
  1063.1 1094.4 %copy-start.12 = (bf16[128,2048]{1,0:T(8,128)(2,1)S(1)}, bf16[128,2048]{1,0:T(8,128)(2,1)}, u32[]{:S(2)}) copy-start(bf16[128,2048]{1,0:T(8,128)(2,1)} %param.27) | copy-start | bytes 1572868
  2157.6 20.7 copy-start.5
  2157.6 20.7 copy-start.32
  2157.6 20.7 copy-start.36
  2157.6 20.7 copy-start.43
  2169.9 10.8 copy-start.51
  2183.3 8.5 copy-start.2
  2198.8 7.3 copy-start.53
  2198.8 417.4 %all-reduce.11.cloned.1.call-start = ((), (), s32[]{:S(2)}) async-start(), calls=%async_computation.30 | async-start | bytes 46137344
  2199.0 7.1 copy-start.24
  2257.0 424.1 %reduce-scatter.14.cloned.1.call-start = ((), (), s32[]{:S(2)}) async-start(), calls=%async_computation.21 | async-start | bytes 7077888 | tf_op jit(solution)/shard_map/reduce_scatter | solution.py:339
  2333.1 533.4 %reduce-scatter.16.cloned.1.call-start = ((), (), s32[]{:S(2)}) async-start(), calls=%async_computation.23 | async-start | bytes 17301504 | tf_op jit(solution)/shard_map/reduce_scatter | solution.py:353
  2342.4 657.9 %reduce-scatter.24.cloned.1.call-start = ((), (), s32[]{:S(2)}) async-start(), calls=%async_computation.29 | async-start | bytes 1081344
  2343.8 762.8 %reduce-scatter.20.cloned.1.call-start = ((), (), s32[]{:S(2)}) async-start(), calls=%async_computation.27 | async-start | bytes 7208960 | tf_op jit(solution)/shard_map/reduce_scatter | solution.py:284
  2357.4 947.4 %reduce-scatter.18.cloned.1.call-start = ((), (), s32[]{:S(2)}) async-start(), calls=%async_computation.26 | async-start | bytes 14417920 | tf_op jit(solution)/shard_map/reduce_scatter | solution.py:281
  2376.0 1024.7 %all-gather.37.cloned.1.call-start = ((), (), s32[]{:S(2)}) async-start(), calls=%async_computation.25 | async-start | bytes 19464192 | tf_op jit(solution)/shard_map/all_gather | solution.py:380
  2622.3 909.9 %reduce-scatter.22.cloned.1.call-start = ((), (), s32[]{:S(2)}) async-start(), calls=%async_computation.28 | async-start | bytes 1081344
  2623.7 957.5 %all-gather.33.cloned.1.call-start = ((), (), s32[]{:S(2)}) async-start(), calls=%async_computation.22 | async-start | bytes 7077888 | tf_op jit(solution)/shard_map/all_gather | solution.py:377
  2681.1 930.1 %all-gather.35.cloned.1.call-start = ((), (), s32[]{:S(2)}) async-start(), calls=%async_computation.24 | async-start | bytes 2359296 | tf_op jit(solution)/shard_map/all_gather | solution.py:365
  3313.2 107.0 %copy-start.3 = (bf16[128,3,16,128]{0,3,2,1:T(8,128)(2,1)S(1)}, bf16[128,3,16,128]{0,3,2,1:T(8,128)(2,1)}, u32[]{:S(2)}) copy-start(bf16[128,3,16,128]{0,3,2,1:T(8,128)(2,1)} %copy.252) | copy-start | bytes 4718596
  3313.2 107.0 %copy-start.34 = (f32[4,1,512]{2,1,0:T(1,128)S(1)}, f32[4,1,512]{2,1,0:T(1,128)}, u32[]{:S(2)}) copy-start(f32[4,1,512]{2,1,0:T(1,128)} %copy-done.33) | copy-start | bytes 24580
  3313.2 107.0 %copy-start.41 = (f32[128]{0:T(128)S(1)}, f32[128]{0:T(128)}, u32[]{:S(2)}) copy-start(f32[128]{0:T(128)} %copy-done.40) | copy-start | bytes 1540
  3420.2 18.1 copy-start.37
  3420.3 72.5 %copy-start.7 = (bf16[128,2048]{1,0:T(8,128)(2,1)S(1)}, bf16[128,2048]{1,0:T(8,128)(2,1)}, u32[]{:S(2)}) copy-start(bf16[128,2048]{1,0:T(8,128)(2,1)} %param.14) | copy-start | bytes 1572868
  3420.3 72.5 %copy-start.50 = (f32[128]{0:T(128)S(1)}, f32[128]{0:T(128)}, u32[]{:S(2)}) copy-start(f32[128]{0:T(128)} %get-tuple-element.136) | copy-start | bytes 1540
  (33 other events, 78.9 us)
Sparse Core Ops, SparseCore 0:
  9.6 427.7 all-gather.16
  439.0 147.8 all-gather.18
  589.0 199.8 all-gather.20
  790.3 104.8 all-gather.22
  897.2 44.0 all-gather.28
  942.7 44.6 all-gather.26
  989.0 1145.2 all-gather.24
  2136.6 41.6 reduce-scatter.11
  2198.9 125.9 all-gather.30
  2329.6 286.4 all-reduce.10
  2619.5 61.5 reduce-scatter.13
  2683.3 183.1 reduce-scatter.15
  2869.5 130.8 reduce-scatter.23
  3003.1 103.4 reduce-scatter.19
  3109.3 195.4 reduce-scatter.17
  3307.2 93.4 all-gather.36
  3402.8 129.3 reduce-scatter.21
  3534.0 47.1 all-gather.32
  3583.2 27.8 all-gather.34
where the time goes:
time: 3640 us; the launch traced here: 3620 us
  waiting for transfers between devices  2950 us (81%)
  matrix products  247 us (7%)
  blocking collectives  177 us (5%)
  local copies, waits for them, and re-layouts  127 us (3%)
  other arithmetic  80.8 us (2%)
    all_gather x1, waiting for transfers between devices, shards(): lax.all_gather(shared_weight, 'dp', axis=0, tiled=True)  1070 us
    unnamed x22, waiting for transfers between devices  410 us
    all_gather x1, waiting for transfers between devices, shards(): lax.all_gather(qkv_weight, 'dp', axis=0, tiled=True)  370 us
    reduce_scatter x1, waiting for transfers between devices, shards(): lax.psum_scatter(up_grad[None].astype(jnp.bfloat16), 'dp', scatter_dimens...  195 us
    reduce_scatter x1, waiting for transfers between devices, shards(): lax.psum_scatter(out_weight_grad, ('dp', 'expert'), scatter_dimension=0,...  185 us
    all_gather x1, waiting for transfers between devices, shards(): lax.all_gather(out_weight, 'dp', axis=0, tiled=True)  130 us
    all_gather x1, waiting for transfers between devices, shards(): lax.all_gather(expert_up, 'dp', axis=3, tiled=True)  119 us
    reduce_scatter x1, waiting for transfers between devices, shards(): lax.psum_scatter(down_grad[None].astype(jnp.bfloat16), 'dp', scatter_dime...  91.3 us
  transfers between devices with their start and end apart: 23, of which 19 were waited for; matrix products, arithmetic and copies ran while one was open for 12% of the time, Pallas kernels for 0%

commit v1 on v0

v1 whole, which is shorter than its diff:
```python
import math

import jax
import jax.numpy as jnp
from jax import lax
from jax.sharding import PartitionSpec as P

HEADS = 16
HEAD = 128


EPS = 1e-06
THETA = 1000000.0
NEGATIVE = -1e30


def rms_scale(values):
    return lax.rsqrt(jnp.mean(values * values, axis=-1, keepdims=True) + EPS)


def rope_tables(length, head_width):
    indices = jnp.arange(head_width // 2).astype(jnp.float32)
    frequency = jnp.exp(indices * (-2.0 * math.log(THETA) / head_width))
    angles = jnp.arange(length).astype(jnp.float32)[:, None] * frequency[None, :]
    return (jnp.cos(angles), jnp.sin(angles))


def rotate(values, cosine_table, sine_table):
    half_width = values.shape[-1] // 2
    lower_half = values[..., :half_width]
    upper_half = values[..., half_width:]
    cos_rows = cosine_table[:, None, :]
    sin_rows = sine_table[:, None, :]
    return jnp.concatenate(
        [
            lower_half * cos_rows - upper_half * sin_rows,
            upper_half * cos_rows + lower_half * sin_rows,
        ],
        axis=-1,
    )


def unrotate(values, cosine_table, sine_table):
    half_width = values.shape[-1] // 2
    lower_half = values[..., :half_width]
    upper_half = values[..., half_width:]
    cos_rows = cosine_table[:, None, :]
    sin_rows = sine_table[:, None, :]
    return jnp.concatenate(
        [
            lower_half * cos_rows + upper_half * sin_rows,
            upper_half * cos_rows - lower_half * sin_rows,
        ],
        axis=-1,
    )


def norm_back(values, scale_rows, gain_row, upstream):
    scaled = gain_row * upstream
    gain_grad = jnp.sum(upstream * values * scale_rows, axis=0)
    input_grad = scale_rows * scaled - values * scale_rows**3 * jnp.mean(
        scaled * values, axis=-1, keepdims=True
    )
    return (gain_grad, input_grad)


def silu_parts(gate):
    logistic = jax.nn.sigmoid(gate)
    silu = gate * logistic
    return (silu, logistic * (1.0 + gate * (1.0 - logistic)))


def gather_all(rows):
    rows = lax.all_gather(rows, "dp", axis=0, tiled=True)
    return lax.all_gather(rows, "expert", axis=0, tiled=True)


def scatter_all(rows):
    rows = lax.psum_scatter(rows, "expert", scatter_dimension=0, tiled=True)
    return lax.psum_scatter(rows, "dp", scatter_dimension=0, tiled=True)


def shards(
    tokens,
    attn_gain,
    qkv_weight,
    qkv_bias,
    out_weight,
    ffn_gain,
    router_weight,
    shared_gate_weight,
    shared_weight,
    expert_up,
    expert_down,
    routes,
    segment_ids,
    cotangent,
):
    num_dp = lax.axis_size("dp")
    num_expert = lax.axis_size("expert")
    me_expert = lax.axis_index("expert")
    seq_len, model_width = tokens.shape
    shard_width = qkv_weight.shape[0]
    head_count = HEADS // num_expert
    head_width = head_count * HEAD
    plane_rows = seq_len * num_expert
    units = shared_weight.shape[0] // num_expert
    score_scale = HEAD ** (-0.5)

    small = jnp.concatenate(
        [
            attn_gain[None],
            ffn_gain[None],
            shared_gate_weight[None],
            qkv_bias,
            router_weight.T,
        ],
        axis=0,
    )
    small = lax.all_gather(small, "dp", axis=1, tiled=True)
    gain_one = small[0].astype(jnp.float32)
    gain_two = small[1].astype(jnp.float32)
    bias_cols = lax.dynamic_slice_in_dim(small[3:6], me_expert * head_width, head_width, 1)
    w_route = jnp.concatenate([small[6:], small[2:3]], axis=0)

    plane_tokens = lax.all_gather(tokens, "expert", axis=0, tiled=True)
    plane_docs = lax.all_gather(segment_ids, "expert", axis=0, tiled=True)
    cols_qkv = lax.dynamic_slice_in_dim(
        qkv_weight.reshape(shard_width, 3, model_width), me_expert * head_width, head_width, 2
    ).reshape(shard_width, 3 * head_width)
    cols_out = lax.dynamic_slice_in_dim(out_weight, me_expert * head_width, head_width, 1)
    attn_weights = lax.all_gather(
        jnp.concatenate([cols_qkv, cols_out], axis=1), "dp", axis=0, tiled=True
    )
    w_qkv = attn_weights[:, : 3 * head_width]
    w_out = lax.all_to_all(
        attn_weights[:, 3 * head_width :], "expert", split_axis=0, concat_axis=1, tiled=True
    )

    expert_full = jnp.concatenate([expert_up[0], expert_down[0][:, None, :]], axis=1)
    expert_units = lax.all_to_all(expert_full, "dp", split_axis=0, concat_axis=2, tiled=True)
    shared_units = lax.dynamic_slice_in_dim(shared_weight, me_expert * units, units, 0)
    mlp_weight = jnp.concatenate([expert_units, shared_units], axis=0)
    routed_units = expert_units.shape[0]
    all_units = routed_units + units

    all_cot = gather_all(cotangent)
    all_routes = gather_all(routes)

    plane_resid = plane_tokens.astype(jnp.float32)
    normed_one = (plane_resid * rms_scale(plane_resid) * gain_one).astype(jnp.bfloat16)
    qkv_rows = jnp.dot(normed_one, w_qkv, preferred_element_type=jnp.float32) + bias_cols.reshape(
        -1
    ).astype(jnp.float32)
    qkv_rows = qkv_rows.reshape(num_expert, seq_len, 3, head_count, HEAD)
    cosine_table, sine_table = rope_tables(seq_len, HEAD)
    query_rows = rotate(qkv_rows[:, :, 0], cosine_table, sine_table).astype(jnp.bfloat16)
    key_rows = rotate(qkv_rows[:, :, 1], cosine_table, sine_table).astype(jnp.bfloat16)
    value_rows = qkv_rows[:, :, 2].astype(jnp.bfloat16)
    positions = jnp.arange(seq_len)
    allowed = (
        (plane_docs[:, :, None] == plane_docs[:, None, :])
        & (positions[:, None] >= positions[None, :])[None]
    )[:, None]
    scores = (
        jnp.einsum("bthd,bshd->bhts", query_rows, key_rows, preferred_element_type=jnp.float32)
        * score_scale
    )
    scores = jnp.where(allowed, scores, NEGATIVE)
    exp_scores = jnp.exp(scores - jnp.max(scores, axis=-1, keepdims=True))
    attn_probs = exp_scores / jnp.sum(exp_scores, axis=-1, keepdims=True)
    probs_low = attn_probs.astype(jnp.bfloat16)
    mixed_heads = (
        jnp.einsum("bhts,bshd->bthd", probs_low, value_rows, preferred_element_type=jnp.float32)
        .reshape(plane_rows, head_width)
        .astype(jnp.bfloat16)
    )
    attn_part = jnp.dot(mixed_heads, w_out, preferred_element_type=jnp.float32)
    attn_out = lax.psum_scatter(
        attn_part.astype(jnp.bfloat16), "expert", scatter_dimension=0, tiled=True
    )

    resid_in = tokens.astype(jnp.float32)
    hidden_state = resid_in + attn_out.astype(jnp.float32)
    rms_two = rms_scale(hidden_state)
    normed_two = (hidden_state * rms_two * gain_two).astype(jnp.bfloat16)

    all_normed = gather_all(normed_two)
    all_logits = jnp.einsum(
        "td,ed->te", all_normed, w_route, preferred_element_type=jnp.float32
    )
    all_probs = jax.nn.softmax(all_logits[:, :num_expert], axis=-1)
    all_named = jnp.any(all_routes == me_expert, axis=1)
    my_prob = jnp.sum(
        jnp.where(jnp.arange(num_expert)[None, :] == me_expert, all_probs, 0.0), axis=1
    )
    gate_routed = jnp.where(all_named, my_prob, 0.0)
    gate_shared = jax.nn.sigmoid(all_logits[:, num_expert])
    is_routed = (jnp.arange(all_units) < routed_units)[None, :]
    row_gate = jnp.where(is_routed, gate_routed[:, None], gate_shared[:, None])

    gate_up = jnp.einsum(
        "td,fgd->gtf", all_normed, mlp_weight[:, :2], preferred_element_type=jnp.float32
    )
    silu, d_silu = silu_parts(gate_up[0])
    act = silu * gate_up[1]
    raw_act_grad = jnp.einsum(
        "td,fd->tf", all_cot, mlp_weight[:, 2], preferred_element_type=jnp.float32
    )
    gated_act = (row_gate * act).astype(jnp.bfloat16)
    act_dots = act * raw_act_grad
    d_gate_routed = jnp.where(
        all_named, jnp.sum(jnp.where(is_routed, act_dots, 0.0), axis=1), 0.0
    )
    d_gate_shared = jnp.sum(jnp.where(is_routed, 0.0, act_dots), axis=1)
    act_grad = raw_act_grad * row_gate
    d_gate_up = jnp.stack([act_grad * gate_up[1] * d_silu, act_grad * silu], axis=0).astype(
        jnp.bfloat16
    )
    d_rows = jnp.einsum(
        "gtf,fgd->td", d_gate_up, mlp_weight[:, :2], preferred_element_type=jnp.float32
    ).astype(jnp.bfloat16)
    gate_cols = jnp.concatenate(
        [
            jnp.where(
                jnp.arange(num_expert)[None, :] == me_expert, d_gate_routed[:, None], 0.0
            ),
            d_gate_shared[:, None],
        ],
        axis=1,
    )
    d_gate_cols = scatter_all(gate_cols)
    d_rows_sum = scatter_all(d_rows).astype(jnp.float32)

    up_grad = jnp.einsum(
        "gtf,td->fgd", d_gate_up, all_normed, preferred_element_type=jnp.float32
    ).astype(jnp.bfloat16)
    down_grad = jnp.einsum(
        "tf,td->fd", gated_act, all_cot, preferred_element_type=jnp.float32
    ).astype(jnp.bfloat16)
    out_rows = jnp.dot(gated_act, mlp_weight[:, 2], preferred_element_type=jnp.float32).astype(
        jnp.bfloat16
    )
    output = (hidden_state + scatter_all(out_rows).astype(jnp.float32)).astype(jnp.bfloat16)
    mlp_grad = jnp.concatenate([up_grad, down_grad[:, None, :]], axis=1)
    expert_grad = lax.all_to_all(
        mlp_grad[:routed_units], "dp", split_axis=2, concat_axis=0, tiled=True
    ).astype(jnp.float32)
    shared_grad = lax.all_gather(
        mlp_grad[routed_units:], "expert", axis=0, tiled=True
    ).astype(jnp.float32)

    back_grad = cotangent.astype(jnp.float32)
    logits = jnp.einsum("td,ed->te", normed_two, w_route, preferred_element_type=jnp.float32)
    router_probs = jax.nn.softmax(logits[:, :num_expert], axis=-1)
    logistic_gate = jax.nn.sigmoid(logits[:, num_expert:])
    d_router_probs = d_gate_cols[:, :num_expert]
    d_logits = router_probs * (
        d_router_probs - jnp.sum(router_probs * d_router_probs, axis=-1, keepdims=True)
    )
    d_gate_logit = d_gate_cols[:, num_expert:] * logistic_gate * (1.0 - logistic_gate)
    d_route = jnp.concatenate([d_logits, d_gate_logit], axis=1).astype(jnp.bfloat16)
    route_grad = jnp.einsum("td,te->ed", normed_two, d_route, preferred_element_type=jnp.float32)
    d_normed = d_rows_sum + jnp.dot(d_route, w_route, preferred_element_type=jnp.float32)
    ffn_gain_grad, d_hidden = norm_back(hidden_state, rms_two, gain_two, d_normed)
    d_hidden = back_grad + d_hidden

    d_attn_out = lax.all_gather(d_hidden.astype(jnp.bfloat16), "expert", axis=0, tiled=True)
    out_grad = jnp.einsum(
        "td,te->de", mixed_heads, d_attn_out, preferred_element_type=jnp.float32
    ).astype(jnp.bfloat16)
    out_grad = lax.all_to_all(out_grad, "expert", split_axis=1, concat_axis=0, tiled=True)
    d_mixed = (
        jnp.einsum("te,de->td", d_attn_out, w_out, preferred_element_type=jnp.float32)
        .astype(jnp.bfloat16)
        .reshape(num_expert, seq_len, head_count, HEAD)
    )
    values_grad = jnp.einsum(
        "bhts,bthd->bshd", probs_low, d_mixed, preferred_element_type=jnp.float32
    )
    d_probs = jnp.einsum("bthd,bshd->bhts", d_mixed, value_rows, preferred_element_type=jnp.float32)
    d_scores = (
        attn_probs * (d_probs - jnp.sum(attn_probs * d_probs, axis=-1, keepdims=True))
    ).astype(jnp.bfloat16)
    d_query = unrotate(
        jnp.einsum("bhts,bshd->bthd", d_scores, key_rows, preferred_element_type=jnp.float32)
        * score_scale,
        cosine_table,
        sine_table,
    )
    d_keys = unrotate(
        jnp.einsum("bhts,bthd->bshd", d_scores, query_rows, preferred_element_type=jnp.float32)
        * score_scale,
        cosine_table,
        sine_table,
    )
    d_qkv = (
        jnp.stack([d_query, d_keys, values_grad], axis=2)
        .reshape(plane_rows, 3 * head_width)
        .astype(jnp.bfloat16)
    )
    bias_part = jnp.sum(d_qkv.astype(jnp.float32), axis=0).reshape(3, head_width)
    bias_grad = lax.dynamic_update_slice_in_dim(
        jnp.zeros((3, model_width), jnp.float32), bias_part, me_expert * head_width, 1
    )
    d_normed_one = lax.psum_scatter(
        jnp.einsum("te,de->td", d_qkv, w_qkv, preferred_element_type=jnp.float32).astype(
            jnp.bfloat16
        ),
        "expert",
        scatter_dimension=0,
        tiled=True,
    ).astype(jnp.float32)
    qkv_grad = jnp.einsum(
        "td,te->de", normed_one, d_qkv, preferred_element_type=jnp.float32
    ).astype(jnp.bfloat16)
    attn_grad = lax.psum_scatter(
        jnp.concatenate([qkv_grad, out_grad], axis=1), "dp", scatter_dimension=0, tiled=True
    )
    attn_grad = lax.all_gather(attn_grad, "expert", axis=0).astype(jnp.float32)
    qkv_weight_grad = (
        attn_grad[:, :, : 3 * head_width]
        .reshape(num_expert, shard_width, 3, head_width)
        .transpose(1, 2, 0, 3)
        .reshape(shard_width, 3 * model_width)
    )
    out_weight_grad = (
        attn_grad[:, :, 3 * head_width :].transpose(1, 0, 2).reshape(shard_width, model_width)
    )
    attn_gain_grad, d_input = norm_back(resid_in, rms_scale(resid_in), gain_one, d_normed_one)
    tokens_grad = d_hidden + d_input

    small_grad = jnp.concatenate(
        [attn_gain_grad[None], ffn_gain_grad[None], bias_grad, route_grad], axis=0
    )
    small_grad = lax.psum_scatter(small_grad, "dp", scatter_dimension=1, tiled=True)
    small_grad = lax.psum(small_grad, "expert")
    return (
        output,
        tokens_grad,
        small_grad[0],
        qkv_weight_grad,
        small_grad[2:5],
        out_weight_grad,
        small_grad[1],
        small_grad[5 : 5 + num_expert].T,
        small_grad[5 + num_expert],
        shared_grad,
        expert_grad[None, :, :2],
        expert_grad[None, :, 2],
    )


def solution(mesh):
    return jax.shard_map(
        shards,
        mesh=mesh,
        in_specs=(
            P(("dp", "expert"), None),
            P("dp"),
            P("dp", None),
            P(None, "dp"),
            P("dp", None),
            P("dp"),
            P("dp", None),
            P("dp"),
            P("dp", None, None),
            P("expert", None, None, "dp"),
            P("expert", None, "dp"),
            P(("dp", "expert"), None),
            P(("dp", "expert"), None),
            P(("dp", "expert"), None),
        ),
        out_specs=(
            P(("dp", "expert"), None),
            P(("dp", "expert"), None),
            P("dp"),
            P("dp", None),
            P(None, "dp"),
            P("dp", None),
            P("dp"),
            P("dp", None),
            P("dp"),
            P("dp", None, None),
            P("expert", None, None, "dp"),
            P("expert", None, "dp"),
        ),
        check_vma=False,
    )
```

time: 3640 us -> 1480 us (0.41)
  waiting for transfers between devices: 2950 us -> 606 us
  blocking collectives: 177 us -> 369 us
  local copies, waits for them, and re-layouts: 127 us -> 190 us
  matrix products: 247 us -> 195 us
    all_gather x11 -> x9, waiting for transfers between devices: 1970 us -> 202 us  [the longest x2 91.6 us: gather_all(): rows = lax.all_gather(rows, 'dp', axis=0, tiled=True)]
    unnamed x22 -> x19, waiting for transfers between devices: 410 us -> 1.51 us
    all_to_all x1, blocking collectives: 22.7 us -> 181 us  [shards(): lax.all_to_all(mlp_grad[:routed_units], 'dp', split_axis=2, concat_axis=0...]
    reduce_scatter x5 -> x10, waiting for transfers between devices: 537 us -> 392 us  [the longest x3 146 us: scatter_all(): rows = lax.psum_scatter(rows, 'expert', scatter_dimension=0, tiled=True)]
    all_gather x7 -> x4, blocking collectives: 102 us -> 166 us  [the longest x1 130 us: gather_all(): rows = lax.all_gather(rows, 'dp', axis=0, tiled=True)]
    unnamed x2 -> x0, blocking collectives: 51.8 us -> none
    unnamed x139 -> x113, local copies, waits for them, and re-layouts: 30.5 us -> 74.1 us
    dot_general x27 -> x18, matrix products: 212 us -> 175 us  [the longest x1 27.7 us: shards(): jnp.einsum('gtf,fgd->td', d_gate_up, mlp_weight[:, :2], preferred_element...]
  transfers between devices with their start and end apart: 23 -> 22, of which waited for: 19 -> 14; matrix products, arithmetic and copies ran while one was open for 12% -> 21% of each run, Pallas kernels for 0% -> 0%
where the time goes in v1:
time: 1480 us; the launch traced here: 1460 us
  waiting for transfers between devices  606 us (41%)
  blocking collectives  369 us (25%)
  matrix products  195 us (13%)
  local copies, waits for them, and re-layouts  190 us (13%)
  other arithmetic  73.8 us (5%)
  between operations  15.4 us (1%)
    all_to_all x1, blocking collectives, shards(): lax.all_to_all(mlp_grad[:routed_units], 'dp', split_axis=2, concat_axis=0...  181 us
    reduce_scatter x3, waiting for transfers between devices, scatter_all(): rows = lax.psum_scatter(rows, 'expert', scatter_dimension=0, tiled=True)  146 us
    all_gather x1, blocking collectives, gather_all(): rows = lax.all_gather(rows, 'dp', axis=0, tiled=True)  130 us
    all_gather x2, waiting for transfers between devices, gather_all(): rows = lax.all_gather(rows, 'dp', axis=0, tiled=True)  91.6 us
    reduce_scatter x1, waiting for transfers between devices, shards(): lax.psum_scatter(jnp.concatenate([qkv_grad, out_grad], axis=1), 'dp', sca...  77.5 us
    unnamed x113, local copies, waits for them, and re-layouts  74.1 us
    reduce_scatter x3, waiting for transfers between devices, scatter_all(): return lax.psum_scatter(rows, 'dp', scatter_dimension=0, tiled=True)  62.9 us
    all_gather x1, waiting for transfers between devices, shards(): lax.all_gather(jnp.concatenate([cols_qkv, cols_out], axis=1), 'dp', axis=...  58 us
  transfers between devices with their start and end apart: 22, of which 14 were waited for; matrix products, arithmetic and copies ran while one was open for 21% of the time, Pallas kernels for 0%

profile of v1, /device:TPU:1, one launch (start us, length us, event | category | flops | bytes accessed | tf_op | source)
XLA Modules:
  0.0 1463.3 jit_solution(13131949691227703045)
XLA Ops:
  9.0 8.6 copy.70
  20.9 11.8 all_gather.43
  32.7 11.8 all-gather.1
  45.2 58.0 %all-gather.14.cloned.1.call-done = bf16[2048,1024]{0,1:T(8,128)(2,1)} async-done(((bf16[512,1024]{0,1:T(8,128)(2,1)}), bf16[2048,1024]{0,1:T(8,128)(2,1)}) %all-gather.14.cloned.1.call-update) | async-done | bytes 4194320 | tf_op jit(solution)/shard_map/all_gather | solution.py:132
  109.8 38.0 %all-gather.12.cloned.1.call-done = bf16[1024,2048]{1,0:T(8,128)(2,1)} async-done(((bf16[128,2048]{1,0:T(8,128)(2,1)}), bf16[1024,2048]{1,0:T(8,128)(2,1)}) %all-gather.12.cloned.1.call-update) | async-done | bytes 4194320 | tf_op jit(solution)/shard_map/all_gather | solution.py:126
  150.9 8.3 fusion.47
  159.2 5.2 reshape.298
  181.6 50.8 %reduce-scatter.11.cloned.1.call-done = bf16[128,2048]{1,0:T(8,128)(2,1)} async-done(((bf16[1024,2048]{1,0:T(8,128)(2,1)}), bf16[128,2048]{1,0:T(8,128)(2,1)}) %reduce-scatter.11.cloned.1.call-update) | async-done | bytes 524304 | tf_op jit(solution)/shard_map/reduce_scatter | solution.py:179
  236.4 45.5 %all-gather.16.cloned.1.call-done = bf16[512,2048]{1,0:T(8,128)(2,1)} async-done(((bf16[128,2048]{1,0:T(8,128)(2,1)}), bf16[512,2048]{1,0:T(8,128)(2,1)}) %all-gather.16.cloned.1.call-update) | async-done | bytes 2097168 | tf_op jit(solution)/shard_map/all_gather | solution.py:74
  281.9 46.1 %all-gather.20.cloned.1.call-done = bf16[512,2048]{1,0:T(8,128)(2,1)} async-done(((bf16[128,2048]{1,0:T(8,128)(2,1)}), bf16[512,2048]{1,0:T(8,128)(2,1)}) %all-gather.20.cloned.1.call-update) | async-done | bytes 2097168 | tf_op jit(solution)/shard_map/all_gather | solution.py:74
  328.1 10.8 copy.78
  338.9 8.8 pad_maximum_fusion.1
  347.7 5.3 all-to-all-start.1
  353.1 129.9 %all_gather.46 = s32[512,4]{0,1:T(4,128)S(1)} all-gather(s32[128,4]{0,1:T(4,128)S(1)} %copy-done.44), channel_id=1, replica_groups=mesh['dp'=4,'expert'=8] {'dp'}, dimensions={0}, use_global_device_ids=true | all-gather | bytes 10240 | tf_op jit(solution)/shard_map/all_gather | solution.py:74
  483.0 12.1 all_gather.47
  498.4 8.8 copy.145
  507.2 9.8 all_to_all.55
  517.0 10.3 fusion.85
  527.6 22.6 %fusion.5 = f32[2,4096,528]{1,2,0:T(8,128)} fusion(bf16[4096,2048]{1,0:T(8,128)(2,1)S(1)} %copy-done.4, bf16[176,3,2048]{2,0,1:T(8,128)(2,1)} %constant_dynamic-slice_fusion, bf16[352,3,2048]{2,0,1:T(8,128)(2,1)} %all_to_all.55), kind=kOutput, calls=%fused_computation.11 | convolution fusion | flops 17729716224 | bytes 40566784 | tf_op jit(solution)/shard_map/td,fgd->gtf/dot_general | solution.py:202
  550.2 24.1 %select_reduce_fusion.1 = (f32[4096]{0:T(1024)S(1)}, f32[4096]{0:T(1024)S(1)}, f32[4096,528]{0,1:T(8,128)}, bf16[1,4096,528]{1,2,0:T(8,128)(2,1)}, bf16[1,4096,528]{1,2,0:T(8,128)(2,1)}) fusion(pred[528]{0:T(1024)(128)(4,1)S(1)} %iota_compare_fusion.1, f32[2,4096,528]{1,2,0:T(8,128)} %fusion.5, f32[4096]{0:T(1024)S(1)} %bitcast.232, ...), kind=kOutput, calls=%fused_computation.28 | convolution fusion | flops 8908103680 | bytes 57934352 | tf_op jit(solution)/shard_map/td,fd->tf/dot_general | solution.py:207
  575.3 27.7 %bitcast_convert_fusion = bf16[4096,2048]{1,0:T(8,128)(2,1)} fusion(bf16[1,4096,528]{1,2,0:T(8,128)(2,1)} %get-tuple-element.48, bf16[1,4096,528]{1,2,0:T(8,128)(2,1)} %get-tuple-element.49, bf16[176,3,2048]{2,0,1:T(8,128)(2,1)} %constant_dynamic-slice_fusion, bf16[352,3,2048]{2,0,1:T(8,128)(2,1)} %all_to_all.55), kind=kOutput, calls=%fused_computation.1 | convolution fusion | flops 17738104832 | bytes 31916032 | tf_op jit(solution)/shard_map/gtf,fgd->td/dot_general | solution.py:220
  605.4 119.9 %reduce-scatter.17.cloned.1.call-done = bf16[512,2048]{1,0:T(8,128)(2,1)} async-done(((bf16[4096,2048]{1,0:T(8,128)(2,1)}), bf16[512,2048]{1,0:T(8,128)(2,1)}) %reduce-scatter.17.cloned.1.call-update) | async-done | bytes 2097168 | tf_op jit(solution)/shard_map/reduce_scatter | solution.py:79
  725.7 18.5 %reduce-scatter.23.cloned.1.call-done = f32[128,9]{0,1:T(8,128)} async-done(((f32[512,9]{0,1:T(8,128)}), f32[128,9]{0,1:T(8,128)}) %reduce-scatter.23.cloned.1.call-update) | async-done | bytes 4624 | tf_op jit(solution)/shard_map/reduce_scatter | solution.py:80
  746.3 44.4 %reduce-scatter.19.cloned.1.call-done = bf16[128,2048]{1,0:T(8,128)(2,1)} async-done(((bf16[512,2048]{1,0:T(8,128)(2,1)}), bf16[128,2048]{1,0:T(8,128)(2,1)}) %reduce-scatter.19.cloned.1.call-update) | async-done | bytes 524304 | tf_op jit(solution)/shard_map/reduce_scatter | solution.py:80
  794.8 22.5 %convolution_convert_fusion = bf16[4096,2048]{1,0:T(8,128)(2,1)} fusion(f32[2,4096,528]{1,2,0:T(8,128)} %fusion.5, f32[4096]{0:T(1024)S(1)} %bitcast.233, f32[4096]{0:T(1024)S(1)} %broadcast_select_fusion.2, pred[528]{0:T(1024)(128)(4,1)S(1)} %iota_compare_fusion.1, bf16[176,3,2048]{2,0,1:T(8,128)(2,1)} %constant_dynamic-slice_fusion, ...), kind=kOutput, calls=%fused_computation.6 | convolution fusion | flops 8888385536 | bytes 40600080 | tf_op jit(solution)/shard_map/dot_general | solution.py:241
  817.4 14.1 all-gather.24.cloned.1.call-done
  848.1 9.2 convolution_convert_fusion.2
  866.4 7.8 convolution_convert_fusion.3
  874.3 11.1 all-to-all-done.2
  890.2 23.8 %convert_bitcast_fusion = bf16[528,2,2048]{2,0,1:T(8,128)(2,1)S(1)} fusion(bf16[1,4096,528]{1,2,0:T(8,128)(2,1)} %get-tuple-element.48, bf16[1,4096,528]{1,2,0:T(8,128)(2,1)} %get-tuple-element.49, bf16[4096,2048]{1,0:T(8,128)(2,1)} %all-gather.18.cloned.1.call-done), kind=kOutput, calls=%fused_computation.47 | convolution fusion | flops 17736204288 | bytes 29753344 | tf_op jit(solution)/shard_map/gtf,td->fgd/dot_general | solution.py:235
  914.0 17.0 %fusion.44 = bf16[528,1,2048]{2,0,1:T(8,128)(2,1)S(1)} fusion(bf16[4096,2048]{1,0:T(8,128)(2,1)} %all-gather.22.cloned.1.call-done, f32[4096,528]{0,1:T(8,128)} %get-tuple-element.45, f32[4096]{0:T(1024)S(1)} %bitcast.234, f32[4096]{0:T(1024)S(1)} %broadcast_select_fusion.2, pred[528]{0:T(1024)(128)(4,1)S(1)} %iota_compare_fusion.1), kind=kOutput, calls=%fused_computation.67 | convolution fusion | flops 8865939456 | bytes 27623952 | tf_op jit(solution)/shard_map/tf,td->fd/dot_general | solution.py:238
  934.0 23.9 %reduce-scatter.13.cloned.1.call-done = bf16[512,2048]{1,0:T(8,128)(2,1)} async-done(((bf16[4096,2048]{1,0:T(8,128)(2,1)}), bf16[512,2048]{1,0:T(8,128)(2,1)}) %reduce-scatter.13.cloned.1.call-update) | async-done | bytes 2097168 | tf_op jit(solution)/shard_map/reduce_scatter | solution.py:79
  958.2 54.9 %reduce-scatter.25.cloned.1.call-done = bf16[128,2048]{1,0:T(8,128)(2,1)} async-done(((bf16[1024,2048]{1,0:T(8,128)(2,1)}), bf16[128,2048]{1,0:T(8,128)(2,1)}) %reduce-scatter.25.cloned.1.call-update) | async-done | bytes 524304 | tf_op jit(solution)/shard_map/reduce_scatter | solution.py:306
  1015.3 77.5 %reduce-scatter.29.cloned.1.call-done = bf16[512,1024]{0,1:T(8,128)(2,1)} async-done(((bf16[2048,1024]{0,1:T(8,128)(2,1)}), bf16[512,1024]{0,1:T(8,128)(2,1)}) %reduce-scatter.29.cloned.1.call-update) | async-done | bytes 1048592 | tf_op jit(solution)/shard_map/reduce_scatter | solution.py:317
  1097.7 10.4 copy.94
  1108.1 181.2 %all_to_all.65 = bf16[352,3,2048]{0,1,2:T(4,128)(2,1)} all-to-all(bf16[352,3,2048]{0,1,2:T(4,128)(2,1)} %copy.94), channel_id=1, replica_groups=mesh['dp'=4,'expert'=8] {'dp'}, dimensions={2} | all-to-all | bytes 8650752 | tf_op jit(solution)/shard_map/all_to_all | solution.py:246
  1289.3 11.3 copy.95
  1303.9 12.1 copy.96
  1319.8 19.5 %convert_element_type.251 = f32[1408,3,2048]{2,0,1:T(8,128)} convert(bf16[1408,3,2048]{2,0,1:T(8,128)(2,1)} %all-gather.26.cloned.1.call-done) | non-fusion elementwise | flops 8650752 | bytes 51904512 | tf_op jit(solution)/shard_map/convert_element_type | solution.py:251
  1342.5 22.2 %psum.7 = f32[14,512]{1,0:T(8,128)S(1)} all-reduce(f32[14,512]{1,0:T(8,128)} %reduce-scatter.27.cloned.1.call-done), channel_id=1, replica_groups=mesh['dp'=4,'expert'=8] {'expert'}, use_global_device_ids=true, to_apply=%region_29.30 | all-reduce | flops 7168 | bytes 57344 | tf_op jit(solution)/shard_map/psum | solution.py:337
  1366.5 11.4 convert_element_type.260
  1377.9 19.1 %copy.115 = f32[128,8,8,512]{3,2,1,0:T(8,128)S(1)} copy(f32[128,8,8,512]{3,1,2,0:T(8,128)} %bitcast.198) | data formatting | bytes 33554432
  1397.1 5.7 copy-done.2
  1405.3 10.9 slice.187
  1416.1 13.1 copy.92
  1429.2 15.2 %copy.116 = f32[64,8,24,256]{3,1,2,0:T(8,128)} copy(f32[64,8,24,256]{3,2,1,0:T(8,128)} %bitcast.200) | data formatting | bytes 25165824
  1444.4 5.7 copy.93
  1450.1 6.2 copy.117
  (241 shorter events, 104.8 us)
Async XLA Ops:
  7.2 96.0 %all-gather.14.cloned.1.call-start = ((), (), s32[]{:S(2)}) async-start(), calls=%async_computation.15 | async-start | bytes 5242880 | tf_op jit(solution)/shard_map/all_gather | solution.py:132
  17.6 15.1 %copy-start.52 = (s32[1,128]{1,0:T(1,128)S(1)}, s32[1,128]{1,0:T(1,128)}, u32[]{:S(2)}) copy-start(s32[1,128]{1,0:T(1,128)} %param.26) | copy-start | bytes 1540
  19.9 127.9 %all-gather.12.cloned.1.call-start = ((), (), s32[]{:S(2)}) async-start(), calls=%async_computation.14 | async-start | bytes 4718592 | tf_op jit(solution)/shard_map/all_gather | solution.py:126
  44.9 125.8 %copy-start.27 = (f32[128,64]{1,0:T(8,128)}, f32[128,64]{1,0:T(8,128)S(1)}, u32[]{:S(2)}) copy-start(f32[128,64]{1,0:T(8,128)S(1)} %get-tuple-element.72) | copy-start | bytes 98308
  44.9 125.8 %copy-start.29 = (f32[128,64]{1,0:T(8,128)}, f32[128,64]{1,0:T(8,128)S(1)}, u32[]{:S(2)}) copy-start(f32[128,64]{1,0:T(8,128)S(1)} %get-tuple-element.73) | copy-start | bytes 98308
  45.2 105.8 %copy-start.34 = (f32[1,2048]{1,0:T(1,128)}, f32[1,2048]{1,0:T(1,128)S(1)}, u32[]{:S(2)}) copy-start(f32[1,2048]{1,0:T(1,128)S(1)} %get-tuple-element.68) | copy-start | bytes 24580
  45.2 747.3 %copy-start.32 = (f32[1,2048]{1,0:T(1,128)}, f32[1,2048]{1,0:T(1,128)S(1)}, u32[]{:S(2)}) copy-start(f32[1,2048]{1,0:T(1,128)S(1)} %get-tuple-element.67) | copy-start | bytes 24580
  105.6 72.4 %all-to-all-start = ((bf16[8,256,256]{1,2,0:T(8,128)(2,1)}), bf16[8,256,256]{1,2,0:T(8,128)(2,1)S(1)}, u32[]{:S(2)}, u32[]{:S(2)}) async-start(bf16[8,256,256]{1,2,0:T(8,128)(2,1)} %bitcast.195), calls=%async_computation | async-start | bytes 2097152 | tf_op jit(solution)/shard_map/all_to_all | solution.py:136
  109.8 122.6 %reduce-scatter.11.cloned.1.call-start = ((), (), s32[]{:S(2)}) async-start(), calls=%async_computation.16 | async-start | bytes 4718592 | tf_op jit(solution)/shard_map/reduce_scatter | solution.py:179
  177.9 54.4 %copy-start.3 = (bf16[128,2048]{1,0:T(8,128)(2,1)S(1)}, bf16[128,2048]{1,0:T(8,128)(2,1)}, u32[]{:S(2)}) copy-start(bf16[128,2048]{1,0:T(8,128)(2,1)} %param.14) | copy-start | bytes 1572868
  181.3 100.5 %all-gather.16.cloned.1.call-start = ((), (), s32[]{:S(2)}) async-start(), calls=%async_computation.17 | async-start | bytes 2621440 | tf_op jit(solution)/shard_map/all_gather | solution.py:74
  181.6 146.5 %copy-start.23 = (bf16[1,1408,512]{2,1,0:T(8,128)(2,1)S(1)}, bf16[1,1408,512]{2,1,0:T(8,128)(2,1)}, u32[]{:S(2)}) copy-start(bf16[1,1408,512]{2,1,0:T(8,128)(2,1)} %param.24) | copy-start | bytes 4325380
  233.7 558.8 %copy-start.39 = (f32[128]{0:T(128)}, f32[128]{0:T(128)S(1)}, u32[]{:S(2)}) copy-start(f32[128]{0:T(128)S(1)} %get-tuple-element.77) | copy-start | bytes 1540
  233.7 558.8 %copy-start.45 = (f32[128]{0:T(128)}, f32[128]{0:T(128)S(1)}, u32[]{:S(2)}) copy-start(f32[128]{0:T(128)S(1)} %get-tuple-element.76) | copy-start | bytes 1540
  235.8 92.3 %all-gather.20.cloned.1.call-start = ((), (), s32[]{:S(2)}) async-start(), calls=%async_computation.21 | async-start | bytes 2621440 | tf_op jit(solution)/shard_map/all_gather | solution.py:74
  236.4 280.6 %all-gather.18.cloned.1.call-start = ((), (), s32[]{:S(2)}) async-start(), calls=%async_computation.18 | async-start | bytes 18874368 | tf_op jit(solution)/shard_map/all_gather | solution.py:75
  281.9 268.3 %all-gather.22.cloned.1.call-start = ((), (), s32[]{:S(2)}) async-start(), calls=%async_computation.22 | async-start | bytes 18874368 | tf_op jit(solution)/shard_map/all_gather | solution.py:75
  347.7 150.7 %all-to-all-start.1 = ((bf16[1408,3,512]{2,1,0:T(4,128)(2,1)}), bf16[1408,3,512]{2,1,0:T(4,128)(2,1)}, u32[]{:S(2)}, u32[]{:S(2)}) async-start(bf16[1408,3,512]{2,1,0:T(4,128)(2,1)} %pad_maximum_fusion.1), calls=%async_computation.2 | async-start | bytes 11534336 | tf_op jit(solution)/shard_map/all_to_all | solution.py:141
  353.0 252.3 %reduce-scatter.21.cloned.1.call-start = ((), (), s32[]{:S(2)}) async-start(), calls=%async_computation.25 | async-start | bytes 294912 | tf_op jit(solution)/shard_map/reduce_scatter | solution.py:79
  517.0 10.6 copy-start.4
  575.2 150.1 %reduce-scatter.17.cloned.1.call-start = ((), (), s32[]{:S(2)}) async-start(), calls=%async_computation.23 | async-start | bytes 18874368 | tf_op jit(solution)/shard_map/reduce_scatter | solution.py:79
  603.0 122.4 %copy-start.7 = (bf16[128,2048]{1,0:T(8,128)(2,1)S(1)}, bf16[128,2048]{1,0:T(8,128)(2,1)}, u32[]{:S(2)}) copy-start(bf16[128,2048]{1,0:T(8,128)(2,1)} %multiply_convert_fusion.4) | copy-start | bytes 1572868
  603.0 187.7 %copy-start.8 = (bf16[128,2048]{1,0:T(8,128)(2,1)S(1)}, bf16[128,2048]{1,0:T(8,128)(2,1)}, u32[]{:S(2)}) copy-start(bf16[128,2048]{1,0:T(8,128)(2,1)} %reduce-scatter.11.cloned.1.call-done) | copy-start | bytes 1572868
  603.0 190.5 %copy-start.10 = (bf16[128,2048]{1,0:T(8,128)(2,1)S(1)}, bf16[128,2048]{1,0:T(8,128)(2,1)}, u32[]{:S(2)}) copy-start(bf16[128,2048]{1,0:T(8,128)(2,1)} %param.27) | copy-start | bytes 1572868
  603.0 141.1 %reduce-scatter.23.cloned.1.call-start = ((), (), s32[]{:S(2)}) async-start(), calls=%async_computation.26 | async-start | bytes 40960 | tf_op jit(solution)/shard_map/reduce_scatter | solution.py:80
  605.3 185.4 %reduce-scatter.19.cloned.1.call-start = ((), (), s32[]{:S(2)}) async-start(), calls=%async_computation.24 | async-start | bytes 2621440 | tf_op jit(solution)/shard_map/reduce_scatter | solution.py:80
  725.3 106.2 %all-gather.24.cloned.1.call-start = ((), (), s32[]{:S(2)}) async-start(), calls=%async_computation.27 | async-start | bytes 4718592 | tf_op jit(solution)/shard_map/all_gather | solution.py:268
  792.4 24.9 %copy-start.47 = (f32[128]{0:T(128)}, f32[128]{0:T(128)S(1)}, u32[]{:S(2)}) copy-start(f32[128]{0:T(128)S(1)} %broadcast_multiply_fusion.1) | copy-start | bytes 1540
  794.7 163.2 %reduce-scatter.13.cloned.1.call-start = ((), (), s32[]{:S(2)}) async-start(), calls=%async_computation.19 | async-start | bytes 18874368 | tf_op jit(solution)/shard_map/reduce_scatter | solution.py:79
  817.3 14.2 copy-start.15
  817.4 20.5 %copy-start.37 = (f32[8,2,128]{2,1,0:T(2,128)S(1)}, f32[8,2,128]{2,1,0:T(2,128)}, u32[]{:S(2)}) copy-start(f32[8,2,128]{2,1,0:T(2,128)} %copy-done.36) | copy-start | bytes 24580
  817.4 195.7 %reduce-scatter.25.cloned.1.call-start = ((), (), s32[]{:S(2)}) async-start(), calls=%async_computation.28 | async-start | bytes 4718592 | tf_op jit(solution)/shard_map/reduce_scatter | solution.py:306
  862.8 22.6 %all-to-all-start.2 = ((bf16[256,8,256]{0,2,1:T(8,128)(2,1)}), bf16[256,8,256]{0,2,1:T(8,128)(2,1)S(1)}, u32[]{:S(2)}, u32[]{:S(2)}) async-start(bf16[256,8,256]{0,2,1:T(8,128)(2,1)} %bitcast.39), calls=%async_computation.11 | async-start | bytes 2097152 | tf_op jit(solution)/shard_map/all_to_all | solution.py:272
  866.4 226.3 %reduce-scatter.29.cloned.1.call-start = ((), (), s32[]{:S(2)}) async-start(), calls=%async_computation.30 | async-start | bytes 5242880 | tf_op jit(solution)/shard_map/reduce_scatter | solution.py:317
  890.1 429.7 %all-gather.26.cloned.1.call-start = ((), (), s32[]{:S(2)}) async-start(), calls=%async_computation.31 | async-start | bytes 19464192 | tf_op jit(solution)/shard_map/all_gather | solution.py:249
  914.0 17.1 %copy-start.5 = (bf16[528,2,2048]{2,0,1:T(8,128)(2,1)}, bf16[528,2,2048]{2,0,1:T(8,128)(2,1)S(1)}, u32[]{:S(2)}) copy-start(bf16[528,2,2048]{2,0,1:T(8,128)(2,1)S(1)} %convert_bitcast_fusion) | copy-start | bytes 12976132
  934.0 405.3 %reduce-scatter.15.cloned.1.call-start = ((), (), s32[]{:S(2)}) async-start(), calls=%async_computation.20 | async-start | bytes 2621440 | tf_op jit(solution)/shard_map/reduce_scatter | solution.py:80
  958.0 384.5 %reduce-scatter.27.cloned.1.call-start = ((), (), s32[]{:S(2)}) async-start(), calls=%async_computation.29 | async-start | bytes 163840 | tf_op jit(solution)/shard_map/reduce_scatter | solution.py:336
  1015.2 351.3 %all-gather.28.cloned.1.call-start = ((), (), s32[]{:S(2)}) async-start(), calls=%async_computation.32 | async-start | bytes 9437184 | tf_op jit(solution)/shard_map/all_gather | solution.py:320
  1319.7 19.6 %copy-start.9 = (bf16[128,2048]{1,0:T(8,128)(2,1)S(1)}, bf16[128,2048]{1,0:T(8,128)(2,1)}, u32[]{:S(2)}) copy-start(bf16[128,2048]{1,0:T(8,128)(2,1)} %reduce-scatter.11.cloned.1.call-done) | copy-start | bytes 1572868
  1319.7 19.6 %copy-start.11 = (bf16[128,2048]{1,0:T(8,128)(2,1)S(1)}, bf16[128,2048]{1,0:T(8,128)(2,1)}, u32[]{:S(2)}) copy-start(bf16[128,2048]{1,0:T(8,128)(2,1)} %param.27) | copy-start | bytes 1572868
  1319.7 19.6 %copy-start.13 = (f32[128,2048]{1,0:T(8,128)S(1)}, f32[128,2048]{1,0:T(8,128)}, u32[]{:S(2)}) copy-start(f32[128,2048]{1,0:T(8,128)} %copy-done.12) | copy-start | bytes 3145732
  1319.7 19.6 %copy-start.22 = (bf16[128,2048]{1,0:T(8,128)(2,1)S(1)}, bf16[128,2048]{1,0:T(8,128)(2,1)}, u32[]{:S(2)}) copy-start(bf16[128,2048]{1,0:T(8,128)(2,1)} %reduce-scatter.25.cloned.1.call-done) | copy-start | bytes 1572868
  1319.7 19.6 %copy-start.33 = (f32[1,2048]{1,0:T(1,128)S(1)}, f32[1,2048]{1,0:T(1,128)}, u32[]{:S(2)}) copy-start(f32[1,2048]{1,0:T(1,128)} %copy-done.32) | copy-start | bytes 24580
  1319.8 19.6 %copy-start.40 = (f32[128]{0:T(128)S(1)}, f32[128]{0:T(128)}, u32[]{:S(2)}) copy-start(f32[128]{0:T(128)} %copy-done.39) | copy-start | bytes 1540
  1319.8 19.6 %copy-start.46 = (f32[128]{0:T(128)S(1)}, f32[128]{0:T(128)}, u32[]{:S(2)}) copy-start(f32[128]{0:T(128)} %copy-done.45) | copy-start | bytes 1540
  1319.8 19.6 %copy-start.48 = (f32[128]{0:T(128)S(1)}, f32[128]{0:T(128)}, u32[]{:S(2)}) copy-start(f32[128]{0:T(128)} %copy-done.47) | copy-start | bytes 1540
  1444.4 11.9 copy-start.1
  (27 other events, 105.1 us)
Sparse Core Ops, SparseCore 0:
  20.1 83.0 all-gather.13
  105.1 42.7 all-gather.11
  181.4 50.8 reduce-scatter.10
  235.9 45.9 all-gather.15
  283.4 44.6 all-gather.19
  330.0 88.9 all-gather.17
  421.0 90.1 all-gather.21
  575.4 29.8 reduce-scatter.20
  608.9 116.3 reduce-scatter.16
  727.4 16.7 reduce-scatter.22
  746.6 44.0 reduce-scatter.18
  794.9 36.6 all-gather.23
  835.1 122.8 reduce-scatter.12
  961.7 51.3 reduce-scatter.24
  1015.9 76.8 reduce-scatter.28
  1094.5 92.9 all-gather.25
  1189.7 68.2 reduce-scatter.14
  1260.7 23.1 reduce-scatter.26
  1285.7 56.6 all-gather.27

commit v2 on v1

--- a/solution.py
+++ b/solution.py
@@ -1,8 +1,11 @@
+import functools
 import math
 
 import jax
 import jax.numpy as jnp
 from jax import lax
+from jax.experimental import pallas as pl
+from jax.experimental.pallas import tpu as pltpu
 from jax.sharding import PartitionSpec as P
 
 HEADS = 16
@@ -62,6 +65,454 @@
         scaled * values, axis=-1, keepdims=True
     )
     return (gain_grad, input_grad)
+
+
+MESH = pl.DeviceIdType.MESH
+NT = (((1,), (1,)), ((), ()))
+
+
+def flip(index, step):
+    return index + step - 2 * step * lax.rem(lax.div(index, step), 2)
+
+
+def flip_pair(index, turn):
+    return index + lax.rem(turn, 2) * (1 - 2 * lax.rem(index, 2)) + lax.div(turn, 2) * (
+        2 - 4 * lax.rem(lax.div(index, 2), 2)
+    )
+
+
+def send(source, target, send_sem, recv_sem, device):
+    return pltpu.make_async_remote_copy(
+        src_ref=source,
+        dst_ref=target,
+        send_sem=send_sem,
+        recv_sem=recv_sem,
+        device_id=device,
+        device_id_type=MESH,
+    )
+
+
+def greet(devices):
+    barrier = pltpu.get_barrier_semaphore()
+    for device in devices:
+        pl.semaphore_signal(barrier, inc=1, device_id=device, device_id_type=MESH)
+    pl.semaphore_wait(barrier, len(devices))
+
+
+def mlp_kernel(
+    routed_units,
+    x_own,
+    g_own,
+    cot,
+    w_gu,
+    w_d,
+    x_all,
+    out_part,
+    dx_own,
+    dg_own,
+    acc_gu,
+    acc_d,
+    g_all,
+    x_tile,
+    c_tile,
+    gu_buf,
+    h_buf,
+    dgu_buf,
+    act_buf,
+    out_buf,
+    dx_buf,
+    dg_buf,
+    sib_x,
+    sib_g,
+    cross_x,
+    cross_g,
+    sum_x,
+    sum_g,
+    far_x,
+    far_g,
+    ag_send,
+    ag_recv,
+    gs_send,
+    gs_recv,
+    rs_send,
+    rs_recv,
+    rg_send,
+    rg_recv,
+    local_sem,
+):
+    me_z = lax.axis_index("dp")
+    me_e = lax.axis_index("expert")
+    core = lax.rem(me_e, 2)
+    me_x = lax.rem(lax.div(me_e, 2), 2)
+    me_y = lax.div(me_e, 4)
+    sib = flip(me_e, 1)
+    nbr = {1: sib, 2: flip(me_e, 2), 4: flip(me_e, 4), 6: flip(flip(me_e, 2), 4)}
+    nbr[3], nbr[5], nbr[7] = flip(nbr[2], 1), flip(nbr[4], 1), flip(nbr[6], 1)
+    units, width = w_d.shape
+    rows = x_own.shape[0]
+    tile = 4 * rows
+    chunk = 256
+
+    def z_of(turn):
+        return flip_pair(me_z, turn)
+
+    plane_step = {1: 1, 2: 2, 3: 4, 4: 6}
+    on_step = {5: 2, 6: 4, 7: 6}
+
+    def gather_send(turn, channel):
+        if channel == 0:
+            block, device = (me_z, me_e), (z_of(turn), me_e)
+        elif channel in plane_step:
+            block, device = (z_of(turn), me_e), (me_z, nbr[plane_step[channel]])
+        else:
+            block, device = (z_of(turn), nbr[on_step[channel]]), (me_z, sib)
+        return (
+            send(x_all.at[block], x_all.at[block], ag_send.at[turn, channel], ag_recv.at[turn, channel], device),
+            send(g_all.at[block], g_all.at[block], gs_send.at[turn, channel], gs_recv.at[turn, channel], device),
+        )
+
+    def gather_wait(turn, channel):
+        if channel == 0:
+            block = (z_of(turn), me_e)
+        elif channel in plane_step:
+            block = (z_of(turn), nbr[plane_step[channel]])
+        else:
+            block = (z_of(turn), nbr[on_step[channel] + 1])
+        for buffer, sems in ((x_all, (ag_send, ag_recv)), (g_all, (gs_send, gs_recv))):
+            send(
+                buffer.at[block],
+                buffer.at[block],
+                sems[0].at[turn, channel],
+                sems[1].at[turn, channel],
+                (me_z, sib),
+            ).wait_recv()
+
+    def start(copies):
+        for copy in copies:
+            copy.start()
+
+    def spread(turn):
+        for channel in (4, 2, 3, 1):
+            start(gather_send(turn, channel))
+
+    def pass_on(turn):
+        for channel in (2, 3, 4):
+            gather_wait(turn, channel)
+            start(gather_send(turn, channel + 3))
+
+    def scatter_send(turn, channel):
+        par = lax.rem(turn, 2)
+        if channel < 2:
+            group = me_y if channel == 0 else 1 - me_y
+            source, target, device = (par, 1 - core, group), (par, channel), (me_z, sib)
+            buffers = (dx_buf, sib_x), (dg_buf, sib_g)
+        elif channel < 5:
+            group = me_y if channel == 2 else 1 - me_y
+            column = me_x if channel == 3 else 1 - me_x
+            source, target = (par, core, group, column), (turn, channel - 2)
+            device = (me_z, nbr[(2, 4, 6)[channel - 2]])
+            buffers = (dx_buf, cross_x), (dg_buf, cross_g)
+        else:
+            source, target, device = (turn,), (turn,), (z_of(turn), me_e)
+            buffers = (sum_x, far_x), (sum_g, far_g)
+        (x_from, x_to), (g_from, g_to) = buffers
+        return (
+            send(x_from.at[source], x_to.at[target], rs_send.at[turn, channel], rs_recv.at[turn, channel], device),
+            send(g_from.at[source], g_to.at[target], rg_send.at[turn, channel], rg_recv.at[turn, channel], device),
+        )
+
+    def wait_recv(copies):
+        for copy in copies:
+            copy.wait_recv()
+
+    def wait_send(copies):
+        for copy in copies:
+            copy.wait_send()
+
+    def pair_sum(turn, half):
+        par = lax.rem(turn, 2)
+        wait_recv(scatter_send(turn, half))
+        group = me_y if half == 0 else 1 - me_y
+        for column in range(2):
+
+            @pl.loop(0, rows, step=32)
+            def _(row):
+                span = pl.ds(pl.multiple_of(row, 32), 32)
+                dx_buf[par, core, group, column, span, :] = (
+                    dx_buf[par, core, group, column, span, :].astype(jnp.float32)
+                    + sib_x[par, half, column, span, :].astype(jnp.float32)
+                ).astype(jnp.bfloat16)
+
+            dg_buf[par, core, group, column] = (
+                dg_buf[par, core, group, column] + sib_g[par, half, column]
+            )
+        if half == 0:
+            start(scatter_send(turn, 2))
+        else:
+            start(scatter_send(turn, 4))
+            start(scatter_send(turn, 3))
+
+    def plane_sum(turn):
+        par = lax.rem(turn, 2)
+        for channel in (2, 3, 4):
+            wait_recv(scatter_send(turn, channel))
+
+        @pl.loop(0, rows, step=32)
+        def _(row):
+            span = pl.ds(pl.multiple_of(row, 32), 32)
+            total = dx_buf[par, core, me_y, me_x, span, :].astype(jnp.float32)
+            for k in range(3):
+                total = total + cross_x[turn, k, span, :].astype(jnp.float32)
+            sum_x[turn, span, :] = total.astype(jnp.bfloat16)
+
+        total = dg_buf[par, core, me_y, me_x]
+        for k in range(3):
+            total = total + cross_g[turn, k]
+        sum_g[turn] = total
+
+        @pl.when(turn > 0)
+        def _():
+            start(scatter_send(turn, 5))
+
+        for channel in range(5):
+            wait_send(scatter_send(turn, channel))
+
+    greet(
+        [(z_of(turn), me_e) for turn in (1, 2, 3)]
+        + [(me_z, nbr[step]) for step in (1, 2, 4, 6)]
+    )
+    own = pltpu.make_async_copy(x_own, x_all.at[me_z, me_e], local_sem.at[0])
+    own.start()
+    g_all[me_z, me_e] = g_own[...]
+    own.wait()
+    spread(0)
+    for turn in (1, 2, 3):
+        start(gather_send(turn, 0))
+
+    @pl.loop(0, 2 * units, step=48)
+    def _(row):
+        acc_gu[pl.ds(pl.multiple_of(row, 16), 48), :] = jnp.zeros((48, width), jnp.float32)
+
+    @pl.loop(0, units, step=48)
+    def _(row):
+        acc_d[pl.ds(pl.multiple_of(row, 16), 48), :] = jnp.zeros((48, width), jnp.float32)
+
+    pass_on(0)
+
+    def step(index, carry):
+        turn, half = lax.div(index, 2), lax.rem(index, 2)
+        par = lax.rem(turn, 2)
+        where = z_of(turn)
+        group = lax.rem(me_y + half, 2)
+        block = pl.ds(pl.multiple_of(group * 4, 4), 4)
+
+        c_load = pltpu.make_async_copy(cot.at[block, where], c_tile, local_sem.at[1])
+        c_load.start()
+
+        @pl.when(half == 0)
+        def _():
+            gather_wait(turn, 1)
+            gather_wait(turn, 5)
+
+        @pl.when(half == 1)
+        def _():
+            gather_wait(turn, 6)
+            gather_wait(turn, 7)
+
+        x_load = pltpu.make_async_copy(x_all.at[where, block], x_tile, local_sem.at[0])
+        x_load.start()
+        x_load.wait()
+        c_load.wait()
+        for j in range(2):
+            xs = x_tile[2 * j : 2 * j + 2].reshape(2 * rows, width)
+            cs = c_tile[2 * j : 2 * j + 2].reshape(2 * rows, width)
+            gu_buf[:, 2 * rows * j : 2 * rows * (j + 1)] = lax.dot_general(
+                w_gu[...], xs, NT, preferred_element_type=jnp.float32
+            )
+            h_buf[:, 2 * rows * j : 2 * rows * (j + 1)] = lax.dot_general(
+                w_d[...], cs, NT, preferred_element_type=jnp.float32
+            )
+
+        def gates(row):
+            return jnp.concatenate(
+                [g_all[where, group * 4 + j, pl.ds(row, 1), :] for j in range(4)], axis=1
+            )
+
+        gate_routed = gates(me_e)
+        gate_shared = gates(8)
+        dots = []
+        for low, high, gate in (
+            (0, routed_units, gate_routed),
+            (routed_units, units, gate_shared),
+        ):
+            part = high - low
+            piece = 16
+
+            def units_step(k, dot, low=low, gate=gate):
+                at = pl.multiple_of(low + k * piece, 16)
+                g = gu_buf[pl.ds(at, piece), :]
+                u = gu_buf[pl.ds(pl.multiple_of(units + at, 16), piece), :]
+                h = h_buf[pl.ds(at, piece), :]
+                logistic = jax.nn.sigmoid(g)
+                silu = g * logistic
+                act = silu * u
+                act_buf[pl.ds(at, piece), :] = (act * gate).astype(jnp.bfloat16)
+                d_act = h * gate
+                dgu_buf[pl.ds(at, piece), :] = (
+                    d_act * u * (logistic * (1.0 + g * (1.0 - logistic)))
+                ).astype(jnp.bfloat16)
+                dgu_buf[pl.ds(pl.multiple_of(units + at, 16), piece), :] = (d_act * silu).astype(
+                    jnp.bfloat16
+                )
+                return dot + jnp.sum(act * h, axis=0, keepdims=True)
+
+            dots.append(
+                lax.fori_loop(0, part // piece, units_step, jnp.zeros((1, tile), jnp.float32))
+            )
+        line = lax.broadcasted_iota(jnp.int32, (16, tile), 0)
+        d_gates = jnp.where(line == me_e, dots[0], 0.0) + jnp.where(line == 8, dots[1], 0.0)
+        for j in range(4):
+            dg_buf[par, j % 2, group, j // 2] = d_gates[:, j * rows : (j + 1) * rows]
+
+        xs = x_tile[...].reshape(tile, width)
+        cs = c_tile[...].reshape(tile, width)
+        for n in range(width // chunk):
+            cols = slice(n * chunk, (n + 1) * chunk)
+            acc_gu[:, cols] += jnp.dot(
+                dgu_buf[...], x_tile[:, :, cols].reshape(tile, chunk), preferred_element_type=jnp.float32
+            )
+            acc_d[:, cols] += jnp.dot(
+                act_buf[...], c_tile[:, :, cols].reshape(tile, chunk), preferred_element_type=jnp.float32
+            )
+
+        out_store = pltpu.make_async_copy(out_buf, out_part.at[block, where], local_sem.at[2])
+
+        @pl.when(index > 0)
+        def _():
+            out_store.wait()
+
+        dgu_t = dgu_buf[...].T
+        act_t = act_buf[...].T
+        for n in range(width // chunk):
+            cols = slice(n * chunk, (n + 1) * chunk)
+            dx = jnp.dot(dgu_t, w_gu[:, cols], preferred_element_type=jnp.float32).astype(jnp.bfloat16)
+            out = jnp.dot(act_t, w_d[:, cols], preferred_element_type=jnp.float32).astype(jnp.bfloat16)
+            for j in range(4):
+                dx_buf[par, j % 2, group, j // 2, :, cols] = dx[j * rows : (j + 1) * rows]
+                out_buf[j, :, cols] = out[j * rows : (j + 1) * rows]
+        out_store.start()
+
+        @pl.when(half == 0)
+        def _():
+            start(scatter_send(turn, 0))
+
+            @pl.when(turn < 3)
+            def _():
+                gather_wait(turn + 1, 0)
+                spread(turn + 1)
+
+            @pl.when(turn > 0)
+            def _():
+                pair_sum(turn - 1, 1)
+
+        @pl.when(half == 1)
+        def _():
+            start(scatter_send(turn, 1))
+            pair_sum(turn, 0)
+
+            @pl.when(turn < 3)
+            def _():
+                pass_on(turn + 1)
+
+            @pl.when(turn > 0)
+            def _():
+                plane_sum(turn - 1)
+
+        return carry
+
+    lax.fori_loop(0, 8, step, 0)
+    pair_sum(3, 1)
+    plane_sum(3)
+    pltpu.make_async_copy(out_buf, out_part.at[pl.ds(0, 4), me_z], local_sem.at[2]).wait()
+    for turn in (1, 2, 3):
+        wait_recv(
+            (
+                send(sum_x.at[turn], far_x.at[turn], rs_send.at[turn, 5], rs_recv.at[turn, 5], (me_z, sib)),
+                send(sum_g.at[turn], far_g.at[turn], rg_send.at[turn, 5], rg_recv.at[turn, 5], (me_z, sib)),
+            )
+        )
+
+    @pl.loop(0, rows, step=32)
+    def _(row):
+        span = pl.ds(pl.multiple_of(row, 32), 32)
+        total = sum_x[0, span, :].astype(jnp.float32)
+        for turn in (1, 2, 3):
+            total = total + far_x[turn, span, :].astype(jnp.float32)
+        dx_own[span, :] = total
+
+    dg_own[...] = sum_g[0] + far_g[1] + far_g[2] + far_g[3]
+    for turn in range(4):
+        if turn > 0:
+            wait_send(gather_send(turn, 0))
+            wait_send(scatter_send(turn, 5))
+        for channel in range(1, 8):
+            wait_send(gather_send(turn, channel))
+
+
+def mlp_call(normed_own, gates_own, all_cot, w_gu, w_d, routed_units):
+    num_expert, num_dp, rows, width = all_cot.shape
+    units = w_d.shape[0]
+    low, full = jnp.bfloat16, jnp.float32
+    any_space = pl.BlockSpec(memory_space=pl.ANY)
+    vmem = pl.BlockSpec(memory_space=pltpu.VMEM)
+    dma = pltpu.SemaphoreType.DMA
+    flops = 18 * num_expert * num_dp * rows * units * width
+    return pl.pallas_call(
+        functools.partial(mlp_kernel, routed_units),
+        out_shape=(
+            jax.ShapeDtypeStruct((num_dp, num_expert, rows, width), low),
+            jax.ShapeDtypeStruct((num_expert, num_dp, rows, width), low),
+            jax.ShapeDtypeStruct((rows, width), full),
+            jax.ShapeDtypeStruct((16, rows), full),
+            jax.ShapeDtypeStruct((2 * units, width), full),
+            jax.ShapeDtypeStruct((units, width), full),
+        ),
+        in_specs=[any_space, vmem, any_space, vmem, vmem],
+        out_specs=(any_space, any_space, vmem, vmem, vmem, vmem),
+        scratch_shapes=[
+            pltpu.VMEM((num_dp, num_expert, 16, rows), full),
+            pltpu.VMEM((4, rows, width), low),
+            pltpu.VMEM((4, rows, width), low),
+            pltpu.VMEM((2 * units, 4 * rows), full),
+            pltpu.VMEM((units, 4 * rows), full),
+            pltpu.VMEM((2 * units, 4 * rows), low),
+            pltpu.VMEM((units, 4 * rows), low),
+            pltpu.VMEM((4, rows, width), low),
+            pltpu.VMEM((2, 2, 2, 2, rows, width), low),
+            pltpu.VMEM((2, 2, 2, 2, 16, rows), full),
+            pltpu.VMEM((2, 2, 2, rows, width), low),
+            pltpu.VMEM((2, 2, 2, 16, rows), full),
+            pltpu.VMEM((4, 3, rows, width), low),
+            pltpu.VMEM((4, 3, 16, rows), full),
+            pltpu.VMEM((4, rows, width), low),
+            pltpu.VMEM((4, 16, rows), full),
+            pltpu.VMEM((4, rows, width), low),
+            pltpu.VMEM((4, 16, rows), full),
+            dma((4, 8)),
+            dma((4, 8)),
+            dma((4, 8)),
+            dma((4, 8)),
+            dma((4, 6)),
+            dma((4, 6)),
+            dma((4, 6)),
+            dma((4, 6)),
+            dma((3,)),
+        ],
+        compiler_params=pltpu.CompilerParams(
+            collective_id=0, has_side_effects=True, vmem_limit_bytes=63 * 2**20
+        ),
+        cost_estimate=pl.CostEstimate(flops=flops, bytes_accessed=80 * 2**20, transcendentals=0),
+    )(normed_own, gates_own, all_cot, w_gu, w_d)
 
 
 def silu_parts(gate):
@@ -351,9 +802,244 @@
     )
 
 
+def fast_shards(
+    tokens,
+    attn_gain,
+    qkv_weight,
+    qkv_bias,
+    out_weight,
+    ffn_gain,
+    router_weight,
+    shared_gate_weight,
+    shared_weight,
+    expert_up,
+    expert_down,
+    routes,
+    segment_ids,
+    cotangent,
+):
+    num_dp = lax.axis_size("dp")
+    num_expert = lax.axis_size("expert")
+    me_expert = lax.axis_index("expert")
+    seq_len, model_width = tokens.shape
+    shard_width = qkv_weight.shape[0]
+    head_count = HEADS // num_expert
+    head_width = head_count * HEAD
+    plane_rows = seq_len * num_expert
+    units = shared_weight.shape[0] // num_expert
+    score_scale = HEAD ** (-0.5)
+
+    small = jnp.concatenate(
+        [
+            attn_gain[None],
+            ffn_gain[None],
+            shared_gate_weight[None],
+            qkv_bias,
+            router_weight.T,
+        ],
+        axis=0,
+    )
+    small = lax.all_gather(small, "dp", axis=1, tiled=True)
+    gain_one = small[0].astype(jnp.float32)
+    gain_two = small[1].astype(jnp.float32)
+    bias_cols = lax.dynamic_slice_in_dim(small[3:6], me_expert * head_width, head_width, 1)
+    w_route = jnp.concatenate([small[6:], small[2:3]], axis=0)
+
+    plane_tokens = lax.all_gather(tokens, "expert", axis=0, tiled=True)
+    plane_docs = lax.all_gather(segment_ids, "expert", axis=0, tiled=True)
+    cols_qkv = lax.dynamic_slice_in_dim(
+        qkv_weight.reshape(shard_width, 3, model_width), me_expert * head_width, head_width, 2
+    ).reshape(shard_width, 3 * head_width)
+    cols_out = lax.dynamic_slice_in_dim(out_weight, me_expert * head_width, head_width, 1)
+    attn_weights = lax.all_gather(
+        jnp.concatenate([cols_qkv, cols_out], axis=1), "dp", axis=0, tiled=True
+    )
+    w_qkv = attn_weights[:, : 3 * head_width]
+    w_out = lax.all_to_all(
+        attn_weights[:, 3 * head_width :], "expert", split_axis=0, concat_axis=1, tiled=True
+    )
+
+    expert_full = jnp.concatenate([expert_up[0], expert_down[0][:, None, :]], axis=1)
+    expert_units = lax.all_to_all(expert_full, "dp", split_axis=0, concat_axis=2, tiled=True)
+    shared_units = lax.dynamic_slice_in_dim(shared_weight, me_expert * units, units, 0)
+    mlp_weight = jnp.concatenate([expert_units, shared_units], axis=0)
+    routed_units = expert_units.shape[0]
+    all_units = routed_units + units
+
+    all_cot = gather_all(cotangent)
+
+    plane_resid = plane_tokens.astype(jnp.float32)
+    normed_one = (plane_resid * rms_scale(plane_resid) * gain_one).astype(jnp.bfloat16)
+    qkv_rows = jnp.dot(normed_one, w_qkv, preferred_element_type=jnp.float32) + bias_cols.reshape(
+        -1
+    ).astype(jnp.float32)
+    qkv_rows = qkv_rows.reshape(num_expert, seq_len, 3, head_count, HEAD)
+    cosine_table, sine_table = rope_tables(seq_len, HEAD)
+    query_rows = rotate(qkv_rows[:, :, 0], cosine_table, sine_table).astype(jnp.bfloat16)
+    key_rows = rotate(qkv_rows[:, :, 1], cosine_table, sine_table).astype(jnp.bfloat16)
+    value_rows = qkv_rows[:, :, 2].astype(jnp.bfloat16)
+    positions = jnp.arange(seq_len)
+    allowed = (
+        (plane_docs[:, :, None] == plane_docs[:, None, :])
+        & (positions[:, None] >= positions[None, :])[None]
+    )[:, None]
+    scores = (
+        jnp.einsum("bthd,bshd->bhts", query_rows, key_rows, preferred_element_type=jnp.float32)
+        * score_scale
+    )
+    scores = jnp.where(allowed, scores, NEGATIVE)
+    exp_scores = jnp.exp(scores - jnp.max(scores, axis=-1, keepdims=True))
+    attn_probs = exp_scores / jnp.sum(exp_scores, axis=-1, keepdims=True)
+    probs_low = attn_probs.astype(jnp.bfloat16)
+    mixed_heads = (
+        jnp.einsum("bhts,bshd->bthd", probs_low, value_rows, preferred_element_type=jnp.float32)
+        .reshape(plane_rows, head_width)
+        .astype(jnp.bfloat16)
+    )
+    attn_part = jnp.dot(mixed_heads, w_out, preferred_element_type=jnp.float32)
+    attn_out = lax.psum_scatter(
+        attn_part.astype(jnp.bfloat16), "expert", scatter_dimension=0, tiled=True
+    )
+
+    resid_in = tokens.astype(jnp.float32)
+    hidden_state = resid_in + attn_out.astype(jnp.float32)
+    rms_two = rms_scale(hidden_state)
+    normed_two = (hidden_state * rms_two * gain_two).astype(jnp.bfloat16)
+
+    logits = jnp.einsum("td,ed->te", normed_two, w_route, preferred_element_type=jnp.float32)
+    router_probs = jax.nn.softmax(logits[:, :num_expert], axis=-1)
+    logistic_gate = jax.nn.sigmoid(logits[:, num_expert:])
+    named = jnp.any(routes[:, :, None] == jnp.arange(num_expert)[None, None, :], axis=1)
+    gates = jnp.concatenate([jnp.where(named, router_probs, 0.0), logistic_gate], axis=1).T
+    gates = jnp.pad(gates, ((0, 16 - gates.shape[0]), (0, 0)))
+    w_gu = mlp_weight[:, :2].transpose(1, 0, 2).reshape(2 * all_units, model_width)
+    w_d = mlp_weight[:, 2]
+    _, out_rows, d_rows_sum, d_gate_rows, gu_grad, down_grad = mlp_call(
+        normed_two,
+        gates,
+        all_cot.reshape(num_expert, num_dp, seq_len, model_width),
+        w_gu,
+        w_d,
+        routed_units,
+    )
+    out_rows = out_rows.reshape(num_expert * num_dp * seq_len, model_width)
+    output = (hidden_state + scatter_all(out_rows).astype(jnp.float32)).astype(jnp.bfloat16)
+    d_gate_cols = d_gate_rows[: num_expert + 1].T
+    d_gate_cols = jnp.where(
+        jnp.concatenate([named, jnp.ones((seq_len, 1), bool)], axis=1), d_gate_cols, 0.0
+    )
+    up_grad = gu_grad.reshape(2, all_units, model_width).transpose(1, 0, 2).astype(jnp.bfloat16)
+    down_grad = down_grad.astype(jnp.bfloat16)
+    mlp_grad = jnp.concatenate([up_grad, down_grad[:, None, :]], axis=1)
+    expert_grad = lax.all_to_all(
+        mlp_grad[:routed_units], "dp", split_axis=2, concat_axis=0, tiled=True
+    ).astype(jnp.float32)
+    shared_grad = lax.all_gather(
+        mlp_grad[routed_units:], "expert", axis=0, tiled=True
+    ).astype(jnp.float32)
+
+    back_grad = cotangent.astype(jnp.float32)
+    d_router_probs = d_gate_cols[:, :num_expert]
+    d_logits = router_probs * (
+        d_router_probs - jnp.sum(router_probs * d_router_probs, axis=-1, keepdims=True)
+    )
+    d_gate_logit = d_gate_cols[:, num_expert:] * logistic_gate * (1.0 - logistic_gate)
+    d_route = jnp.concatenate([d_logits, d_gate_logit], axis=1).astype(jnp.bfloat16)
+    route_grad = jnp.einsum("td,te->ed", normed_two, d_route, preferred_element_type=jnp.float32)
+    d_normed = d_rows_sum + jnp.dot(d_route, w_route, preferred_element_type=jnp.float32)
+    ffn_gain_grad, d_hidden = norm_back(hidden_state, rms_two, gain_two, d_normed)
+    d_hidden = back_grad + d_hidden
+
+    d_attn_out = lax.all_gather(d_hidden.astype(jnp.bfloat16), "expert", axis=0, tiled=True)
+    out_grad = jnp.einsum(
+        "td,te->de", mixed_heads, d_attn_out, preferred_element_type=jnp.float32
+    ).astype(jnp.bfloat16)
+    out_grad = lax.all_to_all(out_grad, "expert", split_axis=1, concat_axis=0, tiled=True)
+    d_mixed = (
+        jnp.einsum("te,de->td", d_attn_out, w_out, preferred_element_type=jnp.float32)
+        .astype(jnp.bfloat16)
+        .reshape(num_expert, seq_len, head_count, HEAD)
+    )
+    values_grad = jnp.einsum(
+        "bhts,bthd->bshd", probs_low, d_mixed, preferred_element_type=jnp.float32
+    )
+    d_probs = jnp.einsum("bthd,bshd->bhts", d_mixed, value_rows, preferred_element_type=jnp.float32)
+    d_scores = (
+        attn_probs * (d_probs - jnp.sum(attn_probs * d_probs, axis=-1, keepdims=True))
+    ).astype(jnp.bfloat16)
+    d_query = unrotate(
+        jnp.einsum("bhts,bshd->bthd", d_scores, key_rows, preferred_element_type=jnp.float32)
+        * score_scale,
+        cosine_table,
+        sine_table,
+    )
+    d_keys = unrotate(
+        jnp.einsum("bhts,bthd->bshd", d_scores, query_rows, preferred_element_type=jnp.float32)
+        * score_scale,
+        cosine_table,
+        sine_table,
+    )
+    d_qkv = (
+        jnp.stack([d_query, d_keys, values_grad], axis=2)
+        .reshape(plane_rows, 3 * head_width)
+        .astype(jnp.bfloat16)
+    )
+    bias_part = jnp.sum(d_qkv.astype(jnp.float32), axis=0).reshape(3, head_width)
+    bias_grad = lax.dynamic_update_slice_in_dim(
+        jnp.zeros((3, model_width), jnp.float32), bias_part, me_expert * head_width, 1
+    )
+    d_normed_one = lax.psum_scatter(
+        jnp.einsum("te,de->td", d_qkv, w_qkv, preferred_element_type=jnp.float32).astype(
+            jnp.bfloat16
+        ),
+        "expert",
+        scatter_dimension=0,
+        tiled=True,
+    ).astype(jnp.float32)
+    qkv_grad = jnp.einsum(
+        "td,te->de", normed_one, d_qkv, preferred_element_type=jnp.float32
+    ).astype(jnp.bfloat16)
+    attn_grad = lax.psum_scatter(
+        jnp.concatenate([qkv_grad, out_grad], axis=1), "dp", scatter_dimension=0, tiled=True
+    )
+    attn_grad = lax.all_gather(attn_grad, "expert", axis=0).astype(jnp.float32)
+    qkv_weight_grad = (
+        attn_grad[:, :, : 3 * head_width]
+        .reshape(num_expert, shard_width, 3, head_width)
+        .transpose(1, 2, 0, 3)
+        .reshape(shard_width, 3 * model_width)
+    )
+    out_weight_grad = (
+        attn_grad[:, :, 3 * head_width :].transpose(1, 0, 2).reshape(shard_width, model_width)
+    )
+    attn_gain_grad, d_input = norm_back(resid_in, rms_scale(resid_in), gain_one, d_normed_one)
+    tokens_grad = d_hidden + d_input
+
+    small_grad = jnp.concatenate(
+        [attn_gain_grad[None], ffn_gain_grad[None], bias_grad, route_grad], axis=0
+    )
+    small_grad = lax.psum_scatter(small_grad, "dp", scatter_dimension=1, tiled=True)
+    small_grad = lax.psum(small_grad, "expert")
+    return (
+        output,
+        tokens_grad,
+        small_grad[0],
+        qkv_weight_grad,
+        small_grad[2:5],
+        out_weight_grad,
+        small_grad[1],
+        small_grad[5 : 5 + num_expert].T,
+        small_grad[5 + num_expert],
+        shared_grad,
+        expert_grad[None, :, :2],
+        expert_grad[None, :, 2],
+    )
+
+
 def solution(mesh):
+    cube = mesh.shape["expert"] == 8 and mesh.shape["dp"] == 4
     return jax.shard_map(
-        shards,
+        fast_shards if cube else shards,
         mesh=mesh,
         in_specs=(
             P(("dp", "expert"), None),

time: 1480 us -> 1370 us (0.926)
  Pallas kernels: 0 us -> 299 us
  matrix products: 195 us -> 43.4 us
  blocking collectives: 369 us -> 225 us
  waiting for transfers between devices: 606 us -> 496 us
    pallas_call x0 -> x1, Pallas kernels: none -> 299 us  [mlp_call(): pl.pallas_call(functools.partial(mlp_kernel, routed_units), out_shape=(ja...]
    dot_general x21 -> x14, matrix products: 192 us -> 42.5 us  [the longest x1 8.5 us: fast_shards(): jnp.einsum('td,te->de', normed_one, d_qkv, preferred_element_type=jnp.flo...]
    all_gather x4 -> x2, blocking collectives: 166 us -> 23.6 us  [the longest x1 11.8 us: fast_shards(): plane_docs = lax.all_gather(segment_ids, 'expert', axis=0, tiled=True)]
    all_to_all x3, waiting for transfers between devices: 11.1 us -> 128 us  [the longest x1 125 us: fast_shards(): lax.all_to_all(expert_full, 'dp', split_axis=0, concat_axis=2, tiled=True)]
    reduce_scatter x4, waiting for transfers between devices: 183 us -> 92.9 us  [the longest x1 69.8 us: fast_shards(): lax.psum_scatter(jnp.concatenate([qkv_grad, out_grad], axis=1), 'dp', sca...]
    all_gather x2 -> x1, waiting for transfers between devices: 91.6 us -> 16.1 us  [gather_all(): rows = lax.all_gather(rows, 'dp', axis=0, tiled=True)]
    reduce_scatter x3 -> x1, waiting for transfers between devices: 62.9 us -> 0.01 us  [scatter_all(): return lax.psum_scatter(rows, 'dp', scatter_dimension=0, tiled=True)]
    all_gather x5, waiting for transfers between devices: 110 us -> 139 us  [the longest x1 56.1 us: fast_shards(): lax.all_gather(jnp.concatenate([cols_qkv, cols_out], axis=1), 'dp', axis=...]
  transfers between devices with their start and end apart: 22 -> 16, of which waited for: 14 -> 9; matrix products, arithmetic and copies ran while one was open for 21% -> 12% of each run, Pallas kernels for 0% -> 0%
where the time goes in v2:
time: 1370 us; the launch traced here: 1360 us
  waiting for transfers between devices  496 us (36%)
  Pallas kernels  299 us (22%)
  blocking collectives  225 us (16%)
  local copies, waits for them, and re-layouts  179 us (13%)
  other arithmetic  84.2 us (6%)
  matrix products  43.4 us (3%)
  starting transfers between devices  15.1 us (1%)
  between operations  15.1 us (1%)
    pallas_call x1, Pallas kernels, mlp_call(): pl.pallas_call(functools.partial(mlp_kernel, routed_units), out_shape=(ja...  299 us
    all_to_all x1, blocking collectives, fast_shards(): lax.all_to_all(mlp_grad[:routed_units], 'dp', split_axis=2, concat_axis=0...  179 us
    all_to_all x1, waiting for transfers between devices, fast_shards(): lax.all_to_all(expert_full, 'dp', split_axis=0, concat_axis=2, tiled=True)  125 us
    reduce_scatter x1, waiting for transfers between devices, scatter_all(): rows = lax.psum_scatter(rows, 'expert', scatter_dimension=0, tiled=True)  117 us
    unnamed x86, local copies, waits for them, and re-layouts  80.7 us
    reduce_scatter x1, waiting for transfers between devices, fast_shards(): lax.psum_scatter(jnp.concatenate([qkv_grad, out_grad], axis=1), 'dp', sca...  69.8 us
    all_gather x1, waiting for transfers between devices, fast_shards(): lax.all_gather(jnp.concatenate([cols_qkv, cols_out], axis=1), 'dp', axis=...  56.1 us
    all_gather x1, waiting for transfers between devices, fast_shards(): lax.all_gather(d_hidden.astype(jnp.bfloat16), 'expert', axis=0, tiled=True)  45.2 us
  transfers between devices with their start and end apart: 16, of which 9 were waited for; matrix products, arithmetic and copies ran while one was open for 12% of the time, Pallas kernels for 0%

profile of v2, /device:TPU:1, one launch (start us, length us, event | category | flops | bytes accessed | tf_op | source)
XLA Modules:
  0.0 1357.1 jit_solution(17864993542599291959)
XLA Ops:
  8.4 8.6 copy.130
  21.0 11.8 all_gather.31
  34.1 11.8 all-gather.1
  46.5 56.1 %all-gather.12.cloned.1.call-done = bf16[2048,1024]{0,1:T(8,128)(2,1)} async-done(((bf16[512,1024]{0,1:T(8,128)(2,1)}), bf16[2048,1024]{0,1:T(8,128)(2,1)}) %all-gather.12.cloned.1.call-update) | async-done | bytes 4194320 | tf_op jit(solution)/shard_map/all_gather | solution.py:854
  104.8 4.8 all-to-all-start
  109.6 38.0 %all-gather.10.cloned.1.call-done = bf16[1024,2048]{1,0:T(8,128)(2,1)} async-done(((bf16[128,2048]{1,0:T(8,128)(2,1)}), bf16[1024,2048]{1,0:T(8,128)(2,1)}) %all-gather.10.cloned.1.call-update) | async-done | bytes 4194320 | tf_op jit(solution)/shard_map/all_gather | solution.py:848
  147.7 3.2 fusion.1
  151.1 7.1 fusion.9
  158.2 3.5 reshape.217
  173.7 4.7 convolution_convert_fusion
  178.7 16.1 %all-gather.14.cloned.1.call-done = bf16[512,2048]{1,0:T(8,128)(2,1)} async-done(((bf16[128,2048]{1,0:T(8,128)(2,1)}), bf16[512,2048]{1,0:T(8,128)(2,1)}) %all-gather.14.cloned.1.call-update) | async-done | bytes 2097168 | tf_op jit(solution)/shard_map/all_gather | solution.py:525
  194.8 7.9 copy.138
  202.8 7.0 pad_maximum_fusion
  209.8 5.3 all-to-all-start.1
  217.0 124.6 %all-to-all-done.1 = bf16[1408,3,512]{2,1,0:T(4,128)(2,1)} async-done(((bf16[1408,3,512]{2,1,0:T(4,128)(2,1)}), bf16[1408,3,512]{2,1,0:T(4,128)(2,1)}, u32[]{:S(2)}, u32[]{:S(2)}) %all-to-all-start.1) | async-done | bytes 4325408 | tf_op jit(solution)/shard_map/all_to_all | solution.py:863
  341.6 8.8 copy.206
  350.4 9.4 all_to_all.55
  369.4 299.4 %shard_map.229 = (bf16[4,8,128,2048]{3,2,1,0:T(8,128)(2,1)}, bf16[8,4,128,2048]{3,2,1,0:T(8,128)(2,1)}, f32[128,2048]{1,0:T(8,128)}, f32[16,128]{1,0:T(8,128)}, ...) custom-call(bf16[128,2048]{1,0:T(8,128)(2,1)} %copy-done.6, f32[16,128]{1,0:T(8,128)} %pad.5.g_own, ...), custom_call_target="tpu_custom_call" | custom-call | flops 79725330432 | bytes 83886080 | tf_op jit(solution)/shard_map/pallas_call | solution.py:470
  675.5 45.2 %all-gather.18.cloned.1.call-done = bf16[1024,2048]{1,0:T(8,128)(2,1)} async-done(((bf16[128,2048]{1,0:T(8,128)(2,1)}), bf16[1024,2048]{1,0:T(8,128)(2,1)}) %all-gather.18.cloned.1.call-update) | async-done | bytes 4194320 | tf_op jit(solution)/shard_map/all_gather | solution.py:953
  720.7 3.7 convolution_convert_fusion.5
  733.2 7.9 convolution_convert_fusion.1
  742.2 3.4 convolution_convert_fusion.3
  746.9 3.7 all-to-all-start.2
  750.8 8.5 convolution_convert_fusion.2
  759.3 3.2 all-to-all-done.2
  762.7 5.1 pad_maximum_fusion.2
  769.1 23.1 %reduce-scatter.13.cloned.1.call-done = bf16[128,2048]{1,0:T(8,128)(2,1)} async-done(((bf16[1024,2048]{1,0:T(8,128)(2,1)}), bf16[128,2048]{1,0:T(8,128)(2,1)}) %reduce-scatter.13.cloned.1.call-update) | async-done | bytes 524304 | tf_op jit(solution)/shard_map/reduce_scatter | solution.py:991
  794.3 117.4 %reduce-scatter.9.cloned.1.call-done = bf16[512,2048]{1,0:T(8,128)(2,1)} async-done(((bf16[4096,2048]{1,0:T(8,128)(2,1)}), bf16[512,2048]{1,0:T(8,128)(2,1)}) %reduce-scatter.9.cloned.1.call-update) | async-done | bytes 2097168 | tf_op jit(solution)/shard_map/reduce_scatter | solution.py:530
  911.7 4.1 convert_element_type.229
  915.9 4.1 convert_bitcast_fusion
  921.6 69.8 %reduce-scatter.17.cloned.1.call-done = bf16[512,1024]{0,1:T(8,128)(2,1)} async-done(((bf16[2048,1024]{0,1:T(8,128)(2,1)}), bf16[512,1024]{0,1:T(8,128)(2,1)}) %reduce-scatter.17.cloned.1.call-update) | async-done | bytes 1048592 | tf_op jit(solution)/shard_map/reduce_scatter | solution.py:1002
  991.4 4.4 pad_maximum_fusion.1
  995.8 10.1 copy.169
  1005.9 178.7 %all_to_all.65 = bf16[352,3,2048]{0,1,2:T(4,128)(2,1)} all-to-all(bf16[352,3,2048]{0,1,2:T(4,128)(2,1)} %copy.169), channel_id=1, replica_groups=mesh['dp'=4,'expert'=8] {'dp'}, dimensions={2} | all-to-all | bytes 8650752 | tf_op jit(solution)/shard_map/all_to_all | solution.py:934
  1184.6 11.2 copy.155
  1195.8 3.3 slice_bitcast_fusion
  1199.1 12.1 copy.156
  1211.2 4.0 slice_bitcast_fusion.2
  1215.2 22.6 %psum.7 = f32[14,512]{1,0:T(8,128)S(1)} all-reduce(f32[14,512]{1,0:T(8,128)} %reduce-scatter.15.cloned.1.call-done), channel_id=1, replica_groups=mesh['dp'=4,'expert'=8] {'expert'}, use_global_device_ids=true, to_apply=%region_20.21 | all-reduce | flops 7168 | bytes 57344 | tf_op jit(solution)/shard_map/psum | solution.py:1022
  1242.9 19.4 %convert_element_type.233 = f32[1408,3,2048]{2,0,1:T(8,128)} convert(bf16[1408,3,2048]{2,0,1:T(8,128)(2,1)} %all-gather.20.cloned.1.call-done) | non-fusion elementwise | flops 8650752 | bytes 51904512 | tf_op jit(solution)/shard_map/convert_element_type | solution.py:939
  1262.3 11.4 convert_element_type.242
  1273.7 21.0 %copy.176 = f32[128,8,8,512]{3,2,1,0:T(8,128)} copy(f32[128,8,8,512]{3,1,2,0:T(8,128)} %bitcast.127) | data formatting | bytes 33554432
  1294.7 10.9 slice.170
  1305.5 4.6 slice_bitcast_fusion.1
  1310.2 13.0 copy.152
  1323.2 15.2 %copy.177 = f32[64,8,24,256]{3,1,2,0:T(8,128)} copy(f32[64,8,24,256]{3,2,1,0:T(8,128)} %bitcast.129) | data formatting | bytes 25165824
  1338.4 5.6 copy.153
  1344.0 6.2 copy.178
  (186 shorter events, 60.9 us)
Async XLA Ops:
  7.2 95.3 %all-gather.12.cloned.1.call-start = ((), (), s32[]{:S(2)}) async-start(), calls=%async_computation.11 | async-start | bytes 5242880 | tf_op jit(solution)/shard_map/all_gather | solution.py:854
  17.0 3.8 copy-start.35
  17.0 3.9 copy-start.36
  17.0 3.9 copy-start.37
  17.0 3.9 copy-start.30
  17.0 3.9 copy-start.31
  17.0 17.1 %copy-start.38 = (s32[1,128]{1,0:T(1,128)S(1)}, s32[1,128]{1,0:T(1,128)}, u32[]{:S(2)}) copy-start(s32[1,128]{1,0:T(1,128)} %param.26) | copy-start | bytes 1540
  19.3 128.4 %all-gather.10.cloned.1.call-start = ((), (), s32[]{:S(2)}) async-start(), calls=%async_computation.10 | async-start | bytes 4718592 | tf_op jit(solution)/shard_map/all_gather | solution.py:848
  20.1 174.7 %all-gather.14.cloned.1.call-start = ((), (), s32[]{:S(2)}) async-start(), calls=%async_computation.13 | async-start | bytes 2621440 | tf_op jit(solution)/shard_map/all_gather | solution.py:525
  104.8 68.8 %all-to-all-start = ((bf16[8,256,256]{1,2,0:T(8,128)(2,1)}), bf16[8,256,256]{1,2,0:T(8,128)(2,1)}, u32[]{:S(2)}, u32[]{:S(2)}) async-start(bf16[8,256,256]{1,2,0:T(8,128)(2,1)} %bitcast.124), calls=%async_computation | async-start | bytes 2097152 | tf_op jit(solution)/shard_map/all_to_all | solution.py:858
  109.6 255.5 %reduce-scatter.7.cloned.1.call-start = ((), (), s32[]{:S(2)}) async-start(), calls=%async_computation.12 | async-start | bytes 4718592 | tf_op jit(solution)/shard_map/reduce_scatter | solution.py:900
  147.7 3.4 copy-start.9
  150.9 7.3 copy-start.32
  170.6 3.0 copy-start.15
  170.6 3.0 copy-start.17
  170.6 3.0 copy-start.19
  171.5 6.9 copy-start.21
  171.5 6.9 copy-start.28
  173.6 4.8 copy-start.10
  178.4 24.3 %copy-start.12 = (bf16[1,1408,2,512]{3,2,1,0:T(2,128)(2,1)S(1)}, bf16[1,1408,2,512]{3,2,1,0:T(2,128)(2,1)}, u32[]{:S(2)}) copy-start(bf16[1,1408,2,512]{3,2,1,0:T(2,128)(2,1)} %param.23) | copy-start | bytes 8650756
  178.4 191.0 %all-gather.16.cloned.1.call-start = ((), (), s32[]{:S(2)}) async-start(), calls=%async_computation.14 | async-start | bytes 18874368 | tf_op jit(solution)/shard_map/all_gather | solution.py:526
  209.8 5.4 copy-start.26
  209.8 5.4 copy-start.34
  209.8 131.8 %all-to-all-start.1 = ((bf16[1408,3,512]{2,1,0:T(4,128)(2,1)}), bf16[1408,3,512]{2,1,0:T(4,128)(2,1)}, u32[]{:S(2)}, u32[]{:S(2)}) async-start(bf16[1408,3,512]{2,1,0:T(4,128)(2,1)} %pad_maximum_fusion), calls=%async_computation.2 | async-start | bytes 11534336 | tf_op jit(solution)/shard_map/all_to_all | solution.py:863
  215.1 505.6 %all-gather.18.cloned.1.call-start = ((), (), s32[]{:S(2)}) async-start(), calls=%async_computation.17 | async-start | bytes 4718592 | tf_op jit(solution)/shard_map/all_gather | solution.py:953
  359.8 3.1 copy-start.1
  362.8 2.3 copy-start.2
  362.8 5.7 copy-start.27
  675.0 50.3 %copy-start.22 = (f32[8,2,128,128]{2,3,1,0:T(8,128)S(1)}, f32[8,2,128,128]{2,3,1,0:T(8,128)}, u32[]{:S(2)}) copy-start(f32[8,2,128,128]{2,3,1,0:T(8,128)} %copy-done.21) | copy-start | bytes 3145732
  675.1 50.3 %copy-start.29 = (f32[8,2,128]{2,1,0:T(2,128)S(1)}, f32[8,2,128]{2,1,0:T(2,128)}, u32[]{:S(2)}) copy-start(f32[8,2,128]{2,1,0:T(2,128)} %copy-done.28) | copy-start | bytes 24580
  675.1 117.1 %reduce-scatter.13.cloned.1.call-start = ((), (), s32[]{:S(2)}) async-start(), calls=%async_computation.18 | async-start | bytes 4718592 | tf_op jit(solution)/shard_map/reduce_scatter | solution.py:991
  725.4 1.0 copy-start.23
  726.4 1.9 copy-start.18
  726.4 2.0 copy-start.20
  726.4 2.5 copy-start.14
  726.4 2.5 copy-start.16
  741.1 170.6 %reduce-scatter.9.cloned.1.call-start = ((), (), s32[]{:S(2)}) async-start(), calls=%async_computation.15 | async-start | bytes 18874368 | tf_op jit(solution)/shard_map/reduce_scatter | solution.py:530
  742.2 8.7 copy-start.33
  746.9 15.6 %all-to-all-start.2 = ((bf16[256,8,256]{0,2,1:T(8,128)(2,1)}), bf16[256,8,256]{0,2,1:T(8,128)(2,1)S(1)}, u32[]{:S(2)}, u32[]{:S(2)}) async-start(bf16[256,8,256]{0,2,1:T(8,128)(2,1)} %bitcast.34), calls=%async_computation.7 | async-start | bytes 2097152 | tf_op jit(solution)/shard_map/all_to_all | solution.py:957
  750.7 240.7 %reduce-scatter.17.cloned.1.call-start = ((), (), s32[]{:S(2)}) async-start(), calls=%async_computation.20 | async-start | bytes 5242880 | tf_op jit(solution)/shard_map/reduce_scatter | solution.py:1002
  767.9 447.4 %reduce-scatter.15.cloned.1.call-start = ((), (), s32[]{:S(2)}) async-start(), calls=%async_computation.19 | async-start | bytes 163840 | tf_op jit(solution)/shard_map/reduce_scatter | solution.py:1021
  794.2 445.4 %reduce-scatter.11.cloned.1.call-start = ((), (), s32[]{:S(2)}) async-start(), calls=%async_computation.16 | async-start | bytes 2621440 | tf_op jit(solution)/shard_map/reduce_scatter | solution.py:531
  911.7 331.2 %all-gather.20.cloned.1.call-start = ((), (), s32[]{:S(2)}) async-start(), calls=%async_computation.21 | async-start | bytes 19464192 | tf_op jit(solution)/shard_map/all_gather | solution.py:937
  915.9 4.1 copy-start
  921.5 340.7 %all-gather.22.cloned.1.call-start = ((), (), s32[]{:S(2)}) async-start(), calls=%async_computation.22 | async-start | bytes 9437184 | tf_op jit(solution)/shard_map/all_gather | solution.py:1005
  1211.2 28.5 %copy-start.3 = (bf16[128,2048]{1,0:T(8,128)(2,1)S(1)}, bf16[128,2048]{1,0:T(8,128)(2,1)}, u32[]{:S(2)}) copy-start(bf16[128,2048]{1,0:T(8,128)(2,1)} %reduce-scatter.7.cloned.1.call-done) | copy-start | bytes 1572868
  1211.2 28.5 %copy-start.5 = (f32[128,2048]{1,0:T(8,128)S(1)}, f32[128,2048]{1,0:T(8,128)}, u32[]{:S(2)}) copy-start(f32[128,2048]{1,0:T(8,128)} %copy-done.4) | copy-start | bytes 3145732
  1211.2 28.5 %copy-start.8 = (bf16[128,2048]{1,0:T(8,128)(2,1)S(1)}, bf16[128,2048]{1,0:T(8,128)(2,1)}, u32[]{:S(2)}) copy-start(bf16[128,2048]{1,0:T(8,128)(2,1)} %param.27) | copy-start | bytes 1572868
  (7 other events, 6.2 us)
Sparse Core Ops, SparseCore 0:
  19.4 83.0 all-gather.11
  104.4 43.2 all-gather.9
  149.3 45.5 all-gather.13
  198.6 50.0 reduce-scatter.6
  250.6 90.2 all-gather.15
  675.2 45.5 all-gather.17
  741.2 50.8 reduce-scatter.12
  795.7 115.9 reduce-scatter.8
  914.5 76.8 reduce-scatter.16
  994.2 17.3 reduce-scatter.14
  1013.8 80.5 reduce-scatter.10
  1097.0 104.9 all-gather.19
  1204.0 56.2 all-gather.21

commit v3 on v1

--- a/solution.py
+++ b/solution.py
@@ -1,8 +1,11 @@
+import functools
 import math
 
 import jax
 import jax.numpy as jnp
 from jax import lax
+from jax.experimental import pallas as pl
+from jax.experimental.pallas import tpu as pltpu
 from jax.sharding import PartitionSpec as P
 
 HEADS = 16
@@ -62,6 +65,1922 @@
         scaled * values, axis=-1, keepdims=True
     )
     return (gain_grad, input_grad)
+
+
+MESH = pl.DeviceIdType.MESH
+NT = (((1,), (1,)), ((), ()))
+
+
+def flip(index, step):
+    return index + step - 2 * step * lax.rem(lax.div(index, step), 2)
+
+
+def flip_pair(index, turn):
+    return index + lax.rem(turn, 2) * (1 - 2 * lax.rem(index, 2)) + lax.div(turn, 2) * (
+        2 - 4 * lax.rem(lax.div(index, 2), 2)
+    )
+
+
+def send(source, target, send_sem, recv_sem, device):
+    return pltpu.make_async_remote_copy(
+        src_ref=source,
+        dst_ref=target,
+        send_sem=send_sem,
+        recv_sem=recv_sem,
+        device_id=device,
+        device_id_type=MESH,
+    )
+
+
+def greet(devices):
+    barrier = pltpu.get_barrier_semaphore()
+    for device in devices:
+        pl.semaphore_signal(barrier, inc=1, device_id=device, device_id_type=MESH)
+    pl.semaphore_wait(barrier, len(devices))
+
+TN = (((0,), (0,)), ((), ()))
+
+
+class PlaneGather:
+    def __init__(self, region, send_sem, recv_sem, me_z, me_e, nbr):
+        self.sems = send_sem, recv_sem
+        self.region, self.me_z, self.nbr = region, me_z, nbr
+        out = {1: (me_e, None, 1), 2: (me_e, None, 2), 3: (me_e, None, 4)}
+        out.update({4: (nbr[2], 0, 4), 5: (nbr[4], 1, 2), 6: (nbr[2], None, 1), 7: (nbr[4], None, 1)})
+        out.update({8: (nbr[6], 0, 1), 9: (nbr[6], 1, 1)})
+        self.out = out
+        self.into = {
+            1: (nbr[1], None), 2: (nbr[2], None), 3: (nbr[4], None), 4: (nbr[6], 0), 5: (nbr[6], 1),
+            6: (nbr[3], None), 7: (nbr[5], None), 8: (nbr[7], 0), 9: (nbr[7], 1),
+        }
+
+    def copy(self, channel):
+        owner, half, step = self.out[channel]
+        ref = self.region(owner, half)
+        return send(
+            ref, ref, self.sems[0].at[channel], self.sems[1].at[channel], (self.me_z, self.nbr[step])
+        )
+
+    def start(self, *channels):
+        for channel in channels:
+            self.copy(channel).start()
+
+    def wait(self, *channels):
+        for channel in channels:
+            ref = self.region(*self.into[channel])
+            send(
+                ref, ref, self.sems[0].at[channel], self.sems[1].at[channel], (self.me_z, self.nbr[1])
+            ).wait_recv()
+
+    def begin(self):
+        self.start(2, 3, 1)
+
+    def relay(self):
+        self.wait(2)
+        self.start(4, 6)
+        self.wait(3)
+        self.start(5, 7)
+
+    def relay_far(self):
+        self.wait(4)
+        self.start(8)
+        self.wait(5)
+        self.start(9)
+
+    def finish(self):
+        self.wait(1, 6, 7, 8, 9)
+
+    def drain(self):
+        for channel in range(1, 10):
+            self.copy(channel).wait_send()
+
+
+def add_rows(target, source, rows):
+    @pl.loop(0, rows, step=32)
+    def _(row):
+        span = pl.ds(pl.multiple_of(row, 32), 32)
+        target[span, :] = target[span, :] + source[span, :]
+
+
+class PlaneScatter:
+    def __init__(self, theirs, own, sib, relayed, crossed, sems, place, me_z, nbr):
+        self.theirs, self.own, self.sib, self.relayed, self.crossed = theirs, own, sib, relayed, crossed
+        self.sems, self.me_z, self.nbr = sems, me_z, nbr
+        y, x = place
+        self.own_block, self.far_block = 2 * y + x, 2 * (1 - y) + 1 - x
+        self.x_block, self.y_block = 2 * y + 1 - x, 2 * (1 - y) + x
+        self.rows = crossed.shape[1]
+
+    def copy(self, channel):
+        half = self.rows // 2
+        low, high = pl.ds(0, half), pl.ds(half, half)
+        own, x_block, y_block, far_block = self.own, self.x_block, self.y_block, self.far_block
+        if channel == 0:
+            source, target, step = self.theirs, self.sib, 1
+        elif channel == 1:
+            source, target, step = own.at[far_block, low], self.relayed.at[0], 2
+        elif channel == 2:
+            source, target, step = own.at[far_block, high], self.relayed.at[1], 4
+        elif channel == 3:
+            source, target, step = own.at[x_block, low], self.crossed.at[0, low], 2
+        elif channel == 4:
+            source, target, step = own.at[y_block, high], self.crossed.at[1, high], 4
+        elif channel == 5:
+            source, target, step = own.at[y_block, low], self.crossed.at[1, low], 4
+        else:
+            source, target, step = own.at[x_block, high], self.crossed.at[0, high], 2
+        return send(
+            source,
+            target,
+            self.sems[0].at[channel],
+            self.sems[1].at[channel],
+            (self.me_z, self.nbr[step]),
+        )
+
+    def first(self):
+        self.copy(0).start()
+
+    def second(self):
+        self.copy(0).wait_recv()
+        own, sib = self.own, self.sib
+        add_rows(own.at[self.far_block], sib.at[self.far_block], self.rows)
+        self.copy(1).start()
+        self.copy(2).start()
+        add_rows(own.at[self.x_block], sib.at[self.x_block], self.rows)
+        self.copy(3).start()
+        add_rows(own.at[self.y_block], sib.at[self.y_block], self.rows)
+        self.copy(4).start()
+        add_rows(own.at[self.own_block], sib.at[self.own_block], self.rows)
+
+    def third(self):
+        half = self.rows // 2
+        self.copy(1).wait_recv()
+        add_rows(self.own.at[self.y_block, pl.ds(0, half)], self.relayed.at[0], half)
+        self.copy(2).wait_recv()
+        add_rows(self.own.at[self.x_block, pl.ds(half, half)], self.relayed.at[1], half)
+        self.copy(5).start()
+        self.copy(6).start()
+
+    def fourth(self, store):
+        for channel in (3, 4, 5, 6):
+            self.copy(channel).wait_recv()
+
+        @pl.loop(0, self.rows, step=32)
+        def _(row):
+            span = pl.ds(pl.multiple_of(row, 32), 32)
+            store(
+                span,
+                self.own[self.own_block, span, :].astype(jnp.float32)
+                + self.crossed[0, span, :].astype(jnp.float32)
+                + self.crossed[1, span, :].astype(jnp.float32),
+            )
+
+    def drain(self):
+        for channel in range(7):
+            self.copy(channel).wait_send()
+
+
+class TileScatter(PlaneScatter):
+    def copy(self, channel):
+        if channel not in (0, 7):
+            return super().copy(channel)
+        part = channel // 7
+        return send(
+            self.theirs.at[part],
+            self.sib.at[part],
+            self.sems[0].at[channel],
+            self.sems[1].at[channel],
+            (self.me_z, self.nbr[1]),
+        )
+
+    def sum_near(self):
+        self.copy(0).wait_recv()
+        own, near = self.own, self.sib.at[0]
+        add_rows(own.at[self.x_block], near.at[lax.rem(self.x_block, 2)], self.rows)
+        self.copy(3).start()
+        add_rows(own.at[self.own_block], near.at[lax.rem(self.own_block, 2)], self.rows)
+
+    def sum_far(self):
+        self.copy(7).wait_recv()
+        own, other = self.own, self.sib.at[1]
+        add_rows(own.at[self.far_block], other.at[lax.rem(self.far_block, 2)], self.rows)
+        self.copy(1).start()
+        self.copy(2).start()
+        add_rows(own.at[self.y_block], other.at[lax.rem(self.y_block, 2)], self.rows)
+        self.copy(4).start()
+
+    def drain(self):
+        for channel in range(1, 7):
+            self.copy(channel).wait_send()
+
+
+class ChainGather:
+    def __init__(self, region, send_sem, recv_sem, me_z, me_e):
+        self.region, self.sems, self.me_z, self.me_e = region, (send_sem, recv_sem), me_z, me_e
+
+    def copy(self, way, hop):
+        step = 1 - 2 * way
+        ref = self.region(jnp.clip(self.me_z - step * hop, 0, 3))
+        return send(
+            ref,
+            ref,
+            self.sems[0].at[way, hop],
+            self.sems[1].at[way, hop],
+            (jnp.clip(self.me_z + step, 0, 3), self.me_e),
+        )
+
+    def sends(self, way, hop):
+        z = self.me_z
+        return (z < 3) & (z >= hop) if way == 0 else (z > 0) & (z <= 3 - hop)
+
+    def takes(self, way, hop):
+        z = self.me_z
+        return z > hop if way == 0 else z < 3 - hop
+
+    def begin(self):
+        for way in range(2):
+            pl.when(self.sends(way, 0))(self.copy(way, 0).start)
+
+    def hop(self, hop):
+        for way in range(2):
+            step = 1 - 2 * way
+            ref = self.region(jnp.clip(self.me_z - step * (hop + 1), 0, 3))
+            arrived = send(
+                ref,
+                ref,
+                self.sems[0].at[way, hop],
+                self.sems[1].at[way, hop],
+                (jnp.clip(self.me_z - step, 0, 3), self.me_e),
+            )
+            pl.when(self.takes(way, hop))(arrived.wait_recv)
+            if hop < 2:
+                pl.when(self.sends(way, hop + 1))(self.copy(way, hop + 1).start)
+
+    def drain(self):
+        for hop in range(3):
+            for way in range(2):
+                pl.when(self.sends(way, hop))(self.copy(way, hop).wait_send)
+
+
+class ChainScatter:
+    def __init__(self, part, landing, add, sems, me_z, me_e):
+        self.part, self.landing, self.add = part, landing, add
+        self.sems, self.me_z, self.me_e = sems, me_z, me_e
+
+    def copy(self, way, hop, source, owner):
+        slot = 4 if way == 1 and hop == 2 else owner
+        return send(
+            source,
+            self.landing.at[slot],
+            self.sems[0].at[way, hop],
+            self.sems[1].at[way, hop],
+            (jnp.clip(self.me_z + 1 - 2 * way, 0, 3), self.me_e),
+        )
+
+    def steps(self, hop):
+        for way in range(2):
+            place = self.me_z if way == 0 else 3 - self.me_z
+            owner = jnp.clip(3 - hop + place if way == 0 else hop - place, 0, 3)
+            yield way, place, owner
+
+    def hop(self, hop):
+        for way, place, owner in self.steps(hop):
+
+            @pl.when(place == 0)
+            def _(way=way, owner=owner):
+                self.copy(way, hop, self.part(owner), owner).start()
+
+            @pl.when((place > 0) & (place <= hop))
+            def _(way=way, owner=owner):
+                here = self.landing.at[owner]
+                self.copy(way, hop - 1, here, owner).wait_recv()
+                self.add(owner, owner)
+                self.copy(way, hop, here, owner).start()
+
+    def last(self, low, middle, high):
+        up = self.copy(0, 2, self.landing.at[self.me_z], self.me_z)
+        down = self.copy(1, 2, self.landing.at[4], 4)
+        pl.when(self.me_z > 0)(up.wait_recv)
+        pl.when(self.me_z < 3)(down.wait_recv)
+        pl.when(self.me_z == 0)(low)
+        pl.when((self.me_z > 0) & (self.me_z < 3))(middle)
+        pl.when(self.me_z == 3)(high)
+
+    def drain(self):
+        for hop in range(3):
+            for way, place, owner in self.steps(hop):
+                pl.when(place <= hop)(self.copy(way, hop, self.part(owner), owner).wait_send)
+
+
+def mlp_kernel(
+    routed_units,
+    _x_in,
+    g_all,
+    cot,
+    w_all,
+    up_weight,
+    down_weight,
+    shared_weight,
+    x_all,
+    out_part,
+    dx_own,
+    dg_own,
+    d_routed,
+    shared_all,
+    expert_all,
+    w_gu,
+    w_d,
+    acc_gu,
+    acc_d,
+    stage,
+    x_tile,
+    c_tile,
+    gu_buf,
+    h_buf,
+    dgu_buf,
+    act_buf,
+    out_buf,
+    theirs,
+    own,
+    sib_x,
+    relayed,
+    crossed,
+    sum_x,
+    far_x,
+    dg_all,
+    dg_in,
+    dg_sum,
+    dg_far,
+    a_send,
+    a_recv,
+    z_send,
+    z_recv,
+    r_send,
+    r_recv,
+    fz_send,
+    fz_recv,
+    dp_send,
+    dp_recv,
+    dz_send,
+    dz_recv,
+    local_sem,
+):
+    me_z = lax.axis_index("dp")
+    me_e = lax.axis_index("expert")
+    core = lax.rem(me_e, 2)
+    me_x = lax.rem(lax.div(me_e, 2), 2)
+    me_y = lax.div(me_e, 4)
+    nbr = {1: flip(me_e, 1), 2: flip(me_e, 2), 4: flip(me_e, 4)}
+    nbr[6] = flip(nbr[2], 4)
+    nbr[3], nbr[5], nbr[7] = flip(nbr[2], 1), flip(nbr[4], 1), flip(nbr[6], 1)
+    units, width = w_d.shape
+    rows = x_all.shape[2]
+    tile = 4 * rows
+    chunk = 256
+
+    def z_of(turn):
+        return flip_pair(me_z, turn)
+
+    def gather(turn):
+        where = z_of(turn)
+
+        def region(owner, half):
+            if half is None:
+                return x_all.at[where, owner]
+            return x_all.at[where, owner, pl.ds(half * (rows // 2), rows // 2)]
+
+        return PlaneGather(region, a_send.at[turn], a_recv.at[turn], me_z, me_e, nbr)
+
+    def z_copy(turn, here):
+        block = (z_of(turn) if here else me_z, me_e)
+        return send(
+            x_all.at[block], x_all.at[block], z_send.at[turn], z_recv.at[turn], (z_of(turn), me_e)
+        )
+
+    def slot_of(turn):
+        return turn - 2 * lax.div(turn, 3)
+
+    def scatter(turn):
+        par = lax.rem(turn, 2)
+        return TileScatter(
+            theirs,
+            own.at[slot_of(turn)],
+            sib_x.at[par],
+            relayed.at[par],
+            crossed.at[slot_of(turn)],
+            (r_send.at[turn], r_recv.at[turn]),
+            (me_y, me_x),
+            me_z,
+            nbr,
+        )
+
+    def far_send(turn):
+        return send(
+            sum_x.at[turn], far_x.at[turn - 1], fz_send.at[turn], fz_recv.at[turn], (z_of(turn), me_e)
+        )
+
+    def plane_sum(turn):
+        sums = scatter(turn)
+
+        def store(span, total):
+            sum_x[turn, span, :] = total.astype(jnp.bfloat16)
+
+        sums.fourth(store)
+        pl.when(turn > 0)(lambda: far_send(turn).start())
+        sums.drain()
+
+    greet([(z_of(turn), me_e) for turn in (1, 2, 3)] + [(me_z, nbr[k]) for k in range(1, 8)])
+    z_copy(1, False).start()
+    shard_width = width // 4
+    shared_units = units - routed_units
+
+    def lanes(index):
+        return pl.ds(pl.multiple_of(index * shard_width, shard_width), shard_width)
+
+    def lines(index, amount):
+        return pl.ds(pl.multiple_of(index * amount, 16), amount)
+
+    w_loads = []
+    for part in range(3):
+        target, base = (w_d, 0) if part == 2 else (w_gu, part * units)
+        routed = pl.ds(base, routed_units)
+        own_units = lines(me_z, routed_units)
+        pairs = [
+            (w_all.at[part, :, lanes(z_of(turn))], target.at[routed, lanes(z_of(turn))])
+            for turn in (1, 2, 3)
+        ]
+        pairs.append(
+            (
+                down_weight.at[own_units] if part == 2 else up_weight.at[part, own_units],
+                target.at[routed, lanes(me_z)],
+            )
+        )
+        pairs.append(
+            (
+                shared_weight.at[part, lines(me_e, shared_units)],
+                target.at[pl.ds(base + routed_units, shared_units)],
+            )
+        )
+        for source, place in pairs:
+            w_loads.append(
+                pltpu.make_async_copy(source, place, local_sem.at[3 + len(w_loads)])
+            )
+    for copy in w_loads:
+        copy.start()
+
+    @pl.loop(0, 2 * units, step=48)
+    def _(row):
+        acc_gu[pl.ds(pl.multiple_of(row, 16), 48), :] = jnp.zeros((48, width), jnp.float32)
+
+    @pl.loop(0, units, step=48)
+    def _(row):
+        acc_d[pl.ds(pl.multiple_of(row, 16), 48), :] = jnp.zeros((48, width), jnp.float32)
+
+    def group_of(half):
+        return lax.rem(me_y + half, 2)
+
+    def place_of(index):
+        turn = lax.rem(lax.div(index + 1, 2), 4)
+        ends = 1 - lax.div(index + 6, 7) + lax.div(index, 7)
+        return turn, lax.rem(index + 1 + ends, 2)
+
+    def load(index):
+        turn, half = place_of(index)
+        block = pl.ds(pl.multiple_of(group_of(half) * 4, 4), 4)
+        return (
+            pltpu.make_async_copy(x_all.at[z_of(turn), block], x_tile, local_sem.at[0]),
+            pltpu.make_async_copy(cot.at[block, z_of(turn)], c_tile, local_sem.at[1]),
+        )
+
+
+    for copy in load(0):
+        copy.start()
+    for copy in w_loads:
+        copy.wait()
+
+    def step(index, carry):
+        turn, half = place_of(index)
+        slot = slot_of(turn)
+        pair, odd = lax.div(index, 2), lax.rem(index, 2)
+        where = z_of(turn)
+        group = group_of(half)
+        block = pl.ds(pl.multiple_of(group * 4, 4), 4)
+
+        for copy in load(index):
+            copy.wait()
+        for j in range(2):
+            xs = x_tile[2 * j : 2 * j + 2].reshape(2 * rows, width)
+            cs = c_tile[2 * j : 2 * j + 2].reshape(2 * rows, width)
+            gu_buf[:, 2 * rows * j : 2 * rows * (j + 1)] = lax.dot_general(
+                w_gu[...], xs, NT, preferred_element_type=jnp.float32
+            )
+            h_buf[:, 2 * rows * j : 2 * rows * (j + 1)] = lax.dot_general(
+                w_d[...], cs, NT, preferred_element_type=jnp.float32
+            )
+
+        def gates(row):
+            return jnp.concatenate(
+                [g_all[group * 4 + j, where, pl.ds(row, 1), :] for j in range(4)], axis=1
+            )
+
+        dots = []
+        for low, high, gate in (
+            (0, routed_units, gates(me_e)),
+            (routed_units, units, gates(8)),
+        ):
+            piece = 16
+
+            def units_step(k, dot, low=low, gate=gate):
+                at = pl.multiple_of(low + k * piece, 16)
+                g = gu_buf[pl.ds(at, piece), :]
+                u = gu_buf[pl.ds(pl.multiple_of(units + at, 16), piece), :]
+                h = h_buf[pl.ds(at, piece), :]
+                logistic = jax.nn.sigmoid(g)
+                silu = g * logistic
+                act = silu * u
+                act_buf[pl.ds(at, piece), :] = (act * gate).astype(jnp.bfloat16)
+                d_act = h * gate
+                dgu_buf[pl.ds(at, piece), :] = (
+                    d_act * u * (logistic * (1.0 + g * (1.0 - logistic)))
+                ).astype(jnp.bfloat16)
+                dgu_buf[pl.ds(pl.multiple_of(units + at, 16), piece), :] = (d_act * silu).astype(
+                    jnp.bfloat16
+                )
+                return dot + jnp.sum(act * h, axis=0, keepdims=True)
+
+            dots.append(
+                lax.fori_loop(
+                    0, (high - low) // piece, units_step, jnp.zeros((1, tile), jnp.float32)
+                )
+            )
+        line = lax.broadcasted_iota(jnp.int32, (8, tile), 0)
+        d_gates = jnp.where(line == 0, dots[0], 0.0) + jnp.where(line == 1, dots[1], 0.0)
+        for j in range(4):
+            dg_all[group * 4 + j, where] = d_gates[:, j * rows : (j + 1) * rows]
+
+        @pl.when(index == 0)
+        def _():
+            z_copy(1, True).wait_recv()
+            gather(1).begin()
+            z_copy(2, False).start()
+
+        @pl.when((odd == 1) & (index < 7))
+        def _():
+            gather(pair + 1).relay_far()
+
+        @pl.when((odd == 1) & (index < 5))
+        def _():
+            z_copy(pair + 2, True).wait_recv()
+            gather(pair + 2).begin()
+            pl.when(index == 1)(lambda: z_copy(3, False).start())
+
+        @pl.when((odd == 1) & (index > 4))
+        def _():
+            plane_sum(pair - 1)
+
+        for n in range(width // chunk):
+            cols = slice(n * chunk, (n + 1) * chunk)
+            acc_gu[:, cols] += jnp.dot(
+                dgu_buf[...], x_tile[:, :, cols].reshape(tile, chunk), preferred_element_type=jnp.float32
+            )
+            acc_d[:, cols] += jnp.dot(
+                act_buf[...], c_tile[:, :, cols].reshape(tile, chunk), preferred_element_type=jnp.float32
+            )
+
+        @pl.when((odd == 0) & (index < 6))
+        def _():
+            gather(pair + 1).relay()
+            gather(pair + 1).wait(1, 6)
+
+        @pl.when((odd == 1) & (index < 7))
+        def _():
+            gather(pair + 1).wait(7, 8, 9)
+
+        @pl.when(index < 7)
+        def _():
+            for copy in load(index + 1):
+                copy.start()
+
+        out_store = pltpu.make_async_copy(out_buf, out_part.at[block, where], local_sem.at[2])
+
+        @pl.when(index > 0)
+        def _():
+            out_store.wait()
+
+        @pl.when((odd == 1) & (index < 7))
+        def _():
+            scatter(turn - 1).copy(0).wait_send()
+
+        @pl.when((odd == 0) & (index > 2))
+        def _():
+            scatter(turn - 1).copy(7).wait_send()
+
+        @pl.when(index == 7)
+        def _():
+            scatter(3).copy(7).wait_send()
+
+        dgu_t = dgu_buf[...].T
+        act_t = act_buf[...].T
+        for n in range(width // chunk):
+            cols = slice(n * chunk, (n + 1) * chunk)
+            dx = jnp.dot(dgu_t, w_gu[:, cols], preferred_element_type=jnp.float32).astype(jnp.bfloat16)
+            out = jnp.dot(act_t, w_d[:, cols], preferred_element_type=jnp.float32).astype(jnp.bfloat16)
+            for column in range(2):
+                core_0 = dx[2 * column * rows : (2 * column + 1) * rows]
+                core_1 = dx[(2 * column + 1) * rows : (2 * column + 2) * rows]
+                own[slot, 2 * group + column, :, cols] = jnp.where(core == 0, core_0, core_1)
+                theirs[half, column, :, cols] = jnp.where(core == 0, core_1, core_0)
+            for j in range(4):
+                out_buf[j, :, cols] = out[j * rows : (j + 1) * rows]
+        out_store.start()
+
+        @pl.when(odd == 1)
+        def _():
+            pl.when(index == 1)(lambda: scatter(0).sum_near())
+            pl.when(index > 2)(lambda: scatter(pair).sum_far())
+
+        @pl.when((odd == 0) & (index > 0))
+        def _():
+            pl.when(index > 2)(lambda: scatter(pair - 1).third())
+            scatter(pair).sum_near()
+
+        pl.when(half == 0)(lambda: scatter(turn).copy(0).start())
+        pl.when(half == 1)(lambda: scatter(turn).copy(7).start())
+        return carry
+
+    lax.fori_loop(0, 8, step, 0)
+
+    def dp_copy(step, here):
+        return send(
+            dg_all.at[nbr[step]],
+            dg_in.at[nbr[step] if here else me_e],
+            dp_send.at[step],
+            dp_recv.at[step],
+            (me_z, nbr[step]),
+        )
+
+    for step_to in range(1, 8):
+        dp_copy(step_to, False).start()
+    dg_in[me_e] = dg_all[me_e]
+    scatter(3).third()
+    scatter(0).sum_far()
+
+    depth = stage.shape[1]
+    stores = []
+
+    def write_out(part):
+        for piece in range(units // depth):
+            row, slot = piece * depth, len(stores) % 2
+            if len(stores) > 1:
+                for copy in stores[-2]:
+                    copy.wait()
+            if part == 2:
+                stage[slot] = acc_d[row : row + depth].astype(jnp.bfloat16)
+            else:
+                at = part * units + row
+                stage[slot] = acc_gu[at : at + depth].astype(jnp.bfloat16)
+            if row < routed_units:
+                pairs = [
+                    (stage.at[slot], d_routed.at[part, pl.ds(row, depth)]),
+                    (
+                        stage.at[slot, :, lanes(me_z)],
+                        expert_all.at[
+                            part, pl.ds(pl.multiple_of(me_z * routed_units + row, 16), depth)
+                        ],
+                    ),
+                ]
+            else:
+                at = pl.multiple_of(me_e * shared_units + row - routed_units, 16)
+                pairs = [(stage.at[slot], shared_all.at[part, pl.ds(at, depth)])]
+            stores.append(
+                [
+                    pltpu.make_async_copy(source, place, local_sem.at[2 * slot + 3 + k])
+                    for k, (source, place) in enumerate(pairs)
+                ]
+            )
+            for copy in stores[-1]:
+                copy.start()
+
+    write_out(0)
+    plane_sum(3)
+    scatter(0).third()
+    for step_to in range(1, 8):
+        dp_copy(step_to, True).wait_recv()
+    total_shared = dg_in[0, :, 1:2, :]
+    for source in range(1, 8):
+        total_shared = total_shared + dg_in[source, :, 1:2, :]
+    dg_sum[...] = jnp.concatenate(
+        [dg_in[source, :, 0:1, :] for source in range(8)]
+        + [total_shared, jnp.zeros((4, 7, rows), jnp.float32)],
+        axis=1,
+    )
+
+    def dz_copy(turn):
+        return send(
+            dg_sum.at[z_of(turn)],
+            dg_far.at[turn - 1],
+            dz_send.at[turn],
+            dz_recv.at[turn],
+            (z_of(turn), me_e),
+        )
+
+    for turn in (1, 2, 3):
+        dz_copy(turn).start()
+    write_out(1)
+    plane_sum(0)
+    write_out(2)
+    pltpu.make_async_copy(out_buf, out_part.at[pl.ds(0, 4), me_z], local_sem.at[2]).wait()
+    for turn in (1, 2, 3):
+        dz_copy(turn).wait_recv()
+    dg_own[...] = dg_sum[me_z] + dg_far[0] + dg_far[1] + dg_far[2]
+    for turn in (1, 2, 3):
+        far_send(turn).wait_recv()
+
+    @pl.loop(0, rows, step=32)
+    def _(row):
+        span = pl.ds(pl.multiple_of(row, 32), 32)
+        total = sum_x[0, span, :].astype(jnp.float32)
+        for turn in range(3):
+            total = total + far_x[turn, span, :].astype(jnp.float32)
+        dx_own[span, :] = total
+
+    for copy in stores[-2] + stores[-1]:
+        copy.wait()
+    scatter(3).copy(0).wait_send()
+    scatter(0).copy(7).wait_send()
+    for turn in (1, 2, 3):
+        z_copy(turn, False).wait_send()
+        dz_copy(turn).wait_send()
+        far_send(turn).wait_send()
+    for step_to in range(1, 8):
+        dp_copy(step_to, False).wait_send()
+    for turn in (1, 2, 3):
+        gather(turn).drain()
+
+
+def mlp_call(x_all, gates_all, all_cot, w_all, up_weight, down_weight, shared_weight):
+    num_expert, num_dp, rows, width = all_cot.shape
+    routed_units = w_all.shape[1]
+    units = routed_units + shared_weight.shape[1] // num_expert
+    low, full = jnp.bfloat16, jnp.float32
+    shape = jax.ShapeDtypeStruct
+    any_space = pl.BlockSpec(memory_space=pl.ANY)
+    vmem = pl.BlockSpec(memory_space=pltpu.VMEM)
+    dma = pltpu.SemaphoreType.DMA
+    flops = 18 * num_expert * num_dp * rows * units * width
+    return pl.pallas_call(
+        functools.partial(mlp_kernel, routed_units),
+        out_shape=(
+            shape((num_dp, num_expert, rows, width), low),
+            shape((num_expert, num_dp, rows, width), low),
+            shape((rows, width), full),
+            shape((16, rows), full),
+            shape((3, routed_units, width), low),
+            shape(shared_weight.shape, low),
+            shape((3, num_dp * routed_units, width // num_dp), low),
+        ),
+        in_specs=[any_space, vmem] + [any_space] * 5,
+        input_output_aliases={0: 0},
+        out_specs=(any_space, any_space, vmem, vmem, any_space, any_space, any_space),
+        scratch_shapes=[
+            pltpu.VMEM((2 * units, width), low),
+            pltpu.VMEM((units, width), low),
+            pltpu.VMEM((2 * units, width), full),
+            pltpu.VMEM((units, width), full),
+            pltpu.VMEM((2, units - routed_units, width), low),
+            pltpu.VMEM((4, rows, width), low),
+            pltpu.VMEM((4, rows, width), low),
+            pltpu.VMEM((2 * units, 4 * rows), full),
+            pltpu.VMEM((units, 4 * rows), full),
+            pltpu.VMEM((2 * units, 4 * rows), low),
+            pltpu.VMEM((units, 4 * rows), low),
+            pltpu.VMEM((4, rows, width), low),
+            pltpu.VMEM((2, 2, rows, width), low),
+            pltpu.VMEM((3, 4, rows, width), low),
+            pltpu.VMEM((2, 2, 2, rows, width), low),
+            pltpu.VMEM((2, 2, rows // 2, width), low),
+            pltpu.VMEM((3, 2, rows, width), low),
+            pltpu.VMEM((4, rows, width), low),
+            pltpu.VMEM((3, rows, width), low),
+            pltpu.VMEM((num_expert, num_dp, 8, rows), full),
+            pltpu.VMEM((num_expert, num_dp, 8, rows), full),
+            pltpu.VMEM((num_dp, 16, rows), full),
+            pltpu.VMEM((3, 16, rows), full),
+            dma((4, 10)),
+            dma((4, 10)),
+            dma((4,)),
+            dma((4,)),
+            dma((4, 8)),
+            dma((4, 8)),
+            dma((4,)),
+            dma((4,)),
+            dma((8,)),
+            dma((8,)),
+            dma((4,)),
+            dma((4,)),
+            dma((18,)),
+        ],
+        compiler_params=pltpu.CompilerParams(
+            collective_id=0, has_side_effects=True, vmem_limit_bytes=63 * 2**20
+        ),
+        cost_estimate=pl.CostEstimate(flops=flops, bytes_accessed=80 * 2**20, transcendentals=0),
+    )(x_all, gates_all, all_cot, w_all, up_weight, down_weight, shared_weight)
+
+
+def swap_halves(values):
+    half = values.shape[-1] // 2
+    return jnp.concatenate([values[:, half:], values[:, :half]], axis=1)
+
+
+def tail_kernel(
+    mixed,
+    qkv,
+    probs,
+    normed,
+    w_qkv,
+    w_out,
+    tables,
+    tokens,
+    params,
+    d_rows,
+    d_gates,
+    named,
+    router_probs,
+    normed_two,
+    hidden,
+    cotangent,
+    out_part,
+    d_routed,
+    _shared_in,
+    _expert_in,
+    output,
+    tokens_grad,
+    small_out,
+    attn_all,
+    shared_all,
+    expert_all,
+    rows_all,
+    normed_part,
+    d_mixed,
+    d_qkv,
+    out_grad,
+    grads,
+    grads_in,
+    out_in,
+    grads_sum,
+    n_sib,
+    n_relayed,
+    n_crossed,
+    f_own,
+    f_sib,
+    f_relayed,
+    f_crossed,
+    f_sum,
+    f_far,
+    d_normed,
+    small,
+    small_far,
+    small_plane,
+    e_send,
+    e_recv,
+    a_send,
+    a_recv,
+    o_send,
+    o_recv,
+    z_send,
+    z_recv,
+    y_send,
+    y_recv,
+    n_send,
+    n_recv,
+    f_send,
+    f_recv,
+    fz_send,
+    fz_recv,
+    s_send,
+    s_recv,
+    g_send,
+    g_recv,
+    h_send,
+    h_recv,
+    t_send,
+    t_recv,
+    p_send,
+    p_recv,
+    local_sem,
+):
+    me_z = lax.axis_index("dp")
+    me_e = lax.axis_index("expert")
+    core = lax.rem(me_e, 2)
+    me_x = lax.rem(lax.div(me_e, 2), 2)
+    me_y = lax.div(me_e, 4)
+    nbr = {1: flip(me_e, 1), 2: flip(me_e, 2), 4: flip(me_e, 4)}
+    nbr[6] = flip(nbr[2], 4)
+    nbr[3], nbr[5], nbr[7] = flip(nbr[2], 1), flip(nbr[4], 1), flip(nbr[6], 1)
+    far = {turn: flip_pair(me_z, turn) for turn in (1, 2, 3)}
+    where = {0: me_z, **far}
+    rows, width = tokens.shape
+    head_width = mixed.shape[1]
+    shard_width = width // 4
+    routed_units = d_routed.shape[1]
+    units = shared_all.shape[1] // 8
+    heads = head_width // HEAD
+    sequences = 8
+    score_scale = HEAD ** (-0.5)
+
+    greet([(far[turn], me_e) for turn in (1, 2, 3)] + [(me_z, nbr[k]) for k in range(1, 8)])
+
+    def lanes(index, amount):
+        return pl.ds(pl.multiple_of(index * amount, amount), amount)
+
+    def expert_send(part, turn):
+        return send(
+            d_routed.at[part, :, lanes(far[turn], shard_width)],
+            expert_all.at[part, pl.ds(pl.multiple_of(me_z * routed_units, 16), routed_units)],
+            e_send.at[part, turn],
+            e_recv.at[part, turn],
+            (far[turn], me_e),
+        )
+
+    def expert_wait(part, turn):
+        here = expert_all.at[part, pl.ds(pl.multiple_of(far[turn] * routed_units, 16), routed_units)]
+        send(here, here, e_send.at[part, turn], e_recv.at[part, turn], (far[turn], me_e)).wait_recv()
+
+    split = units // 32 * 16
+
+    def shared_region(owner, half):
+        base = pl.multiple_of(owner * units, 16)
+        if half is None:
+            return shared_all.at[:, pl.ds(base, units)]
+        if half == 0:
+            return shared_all.at[:, pl.ds(base, split)]
+        return shared_all.at[:, pl.ds(pl.multiple_of(base + split, 16), units - split)]
+
+    shared = PlaneGather(shared_region, s_send, s_recv, me_z, me_e, nbr)
+
+    def rows_region(owner, half):
+        if half is None:
+            return rows_all.at[owner]
+        return rows_all.at[owner, pl.ds(half * (rows // 2), rows // 2)]
+
+    gather = PlaneGather(rows_region, a_send, a_recv, me_z, me_e, nbr)
+    forward = {
+        turn: PlaneScatter(
+            out_part.at[:, 1 - core, where[turn]],
+            f_own.at[turn % 2],
+            f_sib.at[turn],
+            f_relayed.at[turn],
+            f_crossed.at[turn],
+            (f_send.at[turn], f_recv.at[turn]),
+            (me_y, me_x),
+            me_z,
+            nbr,
+        )
+        for turn in range(4)
+    }
+
+    def forward_load(turn):
+        return pltpu.make_async_copy(
+            out_part.at[:, core, where[turn]], f_own.at[turn % 2], local_sem.at[3 + turn % 2]
+        )
+
+    def far_send(turn):
+        return send(
+            f_sum.at[turn], f_far.at[turn - 1], fz_send.at[turn], fz_recv.at[turn], (where[turn], me_e)
+        )
+
+    def forward_last(turn):
+        def store(span, total):
+            f_sum[turn, span, :] = total.astype(jnp.bfloat16)
+
+        forward[turn].fourth(store)
+        if turn:
+            far_send(turn).start()
+
+    forward_load(1).start()
+    forward_load(2).start()
+    forward[1].first()
+    forward[2].first()
+
+    top, gate = router_probs[:8], router_probs[8:9]
+    d_top = d_gates[:8] * named[...]
+    d_logits = top * (d_top - jnp.sum(top * d_top, axis=0, keepdims=True))
+    line = lax.broadcasted_iota(jnp.int32, (8, rows), 0)
+    d_rest = jnp.where(line == 0, d_gates[8:9] * gate * (1.0 - gate), 0.0)
+    d_route = jnp.concatenate([d_logits, d_rest], axis=0).astype(jnp.bfloat16)
+    small[...] = jnp.dot(d_route, normed_two[...], preferred_element_type=jnp.float32)
+    d_normed[...] = d_rows[...] + lax.dot_general(
+        d_route, params[...], TN, preferred_element_type=jnp.float32
+    )
+    gains = params[...].astype(jnp.float32)
+
+    def norm_back_rows(value, up, gain):
+        scale = lax.rsqrt(jnp.mean(value * value, axis=-1, keepdims=True) + EPS)
+        scaled = gain * up
+        grad = scale * scaled - value * (scale * scale * scale) * jnp.mean(
+            scaled * value, axis=-1, keepdims=True
+        )
+        return grad, jnp.sum(up * value * scale, axis=0, keepdims=True)
+
+    def hidden_step(index, gain_sum):
+        span = pl.ds(pl.multiple_of(index * 16, 16), 16)
+        grad, term = norm_back_rows(hidden[span, :], d_normed[span, :], gains[10:11])
+        grad = cotangent[span, :].astype(jnp.float32) + grad
+        tokens_grad[span, :] = grad
+        rows_all[me_e, span, :] = grad.astype(jnp.bfloat16)
+        return gain_sum + term
+
+    small[10:11, :] = lax.fori_loop(0, rows // 16, hidden_step, jnp.zeros((1, width), jnp.float32))
+    gather.begin()
+    for part in range(3):
+        for turn in (1, 2, 3):
+            expert_send(part, turn).start()
+    gather.relay()
+    forward_load(1).wait()
+    forward[1].second()
+    gather.relay_far()
+    gather.finish()
+    forward[1].third()
+    forward[3].first()
+    forward[0].first()
+
+    all_rows = sequences * rows
+    d_mixed[...] = lax.dot_general(
+        rows_all[...].reshape(all_rows, width), w_out[...], NT, preferred_element_type=jnp.float32
+    ).astype(jnp.bfloat16)
+    for n in range(4):
+        cols = slice(n * shard_width, (n + 1) * shard_width)
+        out_grad[:, cols] = lax.dot_general(
+            mixed[...],
+            rows_all[:, :, cols].reshape(all_rows, shard_width),
+            TN,
+            preferred_element_type=jnp.float32,
+        ).astype(jnp.bfloat16)
+    span_out = pl.ds(pl.multiple_of(me_e * head_width, head_width), head_width)
+
+    def out_send(step):
+        return send(
+            out_grad.at[:, lanes(nbr[step], head_width)],
+            grads.at[3, span_out],
+            o_send.at[step],
+            o_recv.at[step],
+            (me_z, nbr[step]),
+        )
+
+    for step in range(1, 8):
+        out_send(step).start()
+    grads[3, span_out, :] = out_grad[:, lanes(me_e, head_width)]
+    forward_load(2).wait()
+    forward[2].second()
+    forward_last(1)
+
+    def chain_of(first, amount, landing, sems):
+        def part(owner):
+            return grads.at[
+                pl.ds(first, amount), pl.ds(pl.multiple_of(owner * shard_width, shard_width), shard_width)
+            ]
+
+        def add(slot, owner):
+            for index in range(amount):
+
+                @pl.loop(0, shard_width, step=64)
+                def _(row, index=index):
+                    span = pl.ds(pl.multiple_of(row, 64), 64)
+                    theirs = pl.ds(pl.multiple_of(owner * shard_width + row, 64), 64)
+                    landing[slot, index, span, :] = (
+                        landing[slot, index, span, :] + grads[first + index, theirs, :]
+                    )
+
+        def total(*slots):
+            for index in range(amount):
+
+                @pl.loop(0, shard_width, step=64)
+                def _(row, index=index):
+                    span = pl.ds(pl.multiple_of(row, 64), 64)
+                    own = pl.ds(pl.multiple_of(me_z * shard_width + row, 64), 64)
+                    value = grads[first + index, own, :].astype(jnp.float32)
+                    for slot in slots:
+                        value = value + landing[slot, index, span, :].astype(jnp.float32)
+                    grads_sum[first + index, span, :] = value.astype(jnp.bfloat16)
+
+        chain = ChainScatter(part, landing, add, sems, me_z, me_e)
+        last = (lambda: total(4), lambda: total(me_z, 4), lambda: total(me_z))
+        return chain, lambda: chain.last(*last)
+
+    chain, chain_last = chain_of(0, 3, grads_in, (z_send, z_recv))
+    out_chain, out_chain_last = chain_of(3, 1, out_in, (y_send, y_recv))
+
+    def projections_of(first, amount, sems, place):
+        def region(owner, half):
+            cols = lanes(owner, head_width)
+            if half is None:
+                return attn_all.at[pl.ds(first, amount), :, cols]
+            return attn_all.at[
+                pl.ds(first, amount), pl.ds(half * (shard_width // 2), shard_width // 2), cols
+            ]
+
+        own = pltpu.make_async_copy(
+            grads_sum.at[pl.ds(first, amount)], region(me_e, None), local_sem.at[place]
+        )
+        return own, PlaneGather(region, *sems, me_z, me_e, nbr)
+
+    qkv_own, projections = projections_of(0, 3, (g_send, g_recv), 2)
+    out_own, out_projection = projections_of(3, 1, (h_send, h_recv), 7)
+
+    def sequence(index, carry):
+        span = pl.ds(pl.multiple_of(index * rows, rows), rows)
+        for head in range(heads):
+            cols = slice(head * HEAD, (head + 1) * HEAD)
+            query, key, value = qkv[0, span, cols], qkv[1, span, cols], qkv[2, span, cols]
+            up = d_mixed[span, cols]
+            weights = probs[index * heads + head]
+            values_grad = lax.dot_general(
+                weights.astype(jnp.bfloat16), up, TN, preferred_element_type=jnp.float32
+            )
+            d_probs = lax.dot_general(up, value, NT, preferred_element_type=jnp.float32)
+            d_scores = (
+                weights * (d_probs - jnp.sum(weights * d_probs, axis=-1, keepdims=True))
+            ).astype(jnp.bfloat16)
+            d_query = jnp.dot(d_scores, key, preferred_element_type=jnp.float32) * score_scale
+            d_key = (
+                lax.dot_general(d_scores, query, TN, preferred_element_type=jnp.float32)
+                * score_scale
+            )
+            d_query = d_query * tables[0] - swap_halves(d_query) * tables[1]
+            d_key = d_key * tables[0] - swap_halves(d_key) * tables[1]
+            for part, value_of in enumerate((d_query, d_key, values_grad)):
+                base = part * head_width + head * HEAD
+                d_qkv[span, base : base + HEAD] = value_of.astype(jnp.bfloat16)
+        return carry
+
+    def normed_load(n):
+        return pltpu.make_async_copy(
+            normed.at[:, n * 256 : (n + 1) * 256], normed_part.at[n % 2], local_sem.at[5 + n % 2]
+        )
+
+    normed_load(0).start()
+    lax.fori_loop(0, sequences // 2, sequence, 0)
+    for step in range(1, 8):
+        here = grads.at[3, pl.ds(pl.multiple_of(nbr[step] * head_width, head_width), head_width)]
+        send(here, here, o_send.at[step], o_recv.at[step], (me_z, nbr[step])).wait_recv()
+    out_chain.hop(0)
+    shared.begin()
+    forward[2].third()
+    lax.fori_loop(sequences // 2, sequences, sequence, 0)
+
+    for n in range(width // 256):
+        cols = slice(n * 256, (n + 1) * 256)
+        if n < width // 256 - 1:
+            normed_load(n + 1).start()
+        normed_load(n).wait()
+        term = lax.dot_general(
+            normed_part[n % 2], d_qkv[...], TN, preferred_element_type=jnp.float32
+        ).astype(jnp.bfloat16)
+        for part in range(3):
+            grads[part, cols, :] = term[:, part * head_width : (part + 1) * head_width]
+    chain.hop(0)
+    out_chain.hop(1)
+    gather.drain()
+
+    for n in range(width // 256):
+        cols = slice(n * 256, (n + 1) * 256)
+        term = lax.dot_general(
+            d_qkv[...], w_qkv[cols, : 3 * head_width], NT, preferred_element_type=jnp.float32
+        ).astype(jnp.bfloat16)
+        for owner in range(8):
+            mine = lax.rem(owner + core + 1, 2)
+            rows_all[4 * mine + owner // 2, :, cols] = term[owner * rows : (owner + 1) * rows]
+    back = PlaneScatter(
+        rows_all.at[pl.ds(0, 4)],
+        rows_all.at[pl.ds(4, 4)],
+        n_sib,
+        n_relayed,
+        n_crossed,
+        (n_send, n_recv),
+        (me_y, me_x),
+        me_z,
+        nbr,
+    )
+    back.first()
+    bias_terms = jnp.sum(d_qkv[...].astype(jnp.float32), axis=0, keepdims=True)
+    for part in range(3):
+        small[11 + part : 12 + part, lanes(me_e, head_width)] = bias_terms[
+            :, part * head_width : (part + 1) * head_width
+        ]
+    forward_last(2)
+    forward[1].drain()
+    forward_load(3).start()
+    back.second()
+    back.third()
+    out_chain.hop(2)
+    shared.relay()
+    chain.hop(1)
+    out_chain_last()
+    out_own.start()
+    out_own.wait()
+    out_projection.begin()
+    forward_load(3).wait()
+    forward[3].second()
+
+    def keep(span, total):
+        d_normed[span, :] = total
+
+    back.fourth(keep)
+
+    def norm_step(index, gain_sum):
+        span = pl.ds(pl.multiple_of(index * 16, 16), 16)
+        grad, term = norm_back_rows(
+            tokens[span, :].astype(jnp.float32), d_normed[span, :], gains[9:10]
+        )
+        tokens_grad[span, :] = tokens_grad[span, :] + grad
+        return gain_sum + term
+
+    small[9:10, :] = lax.fori_loop(0, rows // 16, norm_step, jnp.zeros((1, width), jnp.float32))
+
+    def small_send(turn):
+        return send(
+            small.at[:, lanes(far[turn], shard_width)],
+            small_far.at[turn],
+            t_send.at[turn],
+            t_recv.at[turn],
+            (far[turn], me_e),
+        )
+
+    for turn in (1, 2, 3):
+        small_send(turn).start()
+    forward[2].drain()
+    forward_load(0).start()
+    forward[3].third()
+    forward_load(0).wait()
+    forward[0].second()
+    out_projection.relay()
+    chain.hop(2)
+    out_projection.relay_far()
+    for turn in (1, 2, 3):
+        small_send(turn).wait_recv()
+    small_plane[me_e] = (
+        small[:, lanes(me_z, shard_width)] + small_far[1] + small_far[2] + small_far[3]
+    )
+
+    def plane_send(step):
+        return send(
+            small_plane.at[me_e],
+            small_plane.at[me_e],
+            p_send.at[step],
+            p_recv.at[step],
+            (me_z, nbr[step]),
+        )
+
+    for step in range(1, 8):
+        plane_send(step).start()
+    forward_last(3)
+    shared.relay_far()
+    forward[0].third()
+    for step in range(1, 8):
+        here = small_plane.at[nbr[step]]
+        send(here, here, p_send.at[step], p_recv.at[step], (me_z, nbr[step])).wait_recv()
+    total = small_plane[0]
+    for index in range(1, 8):
+        total = total + small_plane[index]
+    small_out[...] = total
+
+    chain_last()
+    qkv_own.start()
+    qkv_own.wait()
+    projections.begin()
+    forward_last(0)
+    projections.relay()
+    for turn in (1, 2, 3):
+        far_send(turn).wait_recv()
+
+    @pl.loop(0, rows, step=32)
+    def _(row):
+        span = pl.ds(pl.multiple_of(row, 32), 32)
+        total = f_sum[0, span, :].astype(jnp.float32)
+        for turn in (1, 2, 3):
+            total = total + f_far[turn - 1, span, :].astype(jnp.float32)
+        output[span, :] = (hidden[span, :] + total).astype(jnp.bfloat16)
+
+    projections.relay_far()
+    shared.finish()
+    projections.finish()
+    out_projection.finish()
+    for turn in (1, 2, 3):
+        for part in range(3):
+            expert_wait(part, turn)
+            expert_send(part, turn).wait_send()
+        small_send(turn).wait_send()
+        far_send(turn).wait_send()
+    for step in range(1, 8):
+        out_send(step).wait_send()
+        plane_send(step).wait_send()
+    for turn in (3, 0):
+        forward[turn].drain()
+    chain.drain()
+    out_chain.drain()
+    out_projection.drain()
+    back.drain()
+    shared.drain()
+    projections.drain()
+
+
+def tail_call(
+    mixed, qkv, probs, normed, w_qkv, w_out, tables, tokens, params, d_rows, d_gates, named, router_probs,
+    normed_two, hidden, cotangent, out_part, d_routed, shared_all, expert_all,
+):
+    rows, width = tokens.shape
+    head_width = mixed.shape[1]
+    shard_width = width // 4
+    low, full = jnp.bfloat16, jnp.float32
+    shape = jax.ShapeDtypeStruct
+    any_space = pl.BlockSpec(memory_space=pl.ANY)
+    vmem = pl.BlockSpec(memory_space=pltpu.VMEM)
+    dma = pltpu.SemaphoreType.DMA
+    return pl.pallas_call(
+        tail_kernel,
+        out_shape=(
+            shape((rows, width), low),
+            shape((rows, width), full),
+            shape((16, shard_width), full),
+            shape((4, shard_width, width), low),
+            shape(shared_all.shape, low),
+            shape(expert_all.shape, low),
+        ),
+        in_specs=[vmem] * 3 + [any_space] + [vmem] * 12 + [any_space] * 4,
+        input_output_aliases={18: 4, 19: 5},
+        out_specs=(vmem, vmem, vmem, any_space, any_space, any_space),
+        scratch_shapes=[
+            pltpu.VMEM((8, rows, width), low),
+            pltpu.VMEM((2, 8 * rows, 256), low),
+            pltpu.VMEM((8 * rows, head_width), low),
+            pltpu.VMEM((8 * rows, 3 * head_width), low),
+            pltpu.VMEM((head_width, width), low),
+            pltpu.VMEM((4, width, head_width), low),
+            pltpu.VMEM((5, 3, shard_width, head_width), low),
+            pltpu.VMEM((5, 1, shard_width, head_width), low),
+            pltpu.VMEM((4, shard_width, head_width), low),
+            pltpu.VMEM((4, rows, width), low),
+            pltpu.VMEM((2, rows // 2, width), low),
+            pltpu.VMEM((2, rows, width), low),
+            pltpu.VMEM((2, 4, rows, width), low),
+            pltpu.VMEM((4, 4, rows, width), low),
+            pltpu.VMEM((4, 2, rows // 2, width), low),
+            pltpu.VMEM((4, 2, rows, width), low),
+            pltpu.VMEM((4, rows, width), low),
+            pltpu.VMEM((3, rows, width), low),
+            pltpu.VMEM((rows, width), full),
+            pltpu.VMEM((16, width), full),
+            pltpu.VMEM((4, 16, shard_width), full),
+            pltpu.VMEM((8, 16, shard_width), full),
+            dma((3, 4)),
+            dma((3, 4)),
+            dma((10,)),
+            dma((10,)),
+            dma((8,)),
+            dma((8,)),
+            dma((2, 3)),
+            dma((2, 3)),
+            dma((2, 3)),
+            dma((2, 3)),
+            dma((7,)),
+            dma((7,)),
+            dma((4, 7)),
+            dma((4, 7)),
+            dma((4,)),
+            dma((4,)),
+            dma((10,)),
+            dma((10,)),
+            dma((10,)),
+            dma((10,)),
+            dma((10,)),
+            dma((10,)),
+            dma((4,)),
+            dma((4,)),
+            dma((8,)),
+            dma((8,)),
+            dma((8,)),
+        ],
+        compiler_params=pltpu.CompilerParams(
+            collective_id=1, has_side_effects=True, vmem_limit_bytes=63 * 2**20
+        ),
+        cost_estimate=pl.CostEstimate(
+            flops=24 * 8 * rows * width * head_width, bytes_accessed=80 * 2**20, transcendentals=0
+        ),
+    )(
+        mixed, qkv, probs, normed, w_qkv, w_out, tables, tokens, params, d_rows, d_gates, named, router_probs,
+        normed_two, hidden, cotangent, out_part, d_routed, shared_all, expert_all,
+    )
+
+
+def front_kernel(
+    tokens,
+    docs,
+    params,
+    named,
+    tables,
+    cotangent,
+    qkv_weight,
+    out_weight,
+    up_weight,
+    down_weight,
+    qkv,
+    probs,
+    mixed,
+    normed,
+    hidden,
+    normed_two,
+    gates_all,
+    router_probs,
+    params_all,
+    weights_out,
+    w_out_out,
+    cot_all,
+    w_all,
+    x_all,
+    rows_all,
+    weights,
+    w_out,
+    params_in,
+    docs_all,
+    gates_in,
+    qkv_part,
+    n_sib,
+    n_relayed,
+    n_crossed,
+    a_send,
+    a_recv,
+    w_send,
+    w_recv,
+    p_send,
+    p_recv,
+    d_send,
+    d_recv,
+    o_send,
+    o_recv,
+    n_send,
+    n_recv,
+    c_send,
+    c_recv,
+    k_send,
+    k_recv,
+    e_send,
+    e_recv,
+    x_send,
+    x_recv,
+    y_send,
+    y_recv,
+    g_send,
+    g_recv,
+    local_sem,
+):
+    me_z = lax.axis_index("dp")
+    me_e = lax.axis_index("expert")
+    core = lax.rem(me_e, 2)
+    me_x = lax.rem(lax.div(me_e, 2), 2)
+    me_y = lax.div(me_e, 4)
+    nbr = {1: flip(me_e, 1), 2: flip(me_e, 2), 4: flip(me_e, 4)}
+    nbr[6] = flip(nbr[2], 4)
+    nbr[3], nbr[5], nbr[7] = flip(nbr[2], 1), flip(nbr[4], 1), flip(nbr[6], 1)
+    far = {turn: flip_pair(me_z, turn) for turn in (1, 2, 3)}
+    rows, width = tokens.shape
+    shard_width = qkv_weight.shape[0]
+    head_width = w_out.shape[0]
+    heads = head_width // HEAD
+    routed_units = down_weight.shape[0] // 4
+    sequences = 8
+    score_scale = HEAD ** (-0.5)
+
+    def lanes(index, amount):
+        return pl.ds(pl.multiple_of(index * amount, amount), amount)
+
+    def lines(index, amount, grain=16):
+        return pl.ds(pl.multiple_of(index * amount, grain), amount)
+
+    my_lines = lines(me_z, shard_width)
+    own = [
+        pltpu.make_async_copy(
+            qkv_weight.at[:, pl.ds(pl.multiple_of(part * width + me_e * head_width, head_width), head_width)],
+            weights.at[my_lines, part * head_width : (part + 1) * head_width],
+            local_sem.at[part],
+        )
+        for part in range(3)
+    ]
+    own.append(
+        pltpu.make_async_copy(
+            out_weight.at[:, lanes(me_e, head_width)],
+            weights.at[my_lines, 3 * head_width : 4 * head_width],
+            local_sem.at[3],
+        )
+    )
+    own.append(pltpu.make_async_copy(tokens, rows_all.at[me_e], local_sem.at[4]))
+    own.append(pltpu.make_async_copy(cotangent, cot_all.at[me_e, me_z], local_sem.at[5]))
+    for copy in own:
+        copy.start()
+    params_in[me_z] = params[...]
+    docs_all[me_e] = docs[...]
+    greet([(far[turn], me_e) for turn in (1, 2, 3)] + [(me_z, nbr[k]) for k in range(1, 8)])
+    for copy in own:
+        copy.wait()
+
+    attn_weights = ChainGather(
+        lambda z: weights.at[lines(z, shard_width)], w_send, w_recv, me_z, me_e
+    )
+    attn_weights.begin()
+    cot_chain = ChainGather(lambda z: cot_all.at[me_e, z], k_send, k_recv, me_z, me_e)
+    cot_chain.begin()
+
+    def cot_gather(place, z):
+        def region(owner, half):
+            if half is None:
+                return cot_all.at[owner, z]
+            return cot_all.at[owner, z, pl.ds(half * (rows // 2), rows // 2)]
+
+        return PlaneGather(region, c_send.at[place], c_recv.at[place], me_z, me_e, nbr)
+
+    cot_own = cot_gather(6, me_z)
+
+    def cot_step(hop, name):
+        for way in range(2):
+            z = jnp.clip(me_z - (1 - 2 * way) * (hop + 1), 0, 3)
+            pl.when(cot_chain.takes(way, hop))(getattr(cot_gather(way * 3 + hop, z), name))
+
+    def expert_copy(part, turn, here):
+        source = down_weight if part == 2 else up_weight.at[part]
+        z = far[turn] if here else me_z
+        target = w_all.at[part, :, lanes(z, shard_width)]
+        return send(
+            target if here else source.at[lines(far[turn], routed_units)],
+            target,
+            e_send.at[part, turn],
+            e_recv.at[part, turn],
+            (far[turn], me_e),
+        )
+
+    def rows_region(owner, half):
+        if half is None:
+            return rows_all.at[owner]
+        return rows_all.at[owner, pl.ds(half * (rows // 2), rows // 2)]
+
+    gather = PlaneGather(rows_region, a_send, a_recv, me_z, me_e, nbr)
+
+    def params_send(turn):
+        return send(
+            params_in.at[me_z], params_in.at[me_z], p_send.at[turn], p_recv.at[turn], (far[turn], me_e)
+        )
+
+    def docs_send(step):
+        return send(
+            docs_all.at[me_e], docs_all.at[me_e], d_send.at[step], d_recv.at[step], (me_z, nbr[step])
+        )
+
+    for turn in (1, 2, 3):
+        params_send(turn).start()
+    gather.begin()
+    for step in range(1, 8):
+        docs_send(step).start()
+    cot_own.begin()
+    gather.relay()
+    cot_chain.hop(0)
+    cot_step(0, "begin")
+    gather.relay_far()
+    cot_own.relay()
+    for turn in (1, 2, 3):
+        here = params_in.at[far[turn]]
+        send(here, here, p_send.at[turn], p_recv.at[turn], (far[turn], me_e)).wait_recv()
+    params_all[...] = jnp.concatenate([params_in[z] for z in range(4)], axis=1)
+    gather.finish()
+    attn_weights.hop(0)
+    cot_own.relay_far()
+    cot_chain.hop(1)
+    cot_step(0, "relay")
+    cot_step(1, "begin")
+
+    def norm_rows(value, gain):
+        scale = lax.rsqrt(jnp.mean(value * value, axis=-1, keepdims=True) + EPS)
+        return (value * scale * gain).astype(jnp.bfloat16)
+
+    params_full = params_all[...].astype(jnp.float32)
+    gain_one, gain_two = params_full[9:10], params_full[10:11]
+    bias = params_all[:, lanes(me_e, head_width)].astype(jnp.float32)[11:14]
+
+    for owner in range(8):
+
+        @pl.loop(0, rows, step=16)
+        def _(row, owner=owner):
+            span = pl.ds(pl.multiple_of(row, 16), 16)
+            normed[pl.ds(pl.multiple_of(owner * rows + row, 16), 16), :] = norm_rows(
+                rows_all[owner, span, :].astype(jnp.float32), gain_one
+            )
+
+    cot_step(0, "relay_far")
+    attn_weights.hop(1)
+    for part in range(3):
+        for turn in (1, 2, 3):
+            expert_copy(part, turn, False).start()
+    cot_chain.hop(2)
+
+    cot_step(1, "relay")
+    cot_step(2, "begin")
+    attn_weights.hop(2)
+
+    def out_send(step):
+        return send(
+            weights.at[lines(nbr[step], head_width), 3 * head_width : 4 * head_width],
+            w_out.at[:, lanes(me_e, head_width)],
+            o_send.at[step],
+            o_recv.at[step],
+            (me_z, nbr[step]),
+        )
+
+    for step in range(1, 8):
+        out_send(step).start()
+    w_out[:, lanes(me_e, head_width)] = weights[lines(me_e, head_width), 3 * head_width :]
+    weights_store = pltpu.make_async_copy(weights, weights_out, local_sem.at[0])
+    weights_store.start()
+
+    for part in range(3):
+        cols = slice(part * head_width, (part + 1) * head_width)
+        qkv_part[...] = (
+            jnp.dot(normed[...], weights[:, cols], preferred_element_type=jnp.float32)
+            + bias[part : part + 1]
+        )
+        if part == 2:
+            qkv[part] = qkv_part[...].astype(jnp.bfloat16)
+        else:
+
+            @pl.loop(0, sequences)
+            def _(index, part=part):
+                span = pl.ds(pl.multiple_of(index * rows, rows), rows)
+                for head in range(heads):
+                    at = slice(head * HEAD, (head + 1) * HEAD)
+                    value = qkv_part[span, at]
+                    qkv[part, span, at] = (
+                        value * tables[0] + swap_halves(value) * tables[1]
+                    ).astype(jnp.bfloat16)
+
+    order = lax.broadcasted_iota(jnp.int32, (rows, rows), 0) >= lax.broadcasted_iota(
+        jnp.int32, (rows, rows), 1
+    )
+
+    def sequence(index, carry):
+        span = pl.ds(pl.multiple_of(index * rows, rows), rows)
+        doc = jnp.broadcast_to(docs_all[index, 0:1, :], (rows, rows))
+        allowed = (doc == doc.T) & order
+        for head in range(heads):
+            at = slice(head * HEAD, (head + 1) * HEAD)
+            scores = (
+                lax.dot_general(
+                    qkv[0, span, at], qkv[1, span, at], NT, preferred_element_type=jnp.float32
+                )
+                * score_scale
+            )
+            scores = jnp.where(allowed, scores, NEGATIVE)
+            exp_scores = jnp.exp(scores - jnp.max(scores, axis=-1, keepdims=True))
+            weight = exp_scores / jnp.sum(exp_scores, axis=-1, keepdims=True)
+            probs[index * heads + head] = weight
+            mixed[span, at] = jnp.dot(
+                weight.astype(jnp.bfloat16), qkv[2, span, at], preferred_element_type=jnp.float32
+            ).astype(jnp.bfloat16)
+        return carry
+
+    cot_step(1, "relay_far")
+    cot_step(2, "relay")
+    for step in range(1, 8):
+        here = docs_all.at[nbr[step]]
+        send(here, here, d_send.at[step], d_recv.at[step], (me_z, nbr[step])).wait_recv()
+    lax.fori_loop(0, sequences // 2, sequence, 0)
+    cot_step(2, "relay_far")
+    lax.fori_loop(sequences // 2, sequences, sequence, 0)
+    gather.drain()
+
+    for step in range(1, 8):
+        here = w_out.at[:, lanes(nbr[step], head_width)]
+        send(here, here, o_send.at[step], o_recv.at[step], (me_z, nbr[step])).wait_recv()
+    for n in range(width // shard_width):
+        cols = slice(n * shard_width, (n + 1) * shard_width)
+        term = jnp.dot(mixed[...], w_out[:, cols], preferred_element_type=jnp.float32).astype(
+            jnp.bfloat16
+        )
+        for owner in range(8):
+            mine = lax.rem(owner + core + 1, 2)
+            rows_all[4 * mine + owner // 2, :, cols] = term[owner * rows : (owner + 1) * rows]
+    sums = PlaneScatter(
+        rows_all.at[pl.ds(0, 4)],
+        rows_all.at[pl.ds(4, 4)],
+        n_sib,
+        n_relayed,
+        n_crossed,
+        (n_send, n_recv),
+        (me_y, me_x),
+        me_z,
+        nbr,
+    )
+    sums.first()
+    out_store = pltpu.make_async_copy(w_out, w_out_out, local_sem.at[1])
+    out_store.start()
+    sums.second()
+
+    sums.third()
+
+    def keep(span, total):
+        hidden[span, :] = total + tokens[span, :].astype(jnp.float32)
+
+    sums.fourth(keep)
+
+    @pl.loop(0, rows, step=16)
+    def _(row):
+        span = pl.ds(pl.multiple_of(row, 16), 16)
+        normed_two[span, :] = norm_rows(hidden[span, :], gain_two)
+
+    logits = lax.dot_general(
+        params_all[...], normed_two[...], NT, preferred_element_type=jnp.float32
+    )
+    top = jnp.exp(logits[:8] - jnp.max(logits[:8], axis=0, keepdims=True))
+    top = top / jnp.sum(top, axis=0, keepdims=True)
+    line = lax.broadcasted_iota(jnp.int32, (8, rows), 0)
+    rest = jnp.where(line == 0, jax.nn.sigmoid(logits[8:]), 0.0)
+    router_probs[...] = jnp.concatenate([top, rest], axis=0)
+    x_own = pltpu.make_async_copy(normed_two, x_all.at[me_z, me_e], local_sem.at[2])
+    x_own.start()
+    gates_in[me_e, me_z] = jnp.concatenate([top * named[...], rest], axis=0)
+
+    def gates_far(turn, z):
+        here = gates_in.at[me_e, z]
+        return send(here, here, y_send.at[turn], y_recv.at[turn], (far[turn], me_e))
+
+    def gates_near(step, owner):
+        here = gates_in.at[owner]
+        return send(here, here, g_send.at[step], g_recv.at[step], (me_z, nbr[step]))
+
+    for turn in (1, 2, 3):
+        gates_far(turn, me_z).start()
+
+    def x_region(owner, half):
+        if half is None:
+            return x_all.at[me_z, owner]
+        return x_all.at[me_z, owner, pl.ds(half * (rows // 2), rows // 2)]
+
+    x_gather = PlaneGather(x_region, x_send, x_recv, me_z, me_e, nbr)
+    x_own.wait()
+    x_gather.begin()
+    for turn in (1, 2, 3):
+        gates_far(turn, far[turn]).wait_recv()
+    for step in range(1, 8):
+        gates_near(step, me_e).start()
+    x_gather.relay()
+    x_gather.relay_far()
+    for step in range(1, 8):
+        gates_near(step, nbr[step]).wait_recv()
+    gates_all[...] = gates_in[...]
+    x_gather.finish()
+
+    cot_own.finish()
+    for hop in range(3):
+        cot_step(hop, "finish")
+    for turn in (1, 2, 3):
+        for part in range(3):
+            expert_copy(part, turn, True).wait_recv()
+            expert_copy(part, turn, False).wait_send()
+        params_send(turn).wait_send()
+        gates_far(turn, me_z).wait_send()
+    for step in range(1, 8):
+        docs_send(step).wait_send()
+        gates_near(step, me_e).wait_send()
+        out_send(step).wait_send()
+    weights_store.wait()
+    out_store.wait()
+    attn_weights.drain()
+    cot_chain.drain()
+    sums.drain()
+    x_gather.drain()
+    cot_own.drain()
+    for hop in range(3):
+        cot_step(hop, "drain")
+
+
+def front_call(
+    tokens, docs, params, named, tables, cotangent, qkv_weight, out_weight, up_weight, down_weight
+):
+    rows, width = tokens.shape
+    shard_width = qkv_weight.shape[0]
+    head_width = width // 8
+    pairs = 8 * head_width // HEAD
+    routed_units = down_weight.shape[0] // 4
+    low, full = jnp.bfloat16, jnp.float32
+    shape = jax.ShapeDtypeStruct
+    any_space = pl.BlockSpec(memory_space=pl.ANY)
+    vmem = pl.BlockSpec(memory_space=pltpu.VMEM)
+    dma = pltpu.SemaphoreType.DMA
+    return pl.pallas_call(
+        front_kernel,
+        out_shape=(
+            shape((3, 8 * rows, head_width), low),
+            shape((pairs, rows, rows), full),
+            shape((8 * rows, head_width), low),
+            shape((8 * rows, width), low),
+            shape((rows, width), full),
+            shape((rows, width), low),
+            shape((8, 4, 16, rows), full),
+            shape((16, rows), full),
+            shape((16, width), low),
+            shape((width, 4 * head_width), low),
+            shape((head_width, width), low),
+            shape((8, 4, rows, width), low),
+            shape((3, routed_units, width), low),
+            shape((4, 8, rows, width), low),
+        ),
+        in_specs=[vmem] * 6 + [any_space] * 4,
+        out_specs=tuple([vmem] * 9 + [any_space] * 5),
+        scratch_shapes=[
+            pltpu.VMEM((8, rows, width), low),
+            pltpu.VMEM((width, 4 * head_width), low),
+            pltpu.VMEM((head_width, width), low),
+            pltpu.VMEM((4, 16, shard_width), low),
+            pltpu.VMEM((8, 8, rows), full),
+            pltpu.VMEM((8, 4, 16, rows), full),
+            pltpu.VMEM((8 * rows, head_width), full),
+            pltpu.VMEM((4, rows, width), low),
+            pltpu.VMEM((2, rows // 2, width), low),
+            pltpu.VMEM((2, rows, width), low),
+            dma((10,)),
+            dma((10,)),
+            dma((2, 3)),
+            dma((2, 3)),
+            dma((4,)),
+            dma((4,)),
+            dma((8,)),
+            dma((8,)),
+            dma((8,)),
+            dma((8,)),
+            dma((7,)),
+            dma((7,)),
+            dma((7, 10)),
+            dma((7, 10)),
+            dma((2, 3)),
+            dma((2, 3)),
+            dma((3, 4)),
+            dma((3, 4)),
+            dma((10,)),
+            dma((10,)),
+            dma((4,)),
+            dma((4,)),
+            dma((8,)),
+            dma((8,)),
+            dma((6,)),
+        ],
+        compiler_params=pltpu.CompilerParams(
+            collective_id=2, has_side_effects=True, vmem_limit_bytes=60 * 2**20
+        ),
+        cost_estimate=pl.CostEstimate(
+            flops=8 * 8 * rows * width * head_width, bytes_accessed=80 * 2**20, transcendentals=0
+        ),
+    )(
+        tokens, docs, params, named, tables, cotangent, qkv_weight, out_weight, up_weight, down_weight
+    )
+
+
+def widen_kernel(attn_all, shared_all, expert_all, qkv, out, shared, up, down):
+    for part in range(3):
+        width = attn_all.shape[2]
+        qkv[:, part * width : (part + 1) * width] = attn_all[part].astype(jnp.float32)
+        shared[part] = shared_all[part].astype(jnp.float32)
+    out[...] = attn_all[3].astype(jnp.float32)
+    for part in range(2):
+        up[:, part, :] = expert_all[part].astype(jnp.float32)
+    down[...] = expert_all[2].astype(jnp.float32)
+
+
+def widen_call(attn_all, shared_all, expert_all):
+    steps = 8
+    _, depth, width = attn_all.shape
+    units, routed, cols = shared_all.shape[1], expert_all.shape[1], expert_all.shape[2]
+    full = jnp.float32
+    shape = jax.ShapeDtypeStruct
+    return pl.pallas_call(
+        widen_kernel,
+        grid=(steps,),
+        out_shape=(
+            shape((depth, 3 * width), full),
+            shape((depth, width), full),
+            shape(shared_all.shape, full),
+            shape((routed, 2, cols), full),
+            shape((routed, cols), full),
+        ),
+        in_specs=[
+            pl.BlockSpec((4, depth // steps, width), lambda i: (0, i, 0)),
+            pl.BlockSpec((3, units // steps, width), lambda i: (0, i, 0)),
+            pl.BlockSpec((3, routed // steps, cols), lambda i: (0, i, 0)),
+        ],
+        out_specs=(
+            pl.BlockSpec((depth // steps, 3 * width), lambda i: (i, 0)),
+            pl.BlockSpec((depth // steps, width), lambda i: (i, 0)),
+            pl.BlockSpec((3, units // steps, width), lambda i: (0, i, 0)),
+            pl.BlockSpec((routed // steps, 2, cols), lambda i: (i, 0, 0)),
+            pl.BlockSpec((routed // steps, cols), lambda i: (i, 0)),
+        ),
+        compiler_params=pltpu.CompilerParams(vmem_limit_bytes=60 * 2**20),
+        cost_estimate=pl.CostEstimate(flops=0, bytes_accessed=96 * 2**20, transcendentals=0),
+    )(attn_all, shared_all, expert_all)
 
 
 def silu_parts(gate):
@@ -351,9 +2270,131 @@
     )
 
 
+def fast_shards(
+    tokens,
+    attn_gain,
+    qkv_weight,
+    qkv_bias,
+    out_weight,
+    ffn_gain,
+    router_weight,
+    shared_gate_weight,
+    shared_weight,
+    expert_up,
+    expert_down,
+    routes,
+    segment_ids,
+    cotangent,
+):
+    num_dp = lax.axis_size("dp")
+    num_expert = lax.axis_size("expert")
+    seq_len, model_width = tokens.shape
+    up_weight = expert_up[0].transpose(1, 0, 2)
+    low, full = jnp.bfloat16, jnp.float32
+
+    params = jnp.concatenate(
+        [
+            router_weight.T,
+            shared_gate_weight[None],
+            attn_gain[None],
+            ffn_gain[None],
+            qkv_bias,
+            jnp.zeros((16 - 6 - num_expert, attn_gain.shape[0]), low),
+        ],
+        axis=0,
+    )
+    named = jnp.any(routes[:, :, None] == jnp.arange(num_expert)[None, None, :], axis=1)
+    named = named.T.astype(full)
+    cosine_table, sine_table = rope_tables(seq_len, HEAD)
+    tables = jnp.stack(
+        [
+            jnp.concatenate([cosine_table, cosine_table], axis=1),
+            jnp.concatenate([-sine_table, sine_table], axis=1),
+        ]
+    )
+    (
+        qkv,
+        probs,
+        mixed,
+        normed_one,
+        hidden_state,
+        normed_two,
+        gates_all,
+        router_probs,
+        params,
+        attn_weights,
+        w_out,
+        all_cot,
+        mlp_weight,
+        x_all,
+    ) = front_call(
+        tokens,
+        jnp.broadcast_to(segment_ids.astype(full), (8, seq_len)),
+        params,
+        named,
+        tables,
+        cotangent,
+        qkv_weight,
+        out_weight,
+        up_weight,
+        expert_down[0],
+    )
+
+    _, out_part, d_rows, d_gates, d_routed, shared_grad, expert_grad = mlp_call(
+        x_all,
+        gates_all,
+        all_cot,
+        mlp_weight,
+        up_weight,
+        expert_down[0],
+        shared_weight.transpose(1, 0, 2),
+    )
+
+    output, tokens_grad, small_grad, attn_grad, shared_grad, expert_grad = tail_call(
+        mixed,
+        qkv,
+        probs,
+        normed_one,
+        attn_weights,
+        w_out,
+        tables,
+        tokens,
+        params,
+        d_rows,
+        d_gates,
+        named,
+        router_probs,
+        normed_two,
+        hidden_state,
+        cotangent,
+        out_part.reshape(num_expert // 2, 2, num_dp, seq_len, model_width),
+        d_routed,
+        shared_grad,
+        expert_grad,
+    )
+    qkv_grad, out_grad, shared_grad, up_grad, down_grad = widen_call(
+        attn_grad, shared_grad, expert_grad
+    )
+    return (
+        output,
+        tokens_grad,
+        small_grad[num_expert + 1],
+        qkv_grad,
+        small_grad[num_expert + 3 : num_expert + 6],
+        out_grad,
+        small_grad[num_expert + 2],
+        small_grad[:num_expert].T,
+        small_grad[num_expert],
+        shared_grad.transpose(1, 0, 2),
+        up_grad[None],
+        down_grad[None],
+    )
+
+
 def solution(mesh):
+    cube = mesh.shape["expert"] == 8 and mesh.shape["dp"] == 4
     return jax.shard_map(
-        shards,
+        fast_shards if cube else shards,
         mesh=mesh,
         in_specs=(
             P(("dp", "expert"), None),

time: 1480 us -> 685 us (0.46); the launches traced: 1460 us -> 684 us
  Pallas kernels: 0 us -> 666 us
  waiting for transfers between devices: 606 us -> 0 us
  blocking collectives: 369 us -> 0 us
  matrix products: 195 us -> 0 us
  local copies, waits for them, and re-layouts: 190 us -> 14.9 us
  other arithmetic: 73.8 us -> 3.03 us
    pallas_call x0 -> x4, Pallas kernels: none -> 666 us  [the longest x1 245 us: tail_call(): pl.pallas_call(tail_kernel, out_shape=(shape((rows, width), low), shape((...]
    reduce_scatter x10 -> x0, waiting for transfers between devices: 392 us -> none  [the longest x3 146 us: scatter_all(): rows = lax.psum_scatter(rows, 'expert', scatter_dimension=0, tiled=True)]
    all_gather x9 -> x0, waiting for transfers between devices: 202 us -> none  [the longest x2 91.6 us: gather_all(): rows = lax.all_gather(rows, 'dp', axis=0, tiled=True)]
    dot_general x21 -> x0, matrix products: 192 us -> none  [the longest x1 27.7 us: shards(): jnp.einsum('gtf,fgd->td', d_gate_up, mlp_weight[:, :2], preferred_element...]
    all_to_all x1 -> x0, blocking collectives: 181 us -> none  [shards(): lax.all_to_all(mlp_grad[:routed_units], 'dp', split_axis=2, concat_axis=0...]
    all_gather x4 -> x0, blocking collectives: 166 us -> none  [the longest x1 130 us: gather_all(): rows = lax.all_gather(rows, 'dp', axis=0, tiled=True)]
    unnamed x113 -> x7, local copies, waits for them, and re-layouts: 74.1 us -> 5.62 us
    convert_element_type x6 -> x1, other arithmetic: 34.4 us -> 0.6 us  [fast_shards(): named = named.T.astype(full)]
  transfers between devices with their start and end apart: 22 -> 0, of which waited for: 14 -> 0; matrix products, arithmetic and copies ran while one was open for 21% -> 0% of each run, Pallas kernels for 0% -> 0%
where the time goes in v3:
time: 685 us; the launch traced here: 684 us
  Pallas kernels  666 us (97%)
  local copies, waits for them, and re-layouts  14.9 us (2%)
    pallas_call x1, Pallas kernels, tail_call(): pl.pallas_call(tail_kernel, out_shape=(shape((rows, width), low), shape((...  245 us
    pallas_call x1, Pallas kernels, front_call(): pl.pallas_call(front_kernel, out_shape=(shape((3, 8 * rows, head_width),...  210 us
    pallas_call x1, Pallas kernels, mlp_call(): pl.pallas_call(functools.partial(mlp_kernel, routed_units), out_shape=(sh...  182 us
    pallas_call x1, Pallas kernels, widen_call(): pl.pallas_call(widen_kernel, grid=(steps,), out_shape=(shape((depth, 3 *...  29.3 us

profile of v3, /device:TPU:1, one launch (start us, length us, event | category | flops | bytes accessed | tf_op | source)
XLA Modules:
  0.0 684.3 jit_solution(7217087779798050704)
XLA Ops:
  0.6 0.7 convert_bitcast_fusion.1
  1.3 0.7 fusion.1
  2.0 0.7 broadcast_in_dim.32
  2.7 0.7 broadcast_in_dim.33
  3.4 0.7 broadcast_in_dim.31
  4.1 0.6 convert_bitcast_fusion.named
  4.6 0.6 broadcast_in_dim.30.docs
  5.2 2.6 concatenate.9.params
  7.9 0.3 multiply_cosine_fusion
  8.2 0.1 maximum_bitcast_fusion
  8.3 0.7 pad_maximum_fusion.tables
  8.9 3.9 copy.33
  12.8 209.8 %shard_map.229 = (bf16[3,1024,256]{2,1,0:T(8,128)(2,1)}, f32[16,128,128]{2,1,0:T(8,128)}, bf16[1024,256]{1,0:T(8,128)(2,1)}, bf16[1024,2048]{1,0:T(8,128)(2,1)},...) custom-call(bf16[128,2048]{1,0:T(8,128)(2,1)} %tokens.3, ...), custom_call_target="tpu_custom_call" | custom-call | flops 4294967296 | bytes 83886080 | tf_op jit(solution)/shard_map/pallas_call | solution.py:1874
  222.6 181.7 %shard_map.230 = (bf16[4,8,128,2048]{3,2,1,0:T(8,128)(2,1)}, bf16[8,4,128,2048]{3,2,1,0:T(8,128)(2,1)}, f32[128,2048]{1,0:T(8,128)}, f32[16,128]{1,0:T(8,128)}, ...) custom-call(bf16[4,8,128,2048]{3,2,1,0:T(8,128)(2,1)} %get-tuple-ele, ...), custom_call_target="tpu_custom_call", output_to_operand_aliasing={{0}: (0, {})} | custom-call | flops 79725330432 | bytes 83886080 | tf_op jit(solution)/shard_map/pallas_call | solution.py:831
  404.4 244.7 %shard_map.231 = (bf16[128,2048]{1,0:T(8,128)(2,1)}, f32[128,2048]{1,0:T(8,128)}, f32[16,512]{1,0:T(8,128)}, bf16[4,512,2048]{2,1,0:T(8,128)(2,1)}, bf16[3,1408,...) custom-call(bf16[1024,256]{1,0:T(8,128)(2,1)} %get-tuple-element.43.mixed, ...), custom_call_target="tpu_custom_call", output_to_operand_aliasing={{4}: (18, {}), {5}: (19, {})} | custom-call | flops 12884901888 | bytes 83886080 | tf_op jit(solution)/shard_map/pallas_call | solution.py:1399
  649.1 1.4 fusion.2
  650.5 1.3 slice.16
  651.8 1.3 slice_bitcast_fusion
  653.2 0.0 copy-start.1
  653.2 0.0 copy-start
  653.2 29.3 %shard_map.232 = (f32[512,6144]{1,0:T(8,128)}, f32[512,2048]{1,0:T(8,128)}, f32[3,1408,2048]{2,1,0:T(8,128)}, f32[1408,2,512]{2,1,0:T(2,128)}, f32[1408,512]{1,0:T(8,128)}) custom-call(bf16[4,512,2048]{2,1,0:T(8,128)(2,1)} %get-tuple-element.66.attn_all, bf16[3,1408,2048]{2,1,0:T(8,128)(2,1)} %get-tuple-element.67.shared_all, ...), custom_call_target="tpu_custom_call" | custom-call | bytes 100663296 | tf_op jit(solution)/shard_map/pallas_call | solution.py:1959
  682.5 0.0 copy-done.1
  682.5 0.8 copy.39
  683.3 0.0 copy-done
  683.3 1.0 copy.40
  (3 shorter events, 0.0 us)
Async XLA Ops:
  653.2 29.3 %copy-start.1 = (bf16[128,2048]{1,0:T(8,128)(2,1)S(1)}, bf16[128,2048]{1,0:T(8,128)(2,1)}, u32[]{:S(2)}) copy-start(bf16[128,2048]{1,0:T(8,128)(2,1)} %get-tuple-element.94) | copy-start | bytes 1572868
  653.2 30.1 %copy-start = (f32[128,2048]{1,0:T(8,128)S(1)}, f32[128,2048]{1,0:T(8,128)}, u32[]{:S(2)}) copy-start(f32[128,2048]{1,0:T(8,128)} %get-tuple-element.95) | copy-start | bytes 3145732

commit v4 on v3

--- a/solution.py
+++ b/solution.py
@@ -3,6 +3,7 @@
 
 import jax
 import jax.numpy as jnp
+import numpy as np
 from jax import lax
 from jax.experimental import pallas as pl
 from jax.experimental.pallas import tpu as pltpu
@@ -370,6 +371,14 @@
         for hop in range(3):
             for way, place, owner in self.steps(hop):
                 pl.when(place <= hop)(self.copy(way, hop, self.part(owner), owner).wait_send)
+
+
+def named_of(routes):
+    expert = lax.broadcasted_iota(jnp.int32, (8, routes.shape[1]), 0)
+    hits = jnp.zeros(expert.shape, jnp.float32)
+    for way in range(routes.shape[0]):
+        hits = hits + jnp.where(routes[way : way + 1, :] == expert, 1.0, 0.0)
+    return hits
 
 
 def mlp_kernel(
@@ -904,7 +913,7 @@
     params,
     d_rows,
     d_gates,
-    named,
+    routes,
     router_probs,
     normed_two,
     hidden,
@@ -1063,7 +1072,7 @@
     forward[2].first()
 
     top, gate = router_probs[:8], router_probs[8:9]
-    d_top = d_gates[:8] * named[...]
+    d_top = d_gates[:8] * named_of(routes)
     d_logits = top * (d_top - jnp.sum(top * d_top, axis=0, keepdims=True))
     line = lax.broadcasted_iota(jnp.int32, (8, rows), 0)
     d_rest = jnp.where(line == 0, d_gates[8:9] * gate * (1.0 - gate), 0.0)
@@ -1261,31 +1270,8 @@
         me_z,
         nbr,
     )
-    back.first()
-    bias_terms = jnp.sum(d_qkv[...].astype(jnp.float32), axis=0, keepdims=True)
-    for part in range(3):
-        small[11 + part : 12 + part, lanes(me_e, head_width)] = bias_terms[
-            :, part * head_width : (part + 1) * head_width
-        ]
-    forward_last(2)
-    forward[1].drain()
-    forward_load(3).start()
-    back.second()
-    back.third()
-    out_chain.hop(2)
-    shared.relay()
-    chain.hop(1)
-    out_chain_last()
-    out_own.start()
-    out_own.wait()
-    out_projection.begin()
-    forward_load(3).wait()
-    forward[3].second()
-
     def keep(span, total):
         d_normed[span, :] = total
-
-    back.fourth(keep)
 
     def norm_step(index, gain_sum):
         span = pl.ds(pl.multiple_of(index * 16, 16), 16)
@@ -1294,8 +1280,6 @@
         )
         tokens_grad[span, :] = tokens_grad[span, :] + grad
         return gain_sum + term
-
-    small[9:10, :] = lax.fori_loop(0, rows // 16, norm_step, jnp.zeros((1, width), jnp.float32))
 
     def small_send(turn):
         return send(
@@ -1306,22 +1290,6 @@
             (far[turn], me_e),
         )
 
-    for turn in (1, 2, 3):
-        small_send(turn).start()
-    forward[2].drain()
-    forward_load(0).start()
-    forward[3].third()
-    forward_load(0).wait()
-    forward[0].second()
-    out_projection.relay()
-    chain.hop(2)
-    out_projection.relay_far()
-    for turn in (1, 2, 3):
-        small_send(turn).wait_recv()
-    small_plane[me_e] = (
-        small[:, lanes(me_z, shard_width)] + small_far[1] + small_far[2] + small_far[3]
-    )
-
     def plane_send(step):
         return send(
             small_plane.at[me_e],
@@ -1331,10 +1299,52 @@
             (me_z, nbr[step]),
         )
 
+    back.first()
+    bias_terms = jnp.sum(d_qkv[...].astype(jnp.float32), axis=0, keepdims=True)
+    for part in range(3):
+        small[11 + part : 12 + part, lanes(me_e, head_width)] = bias_terms[
+            :, part * head_width : (part + 1) * head_width
+        ]
+    back.second()
+    out_chain.hop(2)
+    chain.hop(1)
+    out_chain_last()
+    out_own.start()
+    out_own.wait()
+    out_projection.begin()
+    back.third()
+    out_projection.relay()
+    chain.hop(2)
+    out_projection.relay_far()
+    shared.relay()
+    back.fourth(keep)
+    small[9:10, :] = lax.fori_loop(0, rows // 16, norm_step, jnp.zeros((1, width), jnp.float32))
+    for turn in (1, 2, 3):
+        small_send(turn).start()
+    forward_last(2)
+    forward[1].drain()
+    forward_load(3).start()
+    forward_load(3).wait()
+    forward[3].second()
+    forward[2].drain()
+    forward_load(0).start()
+    chain_last()
+    qkv_own.start()
+    qkv_own.wait()
+    projections.begin()
+    forward[3].third()
+    forward_load(0).wait()
+    forward[0].second()
+    for turn in (1, 2, 3):
+        small_send(turn).wait_recv()
+    small_plane[me_e] = (
+        small[:, lanes(me_z, shard_width)] + small_far[1] + small_far[2] + small_far[3]
+    )
     for step in range(1, 8):
         plane_send(step).start()
+    shared.relay_far()
+    projections.relay()
     forward_last(3)
-    shared.relay_far()
     forward[0].third()
     for step in range(1, 8):
         here = small_plane.at[nbr[step]]
@@ -1343,13 +1353,7 @@
     for index in range(1, 8):
         total = total + small_plane[index]
     small_out[...] = total
-
-    chain_last()
-    qkv_own.start()
-    qkv_own.wait()
-    projections.begin()
     forward_last(0)
-    projections.relay()
     for turn in (1, 2, 3):
         far_send(turn).wait_recv()
 
@@ -1385,7 +1389,7 @@
 
 
 def tail_call(
-    mixed, qkv, probs, normed, w_qkv, w_out, tables, tokens, params, d_rows, d_gates, named, router_probs,
+    mixed, qkv, probs, normed, w_qkv, w_out, tables, tokens, params, d_rows, d_gates, routes, router_probs,
     normed_two, hidden, cotangent, out_part, d_routed, shared_all, expert_all,
 ):
     rows, width = tokens.shape
@@ -1467,7 +1471,7 @@
             flops=24 * 8 * rows * width * head_width, bytes_accessed=80 * 2**20, transcendentals=0
         ),
     )(
-        mixed, qkv, probs, normed, w_qkv, w_out, tables, tokens, params, d_rows, d_gates, named, router_probs,
+        mixed, qkv, probs, normed, w_qkv, w_out, tables, tokens, params, d_rows, d_gates, routes, router_probs,
         normed_two, hidden, cotangent, out_part, d_routed, shared_all, expert_all,
     )
 
@@ -1475,8 +1479,12 @@
 def front_kernel(
     tokens,
     docs,
-    params,
-    named,
+    routes,
+    router,
+    gate_vector,
+    gain_in,
+    gain_out,
+    bias_in,
     tables,
     cotangent,
     qkv_weight,
@@ -1576,8 +1584,11 @@
     own.append(pltpu.make_async_copy(cotangent, cot_all.at[me_e, me_z], local_sem.at[5]))
     for copy in own:
         copy.start()
-    params_in[me_z] = params[...]
-    docs_all[me_e] = docs[...]
+    shards = [router[...]] + [ref[...].reshape(1, shard_width) for ref in (gate_vector, gain_in, gain_out)]
+    shards = [part.astype(jnp.float32) for part in shards + [bias_in[...]]]
+    shards.append(jnp.zeros((2, shard_width), jnp.float32))
+    params_in[me_z] = jnp.concatenate(shards, axis=0).astype(jnp.bfloat16)
+    docs_all[me_e] = jnp.broadcast_to(docs[...].astype(jnp.float32), docs_all.shape[1:])
     greet([(far[turn], me_e) for turn in (1, 2, 3)] + [(me_z, nbr[k]) for k in range(1, 8)])
     for copy in own:
         copy.wait()
@@ -1615,6 +1626,14 @@
             e_recv.at[part, turn],
             (far[turn], me_e),
         )
+
+    ends = (me_z == 0) | (me_z == 3)
+
+    def expert_start(turn, from_ends):
+        @pl.when(ends if from_ends else jnp.logical_not(ends))
+        def _():
+            for part in range(3):
+                expert_copy(part, turn, False).start()
 
     def rows_region(owner, half):
         if half is None:
@@ -1674,14 +1693,17 @@
 
     cot_step(0, "relay_far")
     attn_weights.hop(1)
-    for part in range(3):
-        for turn in (1, 2, 3):
-            expert_copy(part, turn, False).start()
+    expert_start(1, True)
+    expert_start(2, True)
+    expert_start(3, False)
     cot_chain.hop(2)
 
     cot_step(1, "relay")
     cot_step(2, "begin")
     attn_weights.hop(2)
+    expert_start(1, False)
+    expert_start(2, False)
+    expert_start(3, True)
 
     def out_send(step):
         return send(
@@ -1802,7 +1824,7 @@
     router_probs[...] = jnp.concatenate([top, rest], axis=0)
     x_own = pltpu.make_async_copy(normed_two, x_all.at[me_z, me_e], local_sem.at[2])
     x_own.start()
-    gates_in[me_e, me_z] = jnp.concatenate([top * named[...], rest], axis=0)
+    gates_in[me_e, me_z] = jnp.concatenate([top * named_of(routes), rest], axis=0)
 
     def gates_far(turn, z):
         here = gates_in.at[me_e, z]
@@ -1859,7 +1881,8 @@
 
 
 def front_call(
-    tokens, docs, params, named, tables, cotangent, qkv_weight, out_weight, up_weight, down_weight
+    tokens, docs, routes, router, gate_vector, gain_in, gain_out, bias_in, tables, cotangent, qkv_weight,
+    out_weight, up_weight, down_weight,
 ):
     rows, width = tokens.shape
     shard_width = qkv_weight.shape[0]
@@ -1889,7 +1912,7 @@
             shape((3, routed_units, width), low),
             shape((4, 8, rows, width), low),
         ),
-        in_specs=[vmem] * 6 + [any_space] * 4,
+        in_specs=[vmem] * 10 + [any_space] * 4,
         out_specs=tuple([vmem] * 9 + [any_space] * 5),
         scratch_shapes=[
             pltpu.VMEM((8, rows, width), low),
@@ -1935,7 +1958,8 @@
             flops=8 * 8 * rows * width * head_width, bytes_accessed=80 * 2**20, transcendentals=0
         ),
     )(
-        tokens, docs, params, named, tables, cotangent, qkv_weight, out_weight, up_weight, down_weight
+        tokens, docs, routes, router, gate_vector, gain_in, gain_out, bias_in, tables, cotangent, qkv_weight,
+        out_weight, up_weight, down_weight,
     )
 
 
@@ -2292,25 +2316,11 @@
     up_weight = expert_up[0].transpose(1, 0, 2)
     low, full = jnp.bfloat16, jnp.float32
 
-    params = jnp.concatenate(
-        [
-            router_weight.T,
-            shared_gate_weight[None],
-            attn_gain[None],
-            ffn_gain[None],
-            qkv_bias,
-            jnp.zeros((16 - 6 - num_expert, attn_gain.shape[0]), low),
-        ],
-        axis=0,
-    )
-    named = jnp.any(routes[:, :, None] == jnp.arange(num_expert)[None, None, :], axis=1)
-    named = named.T.astype(full)
-    cosine_table, sine_table = rope_tables(seq_len, HEAD)
-    tables = jnp.stack(
-        [
-            jnp.concatenate([cosine_table, cosine_table], axis=1),
-            jnp.concatenate([-sine_table, sine_table], axis=1),
-        ]
+    positions = np.arange(seq_len, dtype=np.float32)[:, None]
+    angles = positions * np.exp(np.arange(HEAD // 2) * (-2.0 * math.log(THETA) / HEAD)).astype(np.float32)
+    sines = np.sin(angles)
+    tables = jnp.asarray(
+        np.stack([np.tile(np.cos(angles), 2), np.concatenate([-sines, sines], axis=1)]), full
     )
     (
         qkv,
@@ -2329,9 +2339,13 @@
         x_all,
     ) = front_call(
         tokens,
-        jnp.broadcast_to(segment_ids.astype(full), (8, seq_len)),
-        params,
-        named,
+        segment_ids,
+        routes.T,
+        router_weight.T,
+        shared_gate_weight,
+        attn_gain,
+        ffn_gain,
+        qkv_bias,
         tables,
         cotangent,
         qkv_weight,
@@ -2362,7 +2376,7 @@
         params,
         d_rows,
         d_gates,
-        named,
+        routes.T,
         router_probs,
         normed_two,
         hidden_state,

time: 685 us -> 663 us (0.968)
  Pallas kernels: 666 us -> 653 us
    pallas_call x1, Pallas kernels: 210 us -> 198 us  [front_call(): pl.pallas_call(front_kernel, out_shape=(shape((3, 8 * rows, head_width),...]
where the time goes in v4:
time: 663 us
  Pallas kernels  653 us (98%)
  local copies, waits for them, and re-layouts  9.68 us (1%)
    pallas_call x1, Pallas kernels, tail_call(): pl.pallas_call(tail_kernel, out_shape=(shape((rows, width), low), shape((...  241 us
    pallas_call x1, Pallas kernels, front_call(): pl.pallas_call(front_kernel, out_shape=(shape((3, 8 * rows, head_width),...  198 us
    pallas_call x1, Pallas kernels, mlp_call(): pl.pallas_call(functools.partial(mlp_kernel, routed_units), out_shape=(sh...  184 us
    pallas_call x1, Pallas kernels, widen_call(): pl.pallas_call(widen_kernel, grid=(steps,), out_shape=(shape((depth, 3 *...  29.3 us

profile of v4, /device:TPU:1, one launch (start us, length us, event | category | flops | bytes accessed | tf_op | source)
XLA Modules:
  0.0 663.0 jit_solution(10665744832622033317)
XLA Ops:
  0.6 3.9 copy.32
  4.5 198.4 %shard_map.238 = (bf16[3,1024,256]{2,1,0:T(8,128)(2,1)}, f32[16,128,128]{2,1,0:T(8,128)}, bf16[1024,256]{1,0:T(8,128)(2,1)}, bf16[1024,2048]{1,0:T(8,128)(2,1)},...) custom-call(bf16[128,2048]{1,0:T(8,128)(2,1)} %tokens.3, ...), custom_call_target="tpu_custom_call" | custom-call | flops 4294967296 | bytes 83886080 | tf_op jit(solution)/shard_map/pallas_call | solution.py:1897
  202.9 183.6 %shard_map.239 = (bf16[4,8,128,2048]{3,2,1,0:T(8,128)(2,1)}, bf16[8,4,128,2048]{3,2,1,0:T(8,128)(2,1)}, f32[128,2048]{1,0:T(8,128)}, f32[16,128]{1,0:T(8,128)}, ...) custom-call(bf16[4,8,128,2048]{3,2,1,0:T(8,128)(2,1)} %get-tuple-ele, ...), custom_call_target="tpu_custom_call", output_to_operand_aliasing={{0}: (0, {})} | custom-call | flops 79725330432 | bytes 83886080 | tf_op jit(solution)/shard_map/pallas_call | solution.py:840
  386.5 241.4 %shard_map.240 = (bf16[128,2048]{1,0:T(8,128)(2,1)}, f32[128,2048]{1,0:T(8,128)}, f32[16,512]{1,0:T(8,128)}, bf16[4,512,2048]{2,1,0:T(8,128)(2,1)}, bf16[3,1408,...) custom-call(bf16[1024,256]{1,0:T(8,128)(2,1)} %get-tuple-element.43.mixed, ...), custom_call_target="tpu_custom_call", output_to_operand_aliasing={{4}: (18, {}), {5}: (19, {})} | custom-call | flops 12884901888 | bytes 83886080 | tf_op jit(solution)/shard_map/pallas_call | solution.py:1403
  627.9 1.4 fusion
  629.3 1.3 slice.16
  630.6 1.3 slice_bitcast_fusion
  631.9 0.0 copy-start.1
  631.9 0.0 copy-start
  631.9 29.3 %shard_map.241 = (f32[512,6144]{1,0:T(8,128)}, f32[512,2048]{1,0:T(8,128)}, f32[3,1408,2048]{2,1,0:T(8,128)}, f32[1408,2,512]{2,1,0:T(2,128)}, f32[1408,512]{1,0:T(8,128)}) custom-call(bf16[4,512,2048]{2,1,0:T(8,128)(2,1)} %get-tuple-element.66.attn_all, bf16[3,1408,2048]{2,1,0:T(8,128)(2,1)} %get-tuple-element.67.shared_all, ...), custom_call_target="tpu_custom_call" | custom-call | bytes 100663296 | tf_op jit(solution)/shard_map/pallas_call | solution.py:1983
  661.3 0.0 copy-done.1
  661.3 0.8 copy.38
  662.1 0.0 copy-done
  662.1 1.0 copy.39
Async XLA Ops:
  631.9 29.3 %copy-start.1 = (bf16[128,2048]{1,0:T(8,128)(2,1)S(1)}, bf16[128,2048]{1,0:T(8,128)(2,1)}, u32[]{:S(2)}) copy-start(bf16[128,2048]{1,0:T(8,128)(2,1)} %get-tuple-element.89) | copy-start | bytes 1572868
  631.9 30.1 %copy-start = (f32[128,2048]{1,0:T(8,128)S(1)}, f32[128,2048]{1,0:T(8,128)}, u32[]{:S(2)}) copy-start(f32[128,2048]{1,0:T(8,128)} %get-tuple-element.90) | copy-start | bytes 3145732

commit v5 on v4

--- a/solution.py
+++ b/solution.py
@@ -1963,7 +1963,9 @@
     )
 
 
-def widen_kernel(attn_all, shared_all, expert_all, qkv, out, shared, up, down):
+def widen_kernel(
+    attn_all, shared_all, expert_all, small, qkv, out, shared, up, down, router, gate, gain_in, gain_out, bias
+):
     for part in range(3):
         width = attn_all.shape[2]
         qkv[:, part * width : (part + 1) * width] = attn_all[part].astype(jnp.float32)
@@ -1973,8 +1975,15 @@
         up[:, part, :] = expert_all[part].astype(jnp.float32)
     down[...] = expert_all[2].astype(jnp.float32)
 
-
-def widen_call(attn_all, shared_all, expert_all):
+    @pl.when(pl.program_id(0) == 0)
+    def _():
+        router[...] = small[:8, :]
+        for row, target in ((8, gate), (9, gain_in), (10, gain_out)):
+            target[...] = small[row, :]
+        bias[...] = small[11:14, :]
+
+
+def widen_call(attn_all, shared_all, expert_all, small):
     steps = 8
     _, depth, width = attn_all.shape
     units, routed, cols = shared_all.shape[1], expert_all.shape[1], expert_all.shape[2]
@@ -1989,11 +1998,17 @@
             shape(shared_all.shape, full),
             shape((routed, 2, cols), full),
             shape((routed, cols), full),
+            shape((8, depth), full),
+            shape((depth,), full),
+            shape((depth,), full),
+            shape((depth,), full),
+            shape((3, depth), full),
         ),
         in_specs=[
             pl.BlockSpec((4, depth // steps, width), lambda i: (0, i, 0)),
             pl.BlockSpec((3, units // steps, width), lambda i: (0, i, 0)),
             pl.BlockSpec((3, routed // steps, cols), lambda i: (0, i, 0)),
+            pl.BlockSpec((16, depth), lambda i: (0, 0)),
         ],
         out_specs=(
             pl.BlockSpec((depth // steps, 3 * width), lambda i: (i, 0)),
@@ -2001,10 +2016,15 @@
             pl.BlockSpec((3, units // steps, width), lambda i: (0, i, 0)),
             pl.BlockSpec((routed // steps, 2, cols), lambda i: (i, 0, 0)),
             pl.BlockSpec((routed // steps, cols), lambda i: (i, 0)),
+            pl.BlockSpec((8, depth), lambda i: (0, 0)),
+            pl.BlockSpec((depth,), lambda i: (0,)),
+            pl.BlockSpec((depth,), lambda i: (0,)),
+            pl.BlockSpec((depth,), lambda i: (0,)),
+            pl.BlockSpec((3, depth), lambda i: (0, 0)),
         ),
         compiler_params=pltpu.CompilerParams(vmem_limit_bytes=60 * 2**20),
         cost_estimate=pl.CostEstimate(flops=0, bytes_accessed=96 * 2**20, transcendentals=0),
-    )(attn_all, shared_all, expert_all)
+    )(attn_all, shared_all, expert_all, small)
 
 
 def silu_parts(gate):
@@ -2386,19 +2406,28 @@
         shared_grad,
         expert_grad,
     )
-    qkv_grad, out_grad, shared_grad, up_grad, down_grad = widen_call(
-        attn_grad, shared_grad, expert_grad
-    )
+    (
+        qkv_grad,
+        out_grad,
+        shared_grad,
+        up_grad,
+        down_grad,
+        router_grad,
+        gate_grad,
+        attn_gain_grad,
+        ffn_gain_grad,
+        bias_grad,
+    ) = widen_call(attn_grad, shared_grad, expert_grad, small_grad)
     return (
         output,
         tokens_grad,
-        small_grad[num_expert + 1],
+        attn_gain_grad,
         qkv_grad,
-        small_grad[num_expert + 3 : num_expert + 6],
+        bias_grad,
         out_grad,
-        small_grad[num_expert + 2],
-        small_grad[:num_expert].T,
-        small_grad[num_expert],
+        ffn_gain_grad,
+        router_grad.T,
+        gate_grad,
         shared_grad.transpose(1, 0, 2),
         up_grad[None],
         down_grad[None],

time: 663 us -> 659 us (level)
  no operation moved by 1% of the time
where the time goes in v5:
time: 659 us
  Pallas kernels  653 us (99%)
    pallas_call x1, Pallas kernels, tail_call(): pl.pallas_call(tail_kernel, out_shape=(shape((rows, width), low), shape((...  241 us
    pallas_call x1, Pallas kernels, front_call(): pl.pallas_call(front_kernel, out_shape=(shape((3, 8 * rows, head_width),...  198 us
    pallas_call x1, Pallas kernels, mlp_call(): pl.pallas_call(functools.partial(mlp_kernel, routed_units), out_shape=(sh...  184 us
    pallas_call x1, Pallas kernels, widen_call(): pl.pallas_call(widen_kernel, grid=(steps,), out_shape=(shape((depth, 3 *...  29.4 us

profile of v5, /device:TPU:1, one launch (start us, length us, event | category | flops | bytes accessed | tf_op | source)
XLA Modules:
  0.0 659.1 jit_solution(9063228824609194380)
XLA Ops:
  0.6 3.9 copy.32
  4.5 198.4 %shard_map.238 = (bf16[3,1024,256]{2,1,0:T(8,128)(2,1)}, f32[16,128,128]{2,1,0:T(8,128)}, bf16[1024,256]{1,0:T(8,128)(2,1)}, bf16[1024,2048]{1,0:T(8,128)(2,1)},...) custom-call(bf16[128,2048]{1,0:T(8,128)(2,1)} %tokens.3, ...), custom_call_target="tpu_custom_call" | custom-call | flops 4294967296 | bytes 83886080 | tf_op jit(solution)/shard_map/pallas_call | solution.py:1897
  202.9 183.6 %shard_map.239 = (bf16[4,8,128,2048]{3,2,1,0:T(8,128)(2,1)}, bf16[8,4,128,2048]{3,2,1,0:T(8,128)(2,1)}, f32[128,2048]{1,0:T(8,128)}, f32[16,128]{1,0:T(8,128)}, ...) custom-call(bf16[4,8,128,2048]{3,2,1,0:T(8,128)(2,1)} %get-tuple-ele, ...), custom_call_target="tpu_custom_call", output_to_operand_aliasing={{0}: (0, {})} | custom-call | flops 79725330432 | bytes 83886080 | tf_op jit(solution)/shard_map/pallas_call | solution.py:840
  386.5 241.3 %shard_map.240 = (bf16[128,2048]{1,0:T(8,128)(2,1)}, f32[128,2048]{1,0:T(8,128)}, f32[16,512]{1,0:T(8,128)}, bf16[4,512,2048]{2,1,0:T(8,128)(2,1)}, bf16[3,1408,...) custom-call(bf16[1024,256]{1,0:T(8,128)(2,1)} %get-tuple-element.48.mixed, ...), custom_call_target="tpu_custom_call", output_to_operand_aliasing={{4}: (18, {}), {5}: (19, {})} | custom-call | flops 12884901888 | bytes 83886080 | tf_op jit(solution)/shard_map/pallas_call | solution.py:1403
  627.9 0.0 copy-start.1
  627.9 0.0 copy-start
  627.9 29.4 %shard_map.241 = (f32[512,6144]{1,0:T(8,128)}, f32[512,2048]{1,0:T(8,128)}, f32[3,1408,2048]{2,1,0:T(8,128)}, f32[1408,2,512]{2,1,0:T(2,128)}, f32[1408,512]{1,0...) custom-call(bf16[4,512,2048]{2,1,0:T(8,128)(2,1)} %get-tuple-element.70.attn_all, ...), custom_call_target="tpu_custom_call" | custom-call | bytes 100663296 | tf_op jit(solution)/shard_map/pallas_call | solution.py:1992
  657.3 0.0 copy-done.1
  657.3 0.8 copy.38
  658.1 0.0 copy-done
  658.1 1.0 copy.39
Async XLA Ops:
  627.9 29.5 %copy-start.1 = (bf16[128,2048]{1,0:T(8,128)(2,1)S(1)}, bf16[128,2048]{1,0:T(8,128)(2,1)}, u32[]{:S(2)}) copy-start(bf16[128,2048]{1,0:T(8,128)(2,1)} %get-tuple-element.96) | copy-start | bytes 1572868
  627.9 30.3 %copy-start = (f32[128,2048]{1,0:T(8,128)S(1)}, f32[128,2048]{1,0:T(8,128)}, u32[]{:S(2)}) copy-start(f32[128,2048]{1,0:T(8,128)} %get-tuple-element.97) | copy-start | bytes 3145732

commit v6 on v5

--- a/solution.py
+++ b/solution.py
@@ -1964,8 +1964,11 @@
 
 
 def widen_kernel(
-    attn_all, shared_all, expert_all, small, qkv, out, shared, up, down, router, gate, gain_in, gain_out, bias
+    attn_all, shared_all, expert_all, small, rows, rows_grad, qkv, out, shared, up, down, router, gate, gain_in,
+    gain_out, bias, output, tokens_grad,
 ):
+    output[...] = rows[...]
+    tokens_grad[...] = rows_grad[...]
     for part in range(3):
         width = attn_all.shape[2]
         qkv[:, part * width : (part + 1) * width] = attn_all[part].astype(jnp.float32)
@@ -1983,7 +1986,7 @@
         bias[...] = small[11:14, :]
 
 
-def widen_call(attn_all, shared_all, expert_all, small):
+def widen_call(attn_all, shared_all, expert_all, small, rows, rows_grad):
     steps = 8
     _, depth, width = attn_all.shape
     units, routed, cols = shared_all.shape[1], expert_all.shape[1], expert_all.shape[2]
@@ -2003,12 +2006,16 @@
             shape((depth,), full),
             shape((depth,), full),
             shape((3, depth), full),
+            shape(rows.shape, rows.dtype),
+            shape(rows.shape, full),
         ),
         in_specs=[
             pl.BlockSpec((4, depth // steps, width), lambda i: (0, i, 0)),
             pl.BlockSpec((3, units // steps, width), lambda i: (0, i, 0)),
             pl.BlockSpec((3, routed // steps, cols), lambda i: (0, i, 0)),
             pl.BlockSpec((16, depth), lambda i: (0, 0)),
+            pl.BlockSpec((rows.shape[0] // steps, width), lambda i: (i, 0)),
+            pl.BlockSpec((rows.shape[0] // steps, width), lambda i: (i, 0)),
         ],
         out_specs=(
             pl.BlockSpec((depth // steps, 3 * width), lambda i: (i, 0)),
@@ -2021,10 +2028,12 @@
             pl.BlockSpec((depth,), lambda i: (0,)),
             pl.BlockSpec((depth,), lambda i: (0,)),
             pl.BlockSpec((3, depth), lambda i: (0, 0)),
+            pl.BlockSpec((rows.shape[0] // steps, width), lambda i: (i, 0)),
+            pl.BlockSpec((rows.shape[0] // steps, width), lambda i: (i, 0)),
         ),
         compiler_params=pltpu.CompilerParams(vmem_limit_bytes=60 * 2**20),
         cost_estimate=pl.CostEstimate(flops=0, bytes_accessed=96 * 2**20, transcendentals=0),
-    )(attn_all, shared_all, expert_all, small)
+    )(attn_all, shared_all, expert_all, small, rows, rows_grad)
 
 
 def silu_parts(gate):
@@ -2417,7 +2426,9 @@
         attn_gain_grad,
         ffn_gain_grad,
         bias_grad,
-    ) = widen_call(attn_grad, shared_grad, expert_grad, small_grad)
+        output,
+        tokens_grad,
+    ) = widen_call(attn_grad, shared_grad, expert_grad, small_grad, output, tokens_grad)
     return (
         output,
         tokens_grad,

time: 659 us -> 659 us (level)
  no operation moved by 1% of the time
where the time goes in v6:
time: 659 us; the launch traced here: 658 us
  Pallas kernels  654 us (99%)
    pallas_call x1, Pallas kernels, tail_call(): pl.pallas_call(tail_kernel, out_shape=(shape((rows, width), low), shape((...  241 us
    pallas_call x1, Pallas kernels, front_call(): pl.pallas_call(front_kernel, out_shape=(shape((3, 8 * rows, head_width),...  198 us
    pallas_call x1, Pallas kernels, mlp_call(): pl.pallas_call(functools.partial(mlp_kernel, routed_units), out_shape=(sh...  184 us
    pallas_call x1, Pallas kernels, widen_call(): pl.pallas_call(widen_kernel, grid=(steps,), out_shape=(shape((depth, 3 *...  30.4 us

profile of v6, /device:TPU:1, one launch (start us, length us, event | category | flops | bytes accessed | tf_op | source)
XLA Modules:
  0.0 658.4 jit_solution(10987754946358318681)
XLA Ops:
  0.6 3.9 copy.32
  4.5 198.4 %shard_map.238 = (bf16[3,1024,256]{2,1,0:T(8,128)(2,1)}, f32[16,128,128]{2,1,0:T(8,128)}, bf16[1024,256]{1,0:T(8,128)(2,1)}, bf16[1024,2048]{1,0:T(8,128)(2,1)},...) custom-call(bf16[128,2048]{1,0:T(8,128)(2,1)} %tokens.3, ...), custom_call_target="tpu_custom_call" | custom-call | flops 4294967296 | bytes 83886080 | tf_op jit(solution)/shard_map/pallas_call | solution.py:1897
  202.9 183.6 %shard_map.239 = (bf16[4,8,128,2048]{3,2,1,0:T(8,128)(2,1)}, bf16[8,4,128,2048]{3,2,1,0:T(8,128)(2,1)}, f32[128,2048]{1,0:T(8,128)}, f32[16,128]{1,0:T(8,128)}, ...) custom-call(bf16[4,8,128,2048]{3,2,1,0:T(8,128)(2,1)} %get-tuple-ele, ...), custom_call_target="tpu_custom_call", output_to_operand_aliasing={{0}: (0, {})} | custom-call | flops 79725330432 | bytes 83886080 | tf_op jit(solution)/shard_map/pallas_call | solution.py:840
  386.5 241.3 %shard_map.240 = (bf16[128,2048]{1,0:T(8,128)(2,1)}, f32[128,2048]{1,0:T(8,128)}, f32[16,512]{1,0:T(8,128)}, bf16[4,512,2048]{2,1,0:T(8,128)(2,1)}, bf16[3,1408,...) custom-call(bf16[1024,256]{1,0:T(8,128)(2,1)} %get-tuple-element.50.mixed, ...), custom_call_target="tpu_custom_call", output_to_operand_aliasing={{4}: (18, {}), {5}: (19, {})} | custom-call | flops 12884901888 | bytes 83886080 | tf_op jit(solution)/shard_map/pallas_call | solution.py:1403
  627.8 30.4 %shard_map.241 = (f32[512,6144]{1,0:T(8,128)}, f32[512,2048]{1,0:T(8,128)}, f32[3,1408,2048]{2,1,0:T(8,128)}, f32[1408,2,512]{2,1,0:T(2,128)}, f32[1408,512]{1,0...) custom-call(bf16[4,512,2048]{2,1,0:T(8,128)(2,1)} %get-tuple-element, ...), custom_call_target="tpu_custom_call" | custom-call | bytes 100663296 | tf_op jit(solution)/shard_map/pallas_call | solution.py:1995
